TPU v7x, 1024 devices: a whole 8x8x8 slice. The times are simulated.
1024 devices in a mesh: pool: 2 (over core), group: 8 (over z), ep: 64 (over y, x).
Axes of the slice: x: 8, y: 8, z: 8, core: 2. Of those that a mesh axis runs over, the one named last changes fastest.
Arguments:
- moe_in: bfloat16 [8192, 2048], P(('group', 'ep')), may hold values from -6 to 6
- out_grad: bfloat16 [8192, 2048], P(('group', 'ep')), may hold values from -6 to 6
- gates: float32 [8192, 8], P(('group', 'ep')), may hold values from 0.1 to 1
- routes: int32 [8192, 8], P(('group', 'ep')), may hold values from 0 to 63, all different within a row; in each aligned block of 16 rows (0 to 15, 16 to 31, ...) at most 4 rows name the same one
- w_gate: bfloat16 [64, 2048, 768], P('ep', None, 'pool'), may hold values from -0.125 to 0.125
- w_up: bfloat16 [64, 2048, 768], P('ep', None, 'pool'), may hold values from -0.125 to 0.125
- w_down: bfloat16 [64, 768, 2048], P('ep', 'pool'), may hold values from -0.21875 to 0.21875
- context_t: bfloat16 [4096, 8192], P('ep', 'group'), may hold values from -0.0625 to 0.0625
Outputs:
- hidden_grad: float32 [8192, 2048], P(('group', 'ep'), 'pool')
- wo_grad: float32 [4096, 2048], P('ep', ('pool', 'group'))
Inputs may be any that keep to these rules, and one draw needn't show every extreme that they name: `routes`: each row names 8 different experts. Among the 16 rows of one index of group and ep no expert is named more than 4 times, a bound that some block reaches.
All inputs are finite; a program needn't handle non-finite values.
Results may differ from a plain program's by a relative error of at most 0.0045.
Values may be sent and summed in bfloat16 or wider, within the bound.
No kernel may reach another device: no remote copies, remote signals or barrier semaphores. Data moves between devices by JAX's collectives and lax.ppermute only.
A program may use at most 32 MiB of HBM per device.

v0:
```python
import jax
import jax.numpy as jnp
from jax import lax
from jax.sharding import PartitionSpec as P


def dot_transposed(left, right):
    return lax.dot_general(
        left, right, (((1,), (1,)), ((), ())), preferred_element_type=jnp.float32
    )


def half_input_grad(inputs_rows, grads_rows, gate_matrix, up_matrix, down_matrix):
    gate_value = jnp.dot(inputs_rows, gate_matrix, preferred_element_type=jnp.float32)
    up_value = jnp.dot(inputs_rows, up_matrix, preferred_element_type=jnp.float32)
    act_grad = dot_transposed(grads_rows, down_matrix)
    sigmoid_gate = jax.nn.sigmoid(gate_value)
    up_grad = (act_grad * gate_value * sigmoid_gate).astype(jnp.bfloat16)
    gate_grad = (
        act_grad * up_value * sigmoid_gate * (1.0 + gate_value * (1.0 - sigmoid_gate))
    ).astype(jnp.bfloat16)
    input_grad = dot_transposed(gate_grad, gate_matrix) + dot_transposed(up_grad, up_matrix)
    return input_grad.astype(jnp.bfloat16)


def per_device(moe_in, out_grad, gates, routes, w_gate, w_up, w_down, context_t):
    tok_rows, model_width = moe_in.shape
    top_count = routes.shape[1]
    experts = lax.axis_size("ep")
    capacity = 2 * tok_rows * top_count // experts
    pool_index = lax.axis_index("pool")
    half_width = model_width // 2
    pair_count = tok_rows * top_count
    expert_ids = routes.reshape(pair_count)
    expert_hits = (expert_ids[:, None] == jnp.arange(experts, dtype=jnp.int32)[None, :]).astype(
        jnp.int32
    )
    earlier = jnp.cumsum(expert_hits, axis=0) - expert_hits
    position = jnp.sum(earlier * expert_hits, axis=1)
    slot_ids = expert_ids * capacity + position
    slot_grid = jnp.arange(experts * capacity, dtype=jnp.int32)
    placed = slot_grid[:, None, None] == slot_ids.reshape(tok_rows, top_count)[None, :, :]
    picker = jnp.any(placed, axis=2).astype(jnp.bfloat16)
    send_x = jnp.dot(picker, moe_in, preferred_element_type=jnp.float32).astype(jnp.bfloat16)
    send_dy = jnp.dot(picker, out_grad, preferred_element_type=jnp.float32).astype(jnp.bfloat16)
    slot_rows = jnp.stack(
        (
            send_x.reshape(experts, capacity, model_width),
            send_dy.reshape(experts, capacity, model_width),
        ),
        1,
    )
    gate_matrix = w_gate[0]
    up_matrix = w_up[0]
    down_matrix = w_down[0]
    received = lax.all_to_all(slot_rows, "ep", split_axis=0, concat_axis=0, tiled=True)
    sources = received.shape[0]
    count = received.shape[2]
    inputs_rows = received[:, 0].reshape(sources * count, model_width)
    grads_rows = received[:, 1].reshape(sources * count, model_width)
    partial_rows = half_input_grad(inputs_rows, grads_rows, gate_matrix, up_matrix, down_matrix)
    send_partial_rows = partial_rows.reshape(sources, count, 2, half_width)
    returned_rows = lax.all_to_all(
        lax.all_to_all(send_partial_rows, "pool", split_axis=2, concat_axis=2, tiled=True),
        "ep",
        split_axis=0,
        concat_axis=0,
        tiled=True,
    )
    picked = jnp.take(returned_rows.reshape(experts * capacity, 2, half_width), slot_ids, axis=0)
    weighted = gates.reshape(pair_count)[:, None, None] * picked.astype(jnp.float32)
    moe_part = jnp.sum(weighted.reshape(tok_rows, top_count * 2, half_width), axis=1)
    grad_half = lax.dynamic_slice_in_dim(out_grad, pool_index * half_width, half_width, 1)
    hidden_grad = grad_half.astype(jnp.float32) + moe_part
    hidden_grad_b = hidden_grad.astype(jnp.bfloat16)
    partial_wo = jnp.dot(
        context_t,
        lax.all_gather(hidden_grad_b, "ep", axis=0, tiled=True),
        preferred_element_type=jnp.float32,
    )
    wo_grad = lax.psum_scatter(partial_wo, "group", scatter_dimension=1, tiled=True)
    return (hidden_grad, wo_grad)


def solution(mesh):
    return jax.shard_map(
        per_device,
        mesh=mesh,
        in_specs=(
            P(("group", "ep"), None),
            P(("group", "ep"), None),
            P(("group", "ep"), None),
            P(("group", "ep"), None),
            P("ep", None, "pool"),
            P("ep", None, "pool"),
            P("ep", "pool", None),
            P("ep", "group"),
        ),
        out_specs=(P(("group", "ep"), "pool"), P("ep", ("pool", "group"))),
        check_vma=False,
    )
```

profile of v0, /device:TPU:4, one launch (start us, length us, event | category | flops | bytes accessed | tf_op | source)
XLA Modules:
  0.0 299.5 jit_solution(3353859453721180037)
XLA Ops:
  7.2 0.0 copy-start
  7.2 0.9 copy.38
  8.1 0.1 reshape.73
  8.1 0.1 fusion.30
  8.2 0.2 reduce_window_sum.11
  8.4 0.2 select_reduce_fusion
  8.6 0.1 reduce_sum.30
  8.7 0.1 fusion.29
  8.8 0.0 copy-start.5
  8.8 1.3 convolution_convert_fusion
  10.2 1.2 stack_reshape.7
  11.4 0.0 copy-done.5
  11.4 0.5 convolution_convert_fusion.1
  11.9 1.2 stack_reshape.6
  13.1 2.9 pad_maximum_fusion
  16.0 64.5 %all_to_all.15 = bf16[64,2,4,2048]{3,2,1,0:T(4,128)(2,1)S(1)} all-to-all(bf16[64,2,4,2048]{3,2,1,0:T(4,128)(2,1)S(1)} %pad_maximum_fusion), channel_id=1, replica_groups=mesh['pool'=2,'group'=8,'ep'=64] {'ep'}, dimensions={0} | all-to-all | bytes 4194304 | tf_op jit(solution)/shard_map/all_to_all | solution.py:56
  80.5 2.4 fusion.37
  82.8 1.3 reshape_squeeze.7
  84.2 2.2 reshape_squeeze.6
  86.4 0.0 copy-start.1
  86.4 0.0 copy-start.2
  86.4 2.3 fusion.3
  88.7 0.0 copy-done.1
  88.7 0.0 copy-done.2
  88.7 0.7 fusion.8
  89.4 0.0 copy-done
  89.4 4.1 %fusion.1 = f32[256,2048]{1,0:T(8,128)} fusion(bf16[1,2048,384]{2,1,0:T(8,128)(2,1)} %param.12, f32[256,384]{1,0:T(8,128)S(1)} %fusion.8, bf16[256,2048]{1,0:T(8,128)(2,1)S(1)} %reshape_squeeze.7, bf16[1,2048,384]{2,1,0:T(8,128)(2,1)S(1)} %copy-done, f32[256,384]{1,0:T(8,128)S(1)} %fusion.3), kind=kOutput, calls=%fused_computation.6 | convolution fusion | flops 806289408 | bytes 7077888 | tf_op jit(solution)/shard_map/dot_general | solution.py:8
  93.6 3.3 %fusion = bf16[256,2048]{1,0:T(8,128)(2,1)} fusion(f32[256,2048]{1,0:T(8,128)} %fusion.1, bf16[1,2048,384]{2,1,0:T(8,128)(2,1)S(1)} %copy-done, f32[256,384]{1,0:T(8,128)S(1)} %fusion.8, f32[256,384]{1,0:T(8,128)S(1)} %fusion.3), kind=kOutput, calls=%fused_computation.4 | convolution fusion | flops 404291584 | bytes 5505024 | tf_op jit(solution)/shard_map/dot_general | solution.py:8
  96.9 1.8 reshape.74
  98.7 0.4 copy.42
  99.1 4.6 %all_to_all.16 = bf16[64,4,2,1024]{3,1,0,2:T(4,128)(2,1)S(1)} all-to-all(bf16[64,4,2,1024]{3,1,0,2:T(4,128)(2,1)S(1)} %copy.42), channel_id=1, replica_groups=mesh['pool'=2,'group'=8,'ep'=64] {'pool'}, dimensions={2} | all-to-all | bytes 2097152 | tf_op jit(solution)/shard_map/all_to_all | solution.py:64
  103.7 1.6 copy.43
  105.3 0.0 copy-start.6
  105.3 9.9 %all-to-all-start.2 = ((bf16[64,4,2,1024]{3,1,2,0:T(4,128)(2,1)}), bf16[64,4,2,1024]{3,1,2,0:T(4,128)(2,1)S(1)}, u32[]{:S(2)}, u32[]{:S(2)}) async-start(bf16[64,4,2,1024]{3,1,2,0:T(4,128)(2,1)} %copy.43), calls=%async_computation.2 | async-start | bytes 2097152 | tf_op jit(solution)/shard_map/all_to_all | solution.py:63
  115.2 0.2 all-gather.2.cloned.1.call-start
  115.4 0.1 mul.69
  115.5 0.0 copy-done.6
  115.5 0.1 copy.37
  115.6 0.1 mul.58
  115.7 0.1 broadcast_in_dim.14
  115.8 28.8 %all-to-all-done.2 = bf16[64,4,2,1024]{3,1,2,0:T(4,128)(2,1)S(1)} async-done(((bf16[64,4,2,1024]{3,1,2,0:T(4,128)(2,1)}), bf16[64,4,2,1024]{3,1,2,0:T(4,128)(2,1)S(1)}, u32[]{:S(2)}, u32[]{:S(2)}) %all-to-all-start.2) | async-done | bytes 1048608 | tf_op jit(solution)/shard_map/all_to_all | solution.py:63
  144.6 2.1 copy.44
  146.7 0.0 copy-start.3
  146.7 0.0 copy-start.4
  146.7 2.9 gather_fusion
  149.6 1.6 multiply_reduce_fusion
  151.2 0.1 bitcast_reduce_fusion
  151.4 0.0 copy-done.3
  151.4 0.7 fusion.35
  152.0 0.0 all-gather.2.cloned.1.call-update
  152.1 0.0 reduce-scatter.2.cloned.1.call-start
  152.1 93.9 %all-gather.2.cloned.1.call-done = bf16[1024,1024]{1,0:T(8,128)(2,1)} async-done(((bf16[16,1024]{1,0:T(8,128)(2,1)}), bf16[1024,1024]{1,0:T(8,128)(2,1)}) %all-gather.2.cloned.1.call-update) | async-done | bytes 2097168 | tf_op jit(solution)/shard_map/all_gather | solution.py:78
  246.0 0.0 copy-done.4
  246.0 2.8 convolution_bitcast_fusion
  248.8 0.0 reduce-scatter.2.cloned.1.call-update
  248.9 43.8 %reduce-scatter.2.cloned.1.call-done = f32[64,128]{1,0:T(8,128)} async-done(((f32[64,1024]{1,0:T(8,128)}), f32[64,128]{1,0:T(8,128)}) %reduce-scatter.2.cloned.1.call-update) | async-done | bytes 32784 | tf_op jit(solution)/shard_map/reduce_scatter | solution.py:81
  (4 shorter events, 0.0 us)
Async XLA Ops:
  7.2 82.2 %copy-start = (bf16[1,2048,384]{2,1,0:T(8,128)(2,1)S(1)}, bf16[1,2048,384]{2,1,0:T(8,128)(2,1)}, u32[]{:S(2)}) copy-start(bf16[1,2048,384]{2,1,0:T(8,128)(2,1)} %param.13) | copy-start | bytes 4718596
  8.8 2.6 copy-start.5
  86.4 2.3 copy-start.1
  86.4 2.3 copy-start.2
  105.3 10.2 %copy-start.6 = (f32[16,8]{0,1:T(8,128)S(1)}, f32[16,8]{0,1:T(8,128)}, u32[]{:S(2)}) copy-start(f32[16,8]{0,1:T(8,128)} %param.10) | copy-start | bytes 1540
  105.3 39.3 %all-to-all-start.2 = ((bf16[64,4,2,1024]{3,1,2,0:T(4,128)(2,1)}), bf16[64,4,2,1024]{3,1,2,0:T(4,128)(2,1)S(1)}, u32[]{:S(2)}, u32[]{:S(2)}) async-start(bf16[64,4,2,1024]{3,1,2,0:T(4,128)(2,1)} %copy.43), calls=%async_computation.2 | async-start | bytes 2097152 | tf_op jit(solution)/shard_map/all_to_all | solution.py:63
  115.2 130.8 %all-gather.2.cloned.1.call-start = ((), (), s32[]{:S(2)}) async-start(), calls=%async_computation.4 | async-start | bytes 2129920 | tf_op jit(solution)/shard_map/all_gather | solution.py:78
  146.7 4.7 %copy-start.3 = (bf16[16,2048]{1,0:T(8,128)(2,1)S(1)}, bf16[16,2048]{1,0:T(8,128)(2,1)}, u32[]{:S(2)}) copy-start(bf16[16,2048]{1,0:T(8,128)(2,1)} %param.9) | copy-start | bytes 196612
  146.7 99.3 %copy-start.4 = (bf16[64,1024]{1,0:T(8,128)(2,1)S(1)}, bf16[64,1024]{1,0:T(8,128)(2,1)}, u32[]{:S(2)}) copy-start(bf16[64,1024]{1,0:T(8,128)(2,1)} %param.15) | copy-start | bytes 393220
  152.1 140.6 %reduce-scatter.2.cloned.1.call-start = ((), (), s32[]{:S(2)}) async-start(), calls=%async_computation.5 | async-start | bytes 294912 | tf_op jit(solution)/shard_map/reduce_scatter | solution.py:81
Sparse Core Ops, SparseCore 0:
  152.2 93.7 all-gather.1
  250.0 42.6 reduce-scatter.1
where the time goes:
time: 300 us
  waiting for transfers between devices  167 us (56%)
  blocking collectives  69 us (23%)
  local copies, waits for them, and re-layouts  18.6 us (6%)
  matrix products  15.1 us (5%)
  between operations  14.2 us (5%)
  starting transfers between devices  10.1 us (3%)
  other arithmetic  5.9 us (2%)
    all_gather x1, waiting for transfers between devices, per_device(): lax.all_gather(hidden_grad_b, 'ep', axis=0, tiled=True)  93.9 us
    all_to_all x1, blocking collectives, per_device(): lax.all_to_all(slot_rows, 'ep', split_axis=0, concat_axis=0, tiled=True)  64.5 us
    reduce_scatter x1, waiting for transfers between devices, per_device(): lax.psum_scatter(partial_wo, 'group', scatter_dimension=1, tiled=True)  43.8 us
    all_to_all x1, waiting for transfers between devices, per_device(): lax.all_to_all(lax.all_to_all(send_partial_rows, 'pool', split_axis=2, co...  28.8 us
    all_to_all x1, starting transfers between devices, per_device(): lax.all_to_all(lax.all_to_all(send_partial_rows, 'pool', split_axis=2, co...  9.88 us
    dot_general x3, matrix products, dot_transposed(): lax.dot_general(left, right, (((1,), (1,)), ((), ())), preferred_element_...  8.21 us
  transfers between devices with their start and end apart: 3, of which 3 were waited for; matrix products, arithmetic and copies ran while one was open for 0% of the time, Pallas kernels for 0%

commit v1 on v0

v1 whole, which is shorter than its diff:
```python
import jax
import jax.numpy as jnp
from jax import lax
from jax.sharding import Mesh, PartitionSpec as P

ROWS = 8
BF = jnp.bfloat16
F32 = jnp.float32


def dot_f32(left, right):
    return jnp.dot(left, right, preferred_element_type=F32)


def dot_transposed(left, right):
    return lax.dot_general(left, right, (((1,), (1,)), ((), ())), preferred_element_type=F32)


def half_input_grad(inputs_rows, grads_rows, gate_matrix, up_matrix, down_matrix):
    gate_value = dot_f32(inputs_rows, gate_matrix)
    up_value = dot_f32(inputs_rows, up_matrix)
    act_grad = dot_transposed(grads_rows, down_matrix)
    sigmoid_gate = jax.nn.sigmoid(gate_value)
    up_grad = (act_grad * gate_value * sigmoid_gate).astype(BF)
    gate_grad = (
        act_grad * up_value * sigmoid_gate * (1.0 + gate_value * (1.0 - sigmoid_gate))
    ).astype(BF)
    return dot_transposed(gate_grad, gate_matrix) + dot_transposed(up_grad, up_matrix)


def swap_pool(value):
    return lax.ppermute(value, "pool", ((0, 1), (1, 0)))


def exchange(value, axes):
    return lax.all_to_all(value, axes, split_axis=0, concat_axis=0, tiled=True)


def per_device(moe_in, out_grad, gates, routes, w_gate, w_up, w_down, context_t):
    tok_rows, model_width = moe_in.shape
    top_count = routes.shape[1]
    y_size, x_size, z_size = lax.axis_size("y"), lax.axis_size("x"), lax.axis_size("group")
    experts = y_size * x_size
    capacity = 2 * tok_rows * top_count // experts
    own_slots = capacity // 2
    pool_index = lax.axis_index("pool")
    half_width = model_width // 2
    pair_count = tok_rows * top_count

    expert_ids = routes.reshape(pair_count)
    hits = (expert_ids[:, None] == jnp.arange(experts, dtype=jnp.int32)[None, :]).astype(jnp.int32)
    earlier = jnp.cumsum(hits, axis=0) - hits
    position = jnp.sum(earlier * hits, axis=1)
    own = position // own_slots == pool_index
    slot_ids = jnp.where(own, expert_ids * own_slots + position % own_slots, -1)
    slot_ids = slot_ids.reshape(tok_rows, top_count)
    slot_grid = jnp.arange(experts * own_slots, dtype=jnp.int32)
    placed = slot_ids[:, :, None] == slot_grid[None, None, :]
    picker = jnp.any(placed, axis=1).astype(BF)
    weights = jnp.sum(jnp.where(placed, gates[:, :, None], 0.0), axis=1)

    piece_width = 2 * model_width * own_slots // ROWS
    parts = 2 * model_width // piece_width
    stacked = jnp.concatenate(
        [a[:, i * piece_width:(i + 1) * piece_width] for a in (moe_in, out_grad) for i in range(parts // 2)], 0
    )
    eye = jnp.eye(parts, dtype=BF)
    spread = (picker.T[:, None, None, :] * eye[None, :, :, None]).reshape(
        experts * ROWS, parts * tok_rows
    )
    send = dot_f32(spread, stacked).astype(BF).reshape(experts, ROWS, piece_width)
    send, context_t, weights = lax.optimization_barrier((send, context_t, weights))
    received = exchange(send, ("y", "x"))
    other_gate, other_up, other_down = swap_pool(w_gate[0]), swap_pool(w_up[0]), swap_pool(w_down[0])
    heads, tokens = context_t.shape
    wide = tokens // y_size
    context_y = exchange(
        jnp.stack([context_t[:, i * wide:(i + 1) * wide] for i in range(y_size)]), "y"
    )
    received, context_y = lax.optimization_barrier((received, context_y))
    context_all = lax.all_gather(context_y.reshape(y_size * heads, wide), "group", axis=0, tiled=False)

    rows = received.reshape(experts * own_slots, 2, model_width)
    inputs_rows, grads_rows = rows[:, 0], rows[:, 1]
    total = half_input_grad(inputs_rows, grads_rows, w_gate[0], w_up[0], w_down[0]).astype(BF).astype(
        F32
    ) + half_input_grad(inputs_rows, grads_rows, other_gate, other_up, other_down).astype(BF).astype(F32)
    back_width = model_width * own_slots // ROWS
    back_parts = model_width // back_width
    back = total.astype(BF).reshape(experts, ROWS, back_width)
    returned = exchange(back, ("y", "x"))

    high = lax.reduce_precision(weights, 8, 7).astype(BF)
    low = (weights - high.astype(F32)).astype(BF)
    both = jnp.stack((high, low))
    back_eye = jnp.eye(back_parts, dtype=BF)
    mixer = (both[None, :, :, :, None] * back_eye[:, None, None, None, :]).reshape(
        back_parts * 2 * tok_rows, experts * ROWS
    )
    mixed = dot_f32(mixer, returned.reshape(experts * ROWS, back_width))
    mixed = jnp.sum(mixed.reshape(back_parts, 2, tok_rows, back_width), axis=1)
    per_half = back_parts // 2
    mine = lax.dynamic_slice_in_dim(mixed, pool_index * per_half, per_half, 0)
    theirs = lax.dynamic_slice_in_dim(mixed, (1 - pool_index) * per_half, per_half, 0)
    moe_part = mine + swap_pool(theirs)
    moe_part = jnp.concatenate([moe_part[i] for i in range(per_half)], axis=1)
    grad_half = lax.dynamic_slice_in_dim(out_grad, pool_index * half_width, half_width, 1)
    hidden_grad = grad_half.astype(F32) + moe_part
    hidden_grad_b = hidden_grad.astype(BF)

    cols = half_width // z_size
    by_column = jnp.stack([hidden_grad_b[:, i * cols:(i + 1) * cols] for i in range(z_size)])
    by_group = exchange(by_column, "group")
    gathered_b = exchange(
        jnp.broadcast_to(by_group[None], (x_size, z_size, tok_rows, cols)).reshape(
            x_size, z_size * tok_rows, cols
        ),
        "x",
    )
    tokens_b = gathered_b.reshape(x_size, z_size, tok_rows, cols).transpose(1, 0, 2, 3)
    rows_c = jnp.concatenate([context_all[i] for i in range(z_size)], axis=1)
    partial_wo = dot_f32(rows_c, tokens_b.reshape(-1, cols)).astype(BF)
    terms = exchange(partial_wo.reshape(y_size, heads, cols), "y")
    wo_grad = jnp.sum(terms.astype(F32), axis=0)
    return (hidden_grad, wo_grad)


def solution(mesh):
    pool, group, ep = (mesh.shape[name] for name in ("pool", "group", "ep"))
    y_size = 8
    grid = Mesh(mesh.devices.reshape(pool, group, y_size, ep // y_size), ("pool", "group", "y", "x"))
    tokens = ("group", "y", "x")
    return jax.shard_map(
        per_device,
        mesh=grid,
        in_specs=(
            P(tokens, None),
            P(tokens, None),
            P(tokens, None),
            P(tokens, None),
            P(("y", "x"), None, "pool"),
            P(("y", "x"), None, "pool"),
            P(("y", "x"), "pool", None),
            P(("y", "x"), "group"),
        ),
        out_specs=(P(tokens, "pool"), P(("y", "x"), ("pool", "group"))),
        check_vma=False,
    )
```

time: 300 us -> 195 us (0.65)
  the two profiles are of different devices: /device:TPU:4 before, /device:TPU:2 now
where the time goes in v1:
time: 195 us; the launch traced here: 194 us
  blocking collectives  72.1 us (37%)
  waiting for transfers between devices  43.2 us (22%)
  starting transfers between devices  28.3 us (15%)
  matrix products  19.4 us (10%)
  between operations  14.6 us (7%)
  local copies, waits for them, and re-layouts  14.4 us (7%)
  other arithmetic  2.27 us (1%)
    all_to_all x4, blocking collectives, exchange(): return lax.all_to_all(value, axes, split_axis=0, concat_axis=0, tiled=True)  72.1 us
    all_to_all x2, waiting for transfers between devices, exchange(): return lax.all_to_all(value, axes, split_axis=0, concat_axis=0, tiled=True)  32.7 us
    all_to_all x2, starting transfers between devices, exchange(): return lax.all_to_all(value, axes, split_axis=0, concat_axis=0, tiled=True)  20.1 us
    dot_general x6, matrix products, dot_transposed(): lax.dot_general(left, right, (((1,), (1,)), ((), ())), preferred_element_...  14.3 us
    all_gather x1, waiting for transfers between devices, per_device(): lax.all_gather(context_y.reshape(y_size * heads, wide), 'group', axis=0,...  9.22 us
    ppermute x4, starting transfers between devices, swap_pool(): return lax.ppermute(value, 'pool', ((0, 1), (1, 0)))  8.18 us
    unnamed x44, local copies, waits for them, and re-layouts  7.95 us
    dot_general x5, matrix products, dot_f32(): return jnp.dot(left, right, preferred_element_type=F32)  5.05 us
  transfers between devices with their start and end apart: 7, of which 4 were waited for; matrix products, arithmetic and copies ran while one was open for 9% of the time, Pallas kernels for 0%

profile of v1, /device:TPU:2, one launch (start us, length us, event | category | flops | bytes accessed | tf_op | source)
XLA Modules:
  0.0 194.2 jit_solution(5156824522481995919)
XLA Ops:
  7.2 0.0 copy-start.5
  7.2 0.8 copy.29
  8.0 0.1 eq.52
  8.1 0.1 fusion.59
  8.2 0.0 copy-start.7
  8.2 0.2 reduce_window_sum.11
  8.4 0.2 select_reduce_fusion.1
  8.5 0.1 reduce_sum.39
  8.7 0.1 fusion.58
  8.8 0.1 copy.31
  8.9 0.3 broadcast_multiply_fusion
  9.2 0.3 mul.102
  9.5 0.1 copy.32
  9.6 0.1 select_reduce_fusion
  9.7 0.0 copy-done.8
  9.7 0.0 copy-done.5
  9.7 1.4 fusion.6
  11.3 16.7 %all_to_all.30 = bf16[8,64,128]{2,1,0:T(8,128)(2,1)} all-to-all(bf16[8,64,128]{2,1,0:T(8,128)(2,1)S(1)} %constant_dynamic-update-slice_fusion), channel_id=1, replica_groups=mesh['pool'=2,'group'=8,'y'=8,'x'=8] {'y'}, dimensions={0} | all-to-all | bytes 262144 | tf_op jit(solution)/shard_map/all_to_all | solution.py:36
  28.0 13.6 %all-to-all-start = ((bf16[64,8,1024]{2,1,0:T(8,128)(2,1)}), bf16[64,8,1024]{2,1,0:T(8,128)(2,1)}, u32[]{:S(2)}, u32[]{:S(2)}) async-start(bf16[64,8,1024]{2,1,0:T(8,128)(2,1)} %fusion.6), calls=%async_computation | async-start | bytes 2097152 | tf_op jit(solution)/shard_map/all_to_all | solution.py:36
  41.6 1.9 collective-permute-start.2
  43.6 2.4 %collective-permute-start = (bf16[384,2048]{1,0:T(8,128)(2,1)}, bf16[384,2048]{1,0:T(8,128)(2,1)}, u32[]{:S(2)}, u32[]{:S(2)}) collective-permute-start(bf16[384,2048]{1,0:T(8,128)(2,1)} %bitcast.13), channel_id=1, source_target_pairs={{0,512},{512,0},{1,513},{513,1},{2,514},{514,2},{3,515},{515,3},{4... | collective-permute-start | bytes 4718600 | tf_op jit(solution)/shard_map/ppermute | solution.py:32
  46.0 1.9 collective-permute-start.1
  47.9 17.1 %all-to-all-done = bf16[64,8,1024]{2,1,0:T(8,128)(2,1)} async-done(((bf16[64,8,1024]{2,1,0:T(8,128)(2,1)}), bf16[64,8,1024]{2,1,0:T(8,128)(2,1)}, u32[]{:S(2)}, u32[]{:S(2)}) %all-to-all-start) | async-done | bytes 1048608 | tf_op jit(solution)/shard_map/all_to_all | solution.py:36
  65.0 1.7 reshape.107
  66.7 1.5 fusion.80
  68.2 0.3 copy.38
  68.5 0.4 fusion.18
  69.0 2.1 %fusion.24 = f32[128,384]{1,0:T(8,128)S(1)} fusion(bf16[128,1,2048]{2,1,0:T(2,128)(2,1)S(1)} %get-tuple-element.15, bf16[1,384,2048]{2,1,0:T(8,128)(2,1)} %param.14), kind=kOutput, calls=%fused_computation.29 | convolution fusion | flops 201326592 | bytes 2293760 | tf_op jit(solution)/shard_map/dot_general | solution.py:16
  71.1 0.0 collective-permute-done.2
  71.1 2.5 %fusion.14 = f32[128,384]{1,0:T(8,128)} fusion(bf16[2048,384]{1,0:T(8,128)(2,1)} %collective-permute-done.2, bf16[128,1,2048]{2,0,1:T(8,128)(2,1)S(1)} %copy.38), kind=kOutput, calls=%fused_computation.21 | convolution fusion | flops 201326592 | bytes 2293760 | tf_op jit(solution)/shard_map/dot_general | solution.py:12
  73.6 0.0 collective-permute-done
  73.6 2.8 %fusion.22 = f32[128,384]{1,0:T(8,128)} fusion(bf16[384,2048]{1,0:T(8,128)(2,1)} %collective-permute-done, bf16[128,1,2048]{2,1,0:T(2,128)(2,1)S(1)} %get-tuple-element.15), kind=kOutput, calls=%fused_computation.27 | convolution fusion | flops 201326592 | bytes 2293760 | tf_op jit(solution)/shard_map/dot_general | solution.py:16
  76.4 2.4 %fusion.13 = f32[128,2048]{1,0:T(8,128)S(1)} fusion(f32[128,384]{1,0:T(8,128)S(1)} %fusion.24, bf16[128,1,2048]{2,0,1:T(8,128)(2,1)S(1)} %copy.38, f32[128,384]{1,0:T(8,128)S(1)} %fusion.18, bf16[1,2048,384]{2,1,0:T(8,128)(2,1)S(1)} %copy-done, bf16[1,2048,384]{2,1,0:T(8,128)(2,1)} %param.13), kind=kOutput, calls=%fused_computation.20 | convolution fusion | flops 403144704 | bytes 5111808 | tf_op jit(solution)/shard_map/dot_general | solution.py:16
  78.8 2.1 %fusion.1 = f32[128,2048]{1,0:T(8,128)S(1)} fusion(f32[128,2048]{1,0:T(8,128)S(1)} %fusion.13, f32[128,384]{1,0:T(8,128)S(1)} %fusion.24, f32[128,384]{1,0:T(8,128)S(1)} %fusion.18, bf16[1,2048,384]{2,1,0:T(8,128)(2,1)} %param.13), kind=kOutput, calls=%fused_computation.3 | convolution fusion | flops 202407936 | bytes 4063232 | tf_op jit(solution)/shard_map/dot_general | solution.py:16
  80.9 0.0 collective-permute-done.1
  81.0 2.1 %fusion.51 = f32[128,2048]{1,0:T(8,128)S(1)} fusion(bf16[2048,384]{1,0:T(8,128)(2,1)} %collective-permute-done.1, f32[128,384]{1,0:T(8,128)S(1)} %copy-done.3, f32[128,384]{1,0:T(8,128)S(1)} %copy-done.1), kind=kOutput, calls=%fused_computation.70 | convolution fusion | flops 201621504 | bytes 3014656 | tf_op jit(solution)/shard_map/dot_general | solution.py:16
  83.1 2.9 %fusion.5 = bf16[128,2048]{1,0:T(8,128)(2,1)S(1)} fusion(f32[128,2048]{1,0:T(8,128)S(1)} %fusion.1, f32[128,2048]{1,0:T(8,128)S(1)} %fusion.51, bf16[2048,384]{1,0:T(8,128)(2,1)} %collective-permute-done.2, f32[128,384]{1,0:T(8,128)S(1)} %copy-done.4, bf16[2048,384]{1,0:T(8,128)(2,1)} %collective-permute-done.1, bf16[128,1,2048]{2,0,1:T(8,128)(2,1)S(1)} %copy.38, ...), kind=kOutput, calls=%fused_computation.7 | convolution fusion | flops 404455424 | bytes 6684672 | tf_op jit(solution)/shard_map/dot_general | solution.py:16
  86.0 1.1 reshape.108
  87.1 6.4 %all-to-all-start.2 = ((bf16[64,8,512]{2,1,0:T(8,128)(2,1)}), bf16[64,8,512]{2,1,0:T(8,128)(2,1)S(1)}, u32[]{:S(2)}, u32[]{:S(2)}) async-start(bf16[64,8,512]{2,1,0:T(8,128)(2,1)} %reshape.108), calls=%async_computation.2 | async-start | bytes 1048576 | tf_op jit(solution)/shard_map/all_to_all | solution.py:36
  93.5 0.0 all-gather.2.cloned.1.call-start
  93.6 0.1 copy.33
  93.7 0.1 mul.103
  93.8 0.1 copy.34
  94.0 0.2 mul.107
  94.1 15.7 %all-to-all-done.2 = bf16[64,8,512]{2,1,0:T(8,128)(2,1)S(1)} async-done(((bf16[64,8,512]{2,1,0:T(8,128)(2,1)}), bf16[64,8,512]{2,1,0:T(8,128)(2,1)S(1)}, u32[]{:S(2)}, u32[]{:S(2)}) %all-to-all-start.2) | async-done | bytes 524320 | tf_op jit(solution)/shard_map/all_to_all | solution.py:36
  109.8 0.2 convolution_reduce_fusion
  110.1 1.9 collective-permute-start.3
  112.0 0.0 all-gather.2.cloned.1.call-update
  112.0 1.2 collective-permute-done.3
  113.3 0.6 fusion.79
  114.0 26.2 %all_to_all.31 = bf16[8,16,128]{2,1,0:T(8,128)(2,1)S(1)} all-to-all(bf16[8,16,128]{2,1,0:T(8,128)(2,1)S(1)} %constant_dynamic-update-slice_fusion.8), channel_id=1, replica_groups=mesh['pool'=2,'group'=8,'y'=8,'x'=8] {'group'}, dimensions={0} | all-to-all | bytes 65536 | tf_op jit(solution)/shard_map/all_to_all | solution.py:36
  140.2 13.5 %all_to_all.32 = bf16[8,128,128]{2,1,0:T(8,128)(2,1)S(1)} all-to-all(bf16[8,128,128]{2,1,0:T(8,128)(2,1)S(1)} %broadcast_in_dim.32), channel_id=1, replica_groups=mesh['pool'=2,'group'=8,'y'=8,'x'=8] {'x'}, dimensions={0} | all-to-all | bytes 524288 | tf_op jit(solution)/shard_map/all_to_all | solution.py:36
  153.8 9.2 %all-gather.2.cloned.1.call-done = bf16[8,512,128]{2,1,0:T(8,128)(2,1)} async-done(((bf16[1,512,128]{2,1,0:T(8,128)(2,1)}), bf16[8,512,128]{2,1,0:T(8,128)(2,1)}) %all-gather.2.cloned.1.call-update) | async-done | bytes 1048592 | tf_op jit(solution)/shard_map/all_gather | solution.py:81
  163.0 0.9 fusion.42
  163.9 0.9 fusion.41
  164.9 0.9 fusion.40
  165.8 0.9 fusion.39
  166.8 0.9 fusion.38
  167.7 0.9 fusion.37
  168.7 0.9 fusion.36
  169.6 0.9 fusion.35
  170.6 0.4 convolution_convert_fusion.1
  171.0 15.7 %all_to_all.33 = bf16[8,64,128]{2,1,0:T(8,128)(2,1)S(1)} all-to-all(bf16[8,64,128]{2,1,0:T(8,128)(2,1)S(1)} %bitcast.150), channel_id=1, replica_groups=mesh['pool'=2,'group'=8,'y'=8,'x'=8] {'y'}, dimensions={0} | all-to-all | bytes 262144 | tf_op jit(solution)/shard_map/all_to_all | solution.py:36
  186.7 0.6 convert_reduce_fusion
  (44 shorter events, 0.4 us)
Async XLA Ops:
  7.2 2.3 %copy-start.9 = (f32[16,8]{0,1:T(8,128)S(1)}, f32[16,8]{0,1:T(8,128)}, u32[]{:S(2)}) copy-start(f32[16,8]{0,1:T(8,128)} %param.10) | copy-start | bytes 1540
  7.2 2.5 %copy-start.8 = (bf16[16,2048]{1,0:T(8,128)(2,1)S(1)}, bf16[16,2048]{1,0:T(8,128)(2,1)}, u32[]{:S(2)}) copy-start(bf16[16,2048]{1,0:T(8,128)(2,1)} %param.8) | copy-start | bytes 196612
  7.2 2.5 %copy-start.5 = (bf16[16,2048]{1,0:T(8,128)(2,1)S(1)}, bf16[16,2048]{1,0:T(8,128)(2,1)}, u32[]{:S(2)}) copy-start(bf16[16,2048]{1,0:T(8,128)(2,1)} %param.9) | copy-start | bytes 196612
  8.2 3.0 %copy-start.7 = (bf16[64,1024]{1,0:T(8,128)(2,1)S(1)}, bf16[64,1024]{1,0:T(8,128)(2,1)}, u32[]{:S(2)}) copy-start(bf16[64,1024]{1,0:T(8,128)(2,1)} %param.15) | copy-start | bytes 393220
  11.1 30.5 %copy-start = (bf16[1,2048,384]{2,1,0:T(8,128)(2,1)S(1)}, bf16[1,2048,384]{2,1,0:T(8,128)(2,1)}, u32[]{:S(2)}) copy-start(bf16[1,2048,384]{2,1,0:T(8,128)(2,1)} %param.12) | copy-start | bytes 4718596
  28.0 37.0 %all-to-all-start = ((bf16[64,8,1024]{2,1,0:T(8,128)(2,1)}), bf16[64,8,1024]{2,1,0:T(8,128)(2,1)}, u32[]{:S(2)}, u32[]{:S(2)}) async-start(bf16[64,8,1024]{2,1,0:T(8,128)(2,1)} %fusion.6), calls=%async_computation | async-start | bytes 2097152 | tf_op jit(solution)/shard_map/all_to_all | solution.py:36
  41.6 29.4 %collective-permute-start.2 = (bf16[2048,384]{1,0:T(8,128)(2,1)S(1)}, bf16[2048,384]{1,0:T(8,128)(2,1)}, u32[]{:S(2)}, u32[]{:S(2)}) collective-permute-start(bf16[2048,384]{1,0:T(8,128)(2,1)S(1)} %bitcast.145), channel_id=1, source_target_pairs={{0,512},{512,0},{1,513},{513,1},{2,514},{514,2},{3,515},{515,3},{4... | collective-permute-start | bytes 4718600 | tf_op jit(solution)/shard_map/ppermute | solution.py:32
  43.6 30.1 %collective-permute-start = (bf16[384,2048]{1,0:T(8,128)(2,1)}, bf16[384,2048]{1,0:T(8,128)(2,1)}, u32[]{:S(2)}, u32[]{:S(2)}) collective-permute-start(bf16[384,2048]{1,0:T(8,128)(2,1)} %bitcast.13), channel_id=1, source_target_pairs={{0,512},{512,0},{1,513},{513,1},{2,514},{514,2},{3,515},{515,3},{4... | collective-permute-start | bytes 4718600 | tf_op jit(solution)/shard_map/ppermute | solution.py:32
  46.0 35.0 %collective-permute-start.1 = (bf16[2048,384]{1,0:T(8,128)(2,1)}, bf16[2048,384]{1,0:T(8,128)(2,1)}, u32[]{:S(2)}, u32[]{:S(2)}) collective-permute-start(bf16[2048,384]{1,0:T(8,128)(2,1)} %bitcast.14), channel_id=1, source_target_pairs={{0,512},{512,0},{1,513},{513,1},{2,514},{514,2},{3,515},{515,3},{4... | collective-permute-start | bytes 4718600 | tf_op jit(solution)/shard_map/ppermute | solution.py:32
  78.8 2.1 %copy-start.1 = (f32[128,384]{1,0:T(8,128)S(1)}, f32[128,384]{1,0:T(8,128)}, u32[]{:S(2)}) copy-start(f32[128,384]{1,0:T(8,128)} %fusion.14) | copy-start | bytes 589828
  78.8 2.1 %copy-start.3 = (f32[128,384]{1,0:T(8,128)S(1)}, f32[128,384]{1,0:T(8,128)}, u32[]{:S(2)}) copy-start(f32[128,384]{1,0:T(8,128)} %fusion.22) | copy-start | bytes 589828
  80.9 2.2 %copy-start.2 = (f32[128,384]{1,0:T(8,128)S(1)}, f32[128,384]{1,0:T(8,128)}, u32[]{:S(2)}) copy-start(f32[128,384]{1,0:T(8,128)} %fusion.14) | copy-start | bytes 589828
  80.9 2.2 %copy-start.4 = (f32[128,384]{1,0:T(8,128)S(1)}, f32[128,384]{1,0:T(8,128)}, u32[]{:S(2)}) copy-start(f32[128,384]{1,0:T(8,128)} %fusion.22) | copy-start | bytes 589828
  87.1 26.2 %copy-start.6 = (bf16[16,2048]{1,0:T(8,128)(2,1)S(1)}, bf16[16,2048]{1,0:T(8,128)(2,1)}, u32[]{:S(2)}) copy-start(bf16[16,2048]{1,0:T(8,128)(2,1)} %param.9) | copy-start | bytes 196612
  87.1 22.7 %all-to-all-start.2 = ((bf16[64,8,512]{2,1,0:T(8,128)(2,1)}), bf16[64,8,512]{2,1,0:T(8,128)(2,1)S(1)}, u32[]{:S(2)}, u32[]{:S(2)}) async-start(bf16[64,8,512]{2,1,0:T(8,128)(2,1)} %reshape.108), calls=%async_computation.2 | async-start | bytes 1048576 | tf_op jit(solution)/shard_map/all_to_all | solution.py:36
  93.5 69.4 %all-gather.2.cloned.1.call-start = ((), (), s32[]{:S(2)}) async-start(), calls=%async_computation.6 | async-start | bytes 1179648 | tf_op jit(solution)/shard_map/all_gather | solution.py:81
  110.1 3.1 %collective-permute-start.3 = (f32[2,16,512]{2,1,0:T(8,128)S(1)}, f32[2,16,512]{2,1,0:T(8,128)S(1)}, u32[]{:S(2)}, u32[]{:S(2)}) collective-permute-start(f32[2,16,512]{2,1,0:T(8,128)S(1)} %constant_dynamic-slice_fusion), channel_id=1, source_target_pairs={{0,512},{512,0},{1,513},{513,1},{2,514},{514,2},{3,515},{515,3},{4... | collective-permute-start | bytes 196616 | tf_op jit(solution)/shard_map/ppermute | solution.py:32
Sparse Core Ops, SparseCore 0:
  112.2 50.7 all-gather.1

commit v2 on v1

--- a/solution.py
+++ b/solution.py
@@ -1,6 +1,8 @@
 import jax
 import jax.numpy as jnp
 from jax import lax
+from jax.experimental import pallas as pl
+from jax.experimental.pallas import tpu as pltpu
 from jax.sharding import Mesh, PartitionSpec as P
 
 ROWS = 8
@@ -16,16 +18,103 @@
     return lax.dot_general(left, right, (((1,), (1,)), ((), ())), preferred_element_type=F32)
 
 
-def half_input_grad(inputs_rows, grads_rows, gate_matrix, up_matrix, down_matrix):
-    gate_value = dot_f32(inputs_rows, gate_matrix)
-    up_value = dot_f32(inputs_rows, up_matrix)
-    act_grad = dot_transposed(grads_rows, down_matrix)
-    sigmoid_gate = jax.nn.sigmoid(gate_value)
-    up_grad = (act_grad * gate_value * sigmoid_gate).astype(BF)
-    gate_grad = (
-        act_grad * up_value * sigmoid_gate * (1.0 + gate_value * (1.0 - sigmoid_gate))
-    ).astype(BF)
-    return dot_transposed(gate_grad, gate_matrix) + dot_transposed(up_grad, up_matrix)
+def moved(rows_out, rows_in, source):
+    at = lax.broadcasted_iota(jnp.int32, (rows_out, rows_in), 0)
+    of = lax.broadcasted_iota(jnp.int32, (rows_out, rows_in), 1)
+    return (of == source(at)).astype(BF)
+
+
+def expert_kernel(rows_ref, *refs):
+    weights, out_ref, held, sems = refs[:6], refs[6], refs[7:13], refs[13]
+    copies = [pltpu.make_async_copy(w, h, sems.at[i]) for i, (w, h) in enumerate(zip(weights, held))]
+    for copy in copies:
+        copy.start()
+    total_rows, piece = rows_ref.shape
+    width = held[0].shape[0]
+    parts = 2 * width // piece
+    slots = total_rows // parts
+    to_parts = moved(total_rows, total_rows, lambda i: lax.rem(i, slots) * parts + lax.div(i, slots))
+    sorted_rows = dot_f32(to_parts, rows_ref[...]).astype(BF)
+    part = [sorted_rows[i * slots:(i + 1) * slots] for i in range(parts)]
+    inputs_rows = jnp.concatenate(part[:parts // 2], axis=1)
+    grads_rows = jnp.concatenate(part[parts // 2:], axis=1)
+    total = None
+    for half in range(2):
+        gate_ref, up_ref, down_ref = held[3 * half:3 * half + 3]
+        copies[3 * half].wait()
+        gate_value = dot_f32(inputs_rows, gate_ref[...])
+        copies[3 * half + 1].wait()
+        up_value = dot_f32(inputs_rows, up_ref[...])
+        copies[3 * half + 2].wait()
+        act_grad = dot_transposed(grads_rows, down_ref[...])
+        sigmoid_gate = jax.nn.sigmoid(gate_value)
+        up_grad = (act_grad * gate_value * sigmoid_gate).astype(BF)
+        gate_grad = (
+            act_grad * up_value * sigmoid_gate * (1.0 + gate_value * (1.0 - sigmoid_gate))
+        ).astype(BF)
+        half_grad = dot_transposed(gate_grad, gate_ref[...]) + dot_transposed(up_grad, up_ref[...])
+        total = half_grad if total is None else total + half_grad
+    total = total.astype(BF)
+    back = out_ref.shape[1]
+    pieces = width // back
+    stacked = jnp.concatenate([total[:, i * back:(i + 1) * back] for i in range(pieces)], axis=0)
+    to_slots = moved(
+        slots * pieces, slots * pieces, lambda i: lax.rem(i, pieces) * slots + lax.div(i, pieces)
+    )
+    out_ref[...] = dot_f32(to_slots, stacked).astype(BF)
+
+
+def expert_rows(rows, weights, back):
+    width = weights[0].shape[0]
+    slots = rows.size // (2 * width)
+    hidden = weights[0].shape[1]
+    vmem = pl.BlockSpec(memory_space=pltpu.VMEM)
+    anywhere = pl.BlockSpec(memory_space=pltpu.HBM)
+    return pl.pallas_call(
+        expert_kernel,
+        out_shape=jax.ShapeDtypeStruct((slots * width // back, back), BF),
+        in_specs=[vmem] + [anywhere] * 6,
+        out_specs=vmem,
+        scratch_shapes=[pltpu.VMEM(w.shape, BF) for w in weights] + [pltpu.SemaphoreType.DMA((6,))],
+        compiler_params=pltpu.CompilerParams(vmem_limit_bytes=50 * 2**20),
+        cost_estimate=pl.CostEstimate(
+            flops=2 * slots * width * hidden * 10,
+            bytes_accessed=12 * width * hidden,
+            transcendentals=2 * slots * hidden,
+        ),
+        name="expert",
+    )(rows, *weights)
+
+
+def product_kernel(*refs):
+    contexts, tokens_ref, out_ref = refs[:-2], refs[-2], refs[-1]
+    x_size, depth, cols = tokens_ref.shape
+    tok = depth // sum(ref.shape[0] for ref in contexts)
+    total, at = None, 0
+    for ref in contexts:
+        for i in range(ref.shape[0]):
+            tokens = tokens_ref[:, at * tok:(at + 1) * tok, :].reshape(x_size * tok, cols)
+            term = dot_f32(ref[i], tokens)
+            total = term if total is None else total + term
+            at += 1
+    out_ref[...] = total.astype(BF)
+
+
+def context_product(contexts, tokens_b):
+    rows, depth = contexts[0].shape[1:]
+    groups = sum(c.shape[0] for c in contexts)
+    cols = tokens_b.shape[2]
+    return pl.pallas_call(
+        product_kernel,
+        out_shape=jax.ShapeDtypeStruct((rows, cols), BF),
+        in_specs=[pl.BlockSpec(memory_space=pltpu.VMEM)] * (len(contexts) + 1),
+        out_specs=pl.BlockSpec(memory_space=pltpu.VMEM),
+        compiler_params=pltpu.CompilerParams(vmem_limit_bytes=16 * 2**20),
+        cost_estimate=pl.CostEstimate(
+            flops=2 * groups * rows * depth * cols, bytes_accessed=2 * groups * rows * depth, transcendentals=0
+        ),
+        name="context_product",
+    )(*contexts, tokens_b)
 
 
 def swap_pool(value):
@@ -34,6 +123,39 @@
 
 def exchange(value, axes):
     return lax.all_to_all(value, axes, split_axis=0, concat_axis=0, tiled=True)
+
+
+def spread_over_y(context_t, y_index, y_size):
+    wide = context_t.shape[1] // y_size
+    places = [
+        lax.dynamic_slice_in_dim(context_t, jnp.bitwise_xor(y_index, r) * wide, wide, 1)
+        for r in range(y_size)
+    ]
+    bit = 1
+    while bit < y_size:
+        crossing = [r for r in range(y_size) if r & bit]
+        came = lax.ppermute(
+            jnp.stack([places[r] for r in crossing]), "y", tuple((s, s ^ bit) for s in range(y_size))
+        )
+        for i, r in enumerate(crossing):
+            places[r] = came[i]
+        bit *= 2
+    order = jnp.bitwise_xor(y_index, jnp.arange(y_size, dtype=jnp.int32))
+    return jnp.take(jnp.stack(places), order, axis=0)
+
+
+def across_group(block, z_size, bit):
+    return lax.ppermute(block, "group", tuple((s, s ^ bit) for s in range(z_size)))
+
+
+def spread_over_group(pieces, z_index, z_size):
+    bit = z_size // 2
+    order = [0, bit]
+    while bit > 1:
+        bit //= 2
+        pieces = pieces + [across_group(jnp.concatenate(pieces, axis=0), z_size, bit)]
+        order += [r ^ bit for r in order]
+    return pieces, jnp.bitwise_xor(z_index, jnp.asarray(order, jnp.int32))
 
 
 def per_device(moe_in, out_grad, gates, routes, w_gate, w_up, w_down, context_t):
@@ -44,6 +166,7 @@
     capacity = 2 * tok_rows * top_count // experts
     own_slots = capacity // 2
     pool_index = lax.axis_index("pool")
+    y_index = lax.axis_index("y")
     half_width = model_width // 2
     pair_count = tok_rows * top_count
 
@@ -72,23 +195,22 @@
     send, context_t, weights = lax.optimization_barrier((send, context_t, weights))
     received = exchange(send, ("y", "x"))
     other_gate, other_up, other_down = swap_pool(w_gate[0]), swap_pool(w_up[0]), swap_pool(w_down[0])
-    heads, tokens = context_t.shape
-    wide = tokens // y_size
-    context_y = exchange(
-        jnp.stack([context_t[:, i * wide:(i + 1) * wide] for i in range(y_size)]), "y"
-    )
-    received, context_y = lax.optimization_barrier((received, context_y))
-    context_all = lax.all_gather(context_y.reshape(y_size * heads, wide), "group", axis=0, tiled=False)
-
-    rows = received.reshape(experts * own_slots, 2, model_width)
-    inputs_rows, grads_rows = rows[:, 0], rows[:, 1]
-    total = half_input_grad(inputs_rows, grads_rows, w_gate[0], w_up[0], w_down[0]).astype(BF).astype(
-        F32
-    ) + half_input_grad(inputs_rows, grads_rows, other_gate, other_up, other_down).astype(BF).astype(F32)
+    heads = context_t.shape[0]
+    context_y = spread_over_y(context_t, y_index, y_size).reshape(1, y_size * heads, -1)
+    z_index = lax.axis_index("group")
+    context_pair = [context_y, across_group(context_y, z_size, z_size // 2)]
+    received, context_pair = lax.optimization_barrier((received, context_pair))
+    context_all, group_order = spread_over_group(context_pair, z_index, z_size)
+
     back_width = model_width * own_slots // ROWS
     back_parts = model_width // back_width
-    back = total.astype(BF).reshape(experts, ROWS, back_width)
+    back = expert_rows(
+        received.reshape(experts * ROWS, piece_width),
+        (w_gate[0], w_up[0], w_down[0], other_gate, other_up, other_down),
+        back_width,
+    ).reshape(experts, ROWS, back_width)
     returned = exchange(back, ("y", "x"))
+    returned, context_all = lax.optimization_barrier((returned, context_all))
 
     high = lax.reduce_precision(weights, 8, 7).astype(BF)
     low = (weights - high.astype(F32)).astype(BF)
@@ -110,16 +232,14 @@
 
     cols = half_width // z_size
     by_column = jnp.stack([hidden_grad_b[:, i * cols:(i + 1) * cols] for i in range(z_size)])
-    by_group = exchange(by_column, "group")
+    by_group = jnp.take(exchange(by_column, "group"), group_order, axis=0)
     gathered_b = exchange(
         jnp.broadcast_to(by_group[None], (x_size, z_size, tok_rows, cols)).reshape(
             x_size, z_size * tok_rows, cols
         ),
         "x",
     )
-    tokens_b = gathered_b.reshape(x_size, z_size, tok_rows, cols).transpose(1, 0, 2, 3)
-    rows_c = jnp.concatenate([context_all[i] for i in range(z_size)], axis=1)
-    partial_wo = dot_f32(rows_c, tokens_b.reshape(-1, cols)).astype(BF)
+    partial_wo = context_product(context_all, gathered_b)
     terms = exchange(partial_wo.reshape(y_size, heads, cols), "y")
     wo_grad = jnp.sum(terms.astype(F32), axis=0)
     return (hidden_grad, wo_grad)

time: 195 us -> 185 us (0.949)
  starting transfers between devices: 28.3 us -> 82.4 us
  blocking collectives: 72.1 us -> 32 us
  matrix products: 19.4 us -> 1.63 us
  between operations: 14.6 us -> 1.12 us
  Pallas kernels: 0 us -> 8.75 us
  local copies, waits for them, and re-layouts: 14.4 us -> 8.32 us
  waiting for transfers between devices: 43.2 us -> 47.2 us
    all_to_all x4 -> x2, blocking collectives: 72.1 us -> 32 us  [exchange(): return lax.all_to_all(value, axes, split_axis=0, concat_axis=0, tiled=True)]
    ppermute x0 -> x6, waiting for transfers between devices: none -> 38.1 us  [the longest x3 22.1 us: across_group(): lax.ppermute(block, 'group', tuple(((s, s ^ bit) for s in range(z_size))))]
    ppermute x0 -> x6, starting transfers between devices: none -> 37.5 us  [the longest x3 20.9 us: across_group(): lax.ppermute(block, 'group', tuple(((s, s ^ bit) for s in range(z_size))))]
    all_to_all x2 -> x3, waiting for transfers between devices: 32.7 us -> 8.02 us  [exchange(): return lax.all_to_all(value, axes, split_axis=0, concat_axis=0, tiled=True)]
    all_to_all x2 -> x3, starting transfers between devices: 20.1 us -> 36.7 us  [exchange(): return lax.all_to_all(value, axes, split_axis=0, concat_axis=0, tiled=True)]
    dot_general x6 -> x0, matrix products: 14.3 us -> none  [dot_transposed(): lax.dot_general(left, right, (((1,), (1,)), ((), ())), preferred_element_...]
    all_gather x1 -> x0, waiting for transfers between devices: 9.22 us -> none  [per_device(): lax.all_gather(context_y.reshape(y_size * heads, wide), 'group', axis=0,...]
    pallas_call x0 -> x2, Pallas kernels: none -> 8.75 us  [the longest x1 8.34 us: expert_rows(): pl.pallas_call(expert_kernel, out_shape=jax.ShapeDtypeStruct((slots * wid...]
  transfers between devices with their start and end apart: 7 -> 13, of which waited for: 4 -> 8; matrix products, arithmetic and copies ran while one was open for 9% -> 1% of each run, Pallas kernels for 0% -> 0%
where the time goes in v2:
time: 185 us; the launch traced here: 184 us
  starting transfers between devices  82.4 us (45%)
  waiting for transfers between devices  47.2 us (26%)
  blocking collectives  32 us (17%)
  Pallas kernels  8.75 us (5%)
  local copies, waits for them, and re-layouts  8.32 us (4%)
  other arithmetic  2.65 us (1%)
    all_to_all x3, starting transfers between devices, exchange(): return lax.all_to_all(value, axes, split_axis=0, concat_axis=0, tiled=True)  36.7 us
    all_to_all x2, blocking collectives, exchange(): return lax.all_to_all(value, axes, split_axis=0, concat_axis=0, tiled=True)  32 us
    ppermute x3, waiting for transfers between devices, across_group(): lax.ppermute(block, 'group', tuple(((s, s ^ bit) for s in range(z_size))))  22.1 us
    ppermute x3, starting transfers between devices, across_group(): lax.ppermute(block, 'group', tuple(((s, s ^ bit) for s in range(z_size))))  20.9 us
    ppermute x3, starting transfers between devices, spread_over_y(): lax.ppermute(jnp.stack([places[r] for r in crossing]), 'y', tuple(((s, s...  16.6 us
    ppermute x3, waiting for transfers between devices, spread_over_y(): lax.ppermute(jnp.stack([places[r] for r in crossing]), 'y', tuple(((s, s...  16 us
    pallas_call x1, Pallas kernels, expert_rows(): pl.pallas_call(expert_kernel, out_shape=jax.ShapeDtypeStruct((slots * wid...  8.34 us
    ppermute x4, starting transfers between devices, swap_pool(): return lax.ppermute(value, 'pool', ((0, 1), (1, 0)))  8.18 us
  transfers between devices with their start and end apart: 13, of which 8 were waited for; matrix products, arithmetic and copies ran while one was open for 1% of the time, Pallas kernels for 0%

profile of v2, /device:TPU:2, one launch (start us, length us, event | category | flops | bytes accessed | tf_op | source)
XLA Modules:
  0.0 184.1 jit_solution(10631953112613460059)
XLA Ops:
  0.7 0.8 copy.24
  1.5 0.1 eq.52
  1.6 0.1 fusion.13
  1.7 0.2 reduce_window_sum.11
  1.8 0.2 select_reduce_fusion.1
  2.0 0.1 reduce_sum.39
  2.1 0.1 fusion.12
  2.2 0.1 copy.26
  2.4 0.3 broadcast_multiply_fusion
  2.6 0.3 mul.90
  2.9 0.1 copy.27
  3.0 0.1 select_reduce_fusion
  3.2 0.0 copy-start.2
  3.2 1.4 fusion
  4.6 17.4 %all-to-all-start = ((bf16[64,8,1024]{2,1,0:T(8,128)(2,1)}), bf16[64,8,1024]{2,1,0:T(8,128)(2,1)S(1)}, u32[]{:S(2)}, u32[]{:S(2)}) async-start(bf16[64,8,1024]{2,1,0:T(8,128)(2,1)} %fusion), calls=%async_computation | async-start | bytes 2097152 | tf_op jit(solution)/shard_map/all_to_all | solution.py:125
  22.1 0.1 dynamic-slice_bitcast_fusion.7
  22.1 3.4 %collective-permute-start = (bf16[4,64,128]{2,1,0:T(8,128)(2,1)S(1)}, bf16[4,64,128]{2,1,0:T(8,128)(2,1)S(1)}, u32[]{:S(2)}, u32[]{:S(2)}) collective-permute-start(bf16[4,64,128]{2,1,0:T(8,128)(2,1)S(1)} %pad_maximum_fusion.3), channel_id=1, source_target_pairs={{0,8},{8,0},{16,24},{24,16},{32,40},{40,32},{48,56},{56,48},{1,9},... | collective-permute-start | bytes 196616 | tf_op jit(solution)/shard_map/ppermute | solution.py:137
  25.6 1.9 %collective-permute-start.4 = (bf16[2048,384]{1,0:T(8,128)(2,1)S(1)}, bf16[2048,384]{1,0:T(8,128)(2,1)}, u32[]{:S(2)}, u32[]{:S(2)}) collective-permute-start(bf16[2048,384]{1,0:T(8,128)(2,1)S(1)} %bitcast.83), channel_id=1, source_target_pairs={{0,512},{512,0},{1,513},{513,1},{2,514},{514,2},{3,515},{515,3},{4... | collective-permute-start | bytes 4718600 | tf_op jit(solution)/shard_map/ppermute | solution.py:121
  27.5 2.4 %collective-permute-start.5 = (bf16[2048,384]{1,0:T(8,128)(2,1)}, bf16[2048,384]{1,0:T(8,128)(2,1)}, u32[]{:S(2)}, u32[]{:S(2)}) collective-permute-start(bf16[2048,384]{1,0:T(8,128)(2,1)} %bitcast.86), channel_id=1, source_target_pairs={{0,512},{512,0},{1,513},{513,1},{2,514},{514,2},{3,515},{515,3},{4... | collective-permute-start | bytes 4718600 | tf_op jit(solution)/shard_map/ppermute | solution.py:121
  29.9 1.9 %collective-permute-start.6 = (bf16[384,2048]{1,0:T(8,128)(2,1)}, bf16[384,2048]{1,0:T(8,128)(2,1)}, u32[]{:S(2)}, u32[]{:S(2)}) collective-permute-start(bf16[384,2048]{1,0:T(8,128)(2,1)} %bitcast.88), channel_id=1, source_target_pairs={{0,512},{512,0},{1,513},{513,1},{2,514},{514,2},{3,515},{515,3},{4... | collective-permute-start | bytes 4718600 | tf_op jit(solution)/shard_map/ppermute | solution.py:121
  31.9 0.1 broadcast_in_dim.59
  32.0 0.1 broadcast_in_dim.60
  32.1 11.3 %collective-permute-done = bf16[4,64,128]{2,1,0:T(8,128)(2,1)S(1)} collective-permute-done((bf16[4,64,128]{2,1,0:T(8,128)(2,1)S(1)}, bf16[4,64,128]{2,1,0:T(8,128)(2,1)S(1)}, u32[]{:S(2)}, u32[]{:S(2)}) %collective-permute-start) | collective-permute-done | bytes 65568 | tf_op jit(solution)/shard_map/ppermute | solution.py:137
  43.4 4.7 %collective-permute-start.1 = (bf16[4,64,128]{2,1,0:T(8,128)(2,1)S(1)}, bf16[4,64,128]{2,1,0:T(8,128)(2,1)S(1)}, u32[]{:S(2)}, u32[]{:S(2)}) collective-permute-start(bf16[4,64,128]{2,1,0:T(8,128)(2,1)S(1)} %pad_maximum_fusion.4), channel_id=1, source_target_pairs={{0,16},{8,24},{16,0},{24,8},{32,48},{40,56},{48,32},{56,40},{1,17}... | collective-permute-start | bytes 196616 | tf_op jit(solution)/shard_map/ppermute | solution.py:137
  48.2 2.3 %collective-permute-done.1 = bf16[4,64,128]{2,1,0:T(8,128)(2,1)S(1)} collective-permute-done((bf16[4,64,128]{2,1,0:T(8,128)(2,1)S(1)}, bf16[4,64,128]{2,1,0:T(8,128)(2,1)S(1)}, u32[]{:S(2)}, u32[]{:S(2)}) %collective-permute-start.1) | collective-permute-done | bytes 65568 | tf_op jit(solution)/shard_map/ppermute | solution.py:137
  50.5 8.4 %collective-permute-start.2 = (bf16[4,64,128]{2,1,0:T(8,128)(2,1)S(1)}, bf16[4,64,128]{2,1,0:T(8,128)(2,1)S(1)}, u32[]{:S(2)}, u32[]{:S(2)}) collective-permute-start(bf16[4,64,128]{2,1,0:T(8,128)(2,1)S(1)} %pad_maximum_fusion.5), channel_id=1, source_target_pairs={{0,32},{8,40},{16,48},{24,56},{32,0},{40,8},{48,16},{56,24},{1,33}... | collective-permute-start | bytes 196616 | tf_op jit(solution)/shard_map/ppermute | solution.py:137
  59.0 2.3 %collective-permute-done.2 = bf16[4,64,128]{2,1,0:T(8,128)(2,1)S(1)} collective-permute-done((bf16[4,64,128]{2,1,0:T(8,128)(2,1)S(1)}, bf16[4,64,128]{2,1,0:T(8,128)(2,1)S(1)}, u32[]{:S(2)}, u32[]{:S(2)}) %collective-permute-start.2) | collective-permute-done | bytes 65568 | tf_op jit(solution)/shard_map/ppermute | solution.py:137
  61.3 0.6 gather_fusion
  61.9 0.1 bitcast_select_fusion.refs_0_
  62.0 12.1 %collective-permute-start.3 = (bf16[1,512,128]{2,1,0:T(8,128)(2,1)S(1)}, bf16[1,512,128]{2,1,0:T(8,128)(2,1)S(1)}, u32[]{:S(2)}, u32[]{:S(2)}) collective-permute-start(bf16[1,512,128]{2,1,0:T(8,128)(2,1)S(1)} %bitcast_select_fusion.refs_0_), channel_id=1, source_target_pairs={{0,256},{64,320},{128,384},{192,448},{256,0},{320,64},{384,128},{4... | collective-permute-start | bytes 393224 | tf_op jit(solution)/shard_map/ppermute | solution.py:148
  74.1 4.2 %collective-permute-done.3.refs_1_ = bf16[1,512,128]{2,1,0:T(8,128)(2,1)S(1)} collective-permute-done((bf16[1,512,128]{2,1,0:T(8,128)(2,1)S(1)}, bf16[1,512,128]{2,1,0:T(8,128)(2,1)S(1)}, u32[]{:S(2)}, u32[]{:S(2)}) %collective-permute-start.3) | collective-permute-done | bytes 131104 | tf_op jit(solution)/shard_map/ppermute | solution.py:148
  78.4 8.3 %expert.1 = bf16[512,512]{1,0:T(8,128)(2,1)} custom-call(bf16[512,1024]{1,0:T(8,128)(2,1)S(1)} %bitcast.82, bf16[2048,384]{1,0:T(8,128)(2,1)S(1)} %bitcast.84, bf16[2048,384]{1,0:T(8,128)(2,1)} %bitcast.87, bf16[384,2048]{1,0:T(8,128)(2,1)} %bitcast.89, bf16[2048,384]{1,0:T(8,128)(2,1)} %collective-permute-done.4.refs_3_, ...), custom_call_target="tpu_custom_call" | custom-call | flops 2013265920 | bytes 9437184 | tf_op jit(solution)/shard_map/expert/pallas_call | solution.py:73
  86.7 13.5 %all-to-all-start.1 = ((bf16[64,8,512]{2,1,0:T(8,128)(2,1)}), bf16[64,8,512]{2,1,0:T(8,128)(2,1)S(1)}, u32[]{:S(2)}, u32[]{:S(2)}) async-start(bf16[64,8,512]{2,1,0:T(8,128)(2,1)} %bitcast.19), calls=%async_computation.1 | async-start | bytes 1048576 | tf_op jit(solution)/shard_map/all_to_all | solution.py:125
  100.3 6.2 %collective-permute-start.7 = (bf16[2,512,128]{2,1,0:T(8,128)(2,1)S(1)}, bf16[2,512,128]{2,1,0:T(8,128)(2,1)S(1)}, u32[]{:S(2)}, u32[]{:S(2)}) collective-permute-start(bf16[2,512,128]{2,1,0:T(8,128)(2,1)S(1)} %pad_maximum_fusion.1), channel_id=1, source_target_pairs={{0,128},{64,192},{128,0},{192,64},{256,384},{320,448},{384,256},{4... | collective-permute-start | bytes 786440 | tf_op jit(solution)/shard_map/ppermute | solution.py:148
  106.5 8.3 %collective-permute-done.7.refs_2_ = bf16[2,512,128]{2,1,0:T(8,128)(2,1)S(1)} collective-permute-done((bf16[2,512,128]{2,1,0:T(8,128)(2,1)S(1)}, bf16[2,512,128]{2,1,0:T(8,128)(2,1)S(1)}, u32[]{:S(2)}, u32[]{:S(2)}) %collective-permute-start.7) | collective-permute-done | bytes 262176 | tf_op jit(solution)/shard_map/ppermute | solution.py:148
  114.8 0.1 pad_maximum_fusion
  114.9 2.6 %collective-permute-start.8 = (bf16[4,512,128]{2,1,0:T(8,128)(2,1)S(1)}, bf16[4,512,128]{2,1,0:T(8,128)(2,1)S(1)}, u32[]{:S(2)}, u32[]{:S(2)}) collective-permute-start(bf16[4,512,128]{2,1,0:T(8,128)(2,1)S(1)} %pad_maximum_fusion), channel_id=1, source_target_pairs={{0,64},{64,0},{128,192},{192,128},{256,320},{320,256},{384,448},{4... | collective-permute-start | bytes 1572872 | tf_op jit(solution)/shard_map/ppermute | solution.py:148
  117.6 0.2 mul.95
  117.8 0.1 copy.28
  117.9 0.1 mul.91
  118.0 0.1 copy.29
  118.1 9.6 %collective-permute-done.8.refs_3_ = bf16[4,512,128]{2,1,0:T(8,128)(2,1)S(1)} collective-permute-done((bf16[4,512,128]{2,1,0:T(8,128)(2,1)S(1)}, bf16[4,512,128]{2,1,0:T(8,128)(2,1)S(1)}, u32[]{:S(2)}, u32[]{:S(2)}) %collective-permute-start.8) | collective-permute-done | bytes 524320 | tf_op jit(solution)/shard_map/ppermute | solution.py:148
  127.7 0.2 convolution_reduce_fusion
  127.9 1.9 %collective-permute-start.9 = (f32[2,16,512]{2,1,0:T(8,128)S(1)}, f32[2,16,512]{2,1,0:T(8,128)S(1)}, u32[]{:S(2)}, u32[]{:S(2)}) collective-permute-start(f32[2,16,512]{2,1,0:T(8,128)S(1)} %constant_dynamic-slice_fusion), channel_id=1, source_target_pairs={{0,512},{512,0},{1,513},{513,1},{2,514},{514,2},{3,515},{515,3},{4... | collective-permute-start | bytes 196616 | tf_op jit(solution)/shard_map/ppermute | solution.py:121
  129.8 0.1 broadcast_in_dim.63
  129.9 0.1 broadcast_in_dim.64
  130.0 1.1 collective-permute-done.9
  131.1 0.6 fusion.24
  131.7 0.6 constant_dynamic-update-slice_fusion.7
  132.3 0.6 constant_dynamic-update-slice_fusion.6
  132.9 0.6 constant_dynamic-update-slice_fusion.5
  133.5 0.6 constant_dynamic-update-slice_fusion.4
  134.1 0.6 constant_dynamic-update-slice_fusion.3
  134.7 0.6 constant_dynamic-update-slice_fusion.2
  135.3 0.6 constant_dynamic-update-slice_fusion.1
  135.9 0.6 constant_dynamic-update-slice_fusion
  136.5 5.8 %all-to-all-start.2 = ((bf16[8,16,128]{2,1,0:T(8,128)(2,1)}), bf16[8,16,128]{2,1,0:T(8,128)(2,1)S(1)}, u32[]{:S(2)}, u32[]{:S(2)}) async-start(bf16[8,16,128]{2,1,0:T(8,128)(2,1)} %constant_dynamic-update-slice_fusion), calls=%async_computation.2 | async-start | bytes 65536 | tf_op jit(solution)/shard_map/all_to_all | solution.py:125
  142.3 8.0 %all-to-all-done.2 = bf16[8,16,128]{2,1,0:T(8,128)(2,1)S(1)} async-done(((bf16[8,16,128]{2,1,0:T(8,128)(2,1)}), bf16[8,16,128]{2,1,0:T(8,128)(2,1)S(1)}, u32[]{:S(2)}, u32[]{:S(2)}) %all-to-all-start.2) | async-done | bytes 32800 | tf_op jit(solution)/shard_map/all_to_all | solution.py:125
  150.3 0.6 gather_fusion.1
  150.9 0.1 bitcast_select_fusion.1
  151.1 16.4 %all_to_all.25.refs_4_ = bf16[8,128,128]{2,1,0:T(8,128)(2,1)S(1)} all-to-all(bf16[8,128,128]{2,1,0:T(8,128)(2,1)S(1)} %broadcast_in_dim.68), channel_id=1, replica_groups=mesh['pool'=2,'group'=8,'y'=8,'x'=8] {'x'}, dimensions={0} | all-to-all | bytes 524288 | tf_op jit(solution)/shard_map/all_to_all | solution.py:125
  167.4 0.4 context_product.1
  167.8 15.7 %all_to_all.26 = bf16[8,64,128]{2,1,0:T(8,128)(2,1)S(1)} all-to-all(bf16[8,64,128]{2,1,0:T(8,128)(2,1)S(1)} %bitcast.85), channel_id=1, replica_groups=mesh['pool'=2,'group'=8,'y'=8,'x'=8] {'y'}, dimensions={0} | all-to-all | bytes 262144 | tf_op jit(solution)/shard_map/all_to_all | solution.py:125
  183.5 0.6 convert_reduce_fusion
  (38 shorter events, 0.3 us)
Async XLA Ops:
  0.6 2.3 %copy-start.4 = (f32[16,8]{0,1:T(8,128)S(1)}, f32[16,8]{0,1:T(8,128)}, u32[]{:S(2)}) copy-start(f32[16,8]{0,1:T(8,128)} %param.11) | copy-start | bytes 1540
  0.6 2.5 %copy-start.3 = (bf16[16,2048]{1,0:T(8,128)(2,1)S(1)}, bf16[16,2048]{1,0:T(8,128)(2,1)}, u32[]{:S(2)}) copy-start(bf16[16,2048]{1,0:T(8,128)(2,1)} %param.9) | copy-start | bytes 196612
  0.6 2.5 %copy-start.1 = (bf16[16,2048]{1,0:T(8,128)(2,1)S(1)}, bf16[16,2048]{1,0:T(8,128)(2,1)}, u32[]{:S(2)}) copy-start(bf16[16,2048]{1,0:T(8,128)(2,1)} %param.10) | copy-start | bytes 196612
  3.2 18.9 %copy-start.2 = (bf16[64,1024]{1,0:T(8,128)(2,1)S(1)}, bf16[64,1024]{1,0:T(8,128)(2,1)}, u32[]{:S(2)}) copy-start(bf16[64,1024]{1,0:T(8,128)(2,1)} %param.16) | copy-start | bytes 393220
  4.6 21.0 %copy-start = (bf16[1,2048,384]{2,1,0:T(8,128)(2,1)S(1)}, bf16[1,2048,384]{2,1,0:T(8,128)(2,1)}, u32[]{:S(2)}) copy-start(bf16[1,2048,384]{2,1,0:T(8,128)(2,1)} %param.13) | copy-start | bytes 4718596
  4.6 27.3 %copy-start.5 = (s32[8]{0:T(128)S(1)}, s32[8]{0:T(128)}, u32[]{:S(2)}) copy-start(s32[8]{0:T(128)} %constant.97.clone) | copy-start | bytes 100
  4.6 73.8 %all-to-all-start = ((bf16[64,8,1024]{2,1,0:T(8,128)(2,1)}), bf16[64,8,1024]{2,1,0:T(8,128)(2,1)S(1)}, u32[]{:S(2)}, u32[]{:S(2)}) async-start(bf16[64,8,1024]{2,1,0:T(8,128)(2,1)} %fusion), calls=%async_computation | async-start | bytes 2097152 | tf_op jit(solution)/shard_map/all_to_all | solution.py:125
  22.1 21.3 %collective-permute-start = (bf16[4,64,128]{2,1,0:T(8,128)(2,1)S(1)}, bf16[4,64,128]{2,1,0:T(8,128)(2,1)S(1)}, u32[]{:S(2)}, u32[]{:S(2)}) collective-permute-start(bf16[4,64,128]{2,1,0:T(8,128)(2,1)S(1)} %pad_maximum_fusion.3), channel_id=1, source_target_pairs={{0,8},{8,0},{16,24},{24,16},{32,40},{40,32},{48,56},{56,48},{1,9},... | collective-permute-start | bytes 196616 | tf_op jit(solution)/shard_map/ppermute | solution.py:137
  25.6 52.8 %collective-permute-start.4 = (bf16[2048,384]{1,0:T(8,128)(2,1)S(1)}, bf16[2048,384]{1,0:T(8,128)(2,1)}, u32[]{:S(2)}, u32[]{:S(2)}) collective-permute-start(bf16[2048,384]{1,0:T(8,128)(2,1)S(1)} %bitcast.83), channel_id=1, source_target_pairs={{0,512},{512,0},{1,513},{513,1},{2,514},{514,2},{3,515},{515,3},{4... | collective-permute-start | bytes 4718600 | tf_op jit(solution)/shard_map/ppermute | solution.py:121
  27.5 50.8 %collective-permute-start.5 = (bf16[2048,384]{1,0:T(8,128)(2,1)}, bf16[2048,384]{1,0:T(8,128)(2,1)}, u32[]{:S(2)}, u32[]{:S(2)}) collective-permute-start(bf16[2048,384]{1,0:T(8,128)(2,1)} %bitcast.86), channel_id=1, source_target_pairs={{0,512},{512,0},{1,513},{513,1},{2,514},{514,2},{3,515},{515,3},{4... | collective-permute-start | bytes 4718600 | tf_op jit(solution)/shard_map/ppermute | solution.py:121
  29.9 48.4 %collective-permute-start.6 = (bf16[384,2048]{1,0:T(8,128)(2,1)}, bf16[384,2048]{1,0:T(8,128)(2,1)}, u32[]{:S(2)}, u32[]{:S(2)}) collective-permute-start(bf16[384,2048]{1,0:T(8,128)(2,1)} %bitcast.88), channel_id=1, source_target_pairs={{0,512},{512,0},{1,513},{513,1},{2,514},{514,2},{3,515},{515,3},{4... | collective-permute-start | bytes 4718600 | tf_op jit(solution)/shard_map/ppermute | solution.py:121
  43.4 7.1 %collective-permute-start.1 = (bf16[4,64,128]{2,1,0:T(8,128)(2,1)S(1)}, bf16[4,64,128]{2,1,0:T(8,128)(2,1)S(1)}, u32[]{:S(2)}, u32[]{:S(2)}) collective-permute-start(bf16[4,64,128]{2,1,0:T(8,128)(2,1)S(1)} %pad_maximum_fusion.4), channel_id=1, source_target_pairs={{0,16},{8,24},{16,0},{24,8},{32,48},{40,56},{48,32},{56,40},{1,17}... | collective-permute-start | bytes 196616 | tf_op jit(solution)/shard_map/ppermute | solution.py:137
  50.5 10.8 %collective-permute-start.2 = (bf16[4,64,128]{2,1,0:T(8,128)(2,1)S(1)}, bf16[4,64,128]{2,1,0:T(8,128)(2,1)S(1)}, u32[]{:S(2)}, u32[]{:S(2)}) collective-permute-start(bf16[4,64,128]{2,1,0:T(8,128)(2,1)S(1)} %pad_maximum_fusion.5), channel_id=1, source_target_pairs={{0,32},{8,40},{16,48},{24,56},{32,0},{40,8},{48,16},{56,24},{1,33}... | collective-permute-start | bytes 196616 | tf_op jit(solution)/shard_map/ppermute | solution.py:137
  62.0 16.3 %collective-permute-start.3 = (bf16[1,512,128]{2,1,0:T(8,128)(2,1)S(1)}, bf16[1,512,128]{2,1,0:T(8,128)(2,1)S(1)}, u32[]{:S(2)}, u32[]{:S(2)}) collective-permute-start(bf16[1,512,128]{2,1,0:T(8,128)(2,1)S(1)} %bitcast_select_fusion.refs_0_), channel_id=1, source_target_pairs={{0,256},{64,320},{128,384},{192,448},{256,0},{320,64},{384,128},{4... | collective-permute-start | bytes 393224 | tf_op jit(solution)/shard_map/ppermute | solution.py:148
  86.7 40.9 %all-to-all-start.1 = ((bf16[64,8,512]{2,1,0:T(8,128)(2,1)}), bf16[64,8,512]{2,1,0:T(8,128)(2,1)S(1)}, u32[]{:S(2)}, u32[]{:S(2)}) async-start(bf16[64,8,512]{2,1,0:T(8,128)(2,1)} %bitcast.19), calls=%async_computation.1 | async-start | bytes 1048576 | tf_op jit(solution)/shard_map/all_to_all | solution.py:125
  100.3 14.6 %collective-permute-start.7 = (bf16[2,512,128]{2,1,0:T(8,128)(2,1)S(1)}, bf16[2,512,128]{2,1,0:T(8,128)(2,1)S(1)}, u32[]{:S(2)}, u32[]{:S(2)}) collective-permute-start(bf16[2,512,128]{2,1,0:T(8,128)(2,1)S(1)} %pad_maximum_fusion.1), channel_id=1, source_target_pairs={{0,128},{64,192},{128,0},{192,64},{256,384},{320,448},{384,256},{4... | collective-permute-start | bytes 786440 | tf_op jit(solution)/shard_map/ppermute | solution.py:148
  114.9 12.8 %collective-permute-start.8 = (bf16[4,512,128]{2,1,0:T(8,128)(2,1)S(1)}, bf16[4,512,128]{2,1,0:T(8,128)(2,1)S(1)}, u32[]{:S(2)}, u32[]{:S(2)}) collective-permute-start(bf16[4,512,128]{2,1,0:T(8,128)(2,1)S(1)} %pad_maximum_fusion), channel_id=1, source_target_pairs={{0,64},{64,0},{128,192},{192,128},{256,320},{320,256},{384,448},{4... | collective-permute-start | bytes 1572872 | tf_op jit(solution)/shard_map/ppermute | solution.py:148
  127.9 3.1 %collective-permute-start.9 = (f32[2,16,512]{2,1,0:T(8,128)S(1)}, f32[2,16,512]{2,1,0:T(8,128)S(1)}, u32[]{:S(2)}, u32[]{:S(2)}) collective-permute-start(f32[2,16,512]{2,1,0:T(8,128)S(1)} %constant_dynamic-slice_fusion), channel_id=1, source_target_pairs={{0,512},{512,0},{1,513},{513,1},{2,514},{514,2},{3,515},{515,3},{4... | collective-permute-start | bytes 196616 | tf_op jit(solution)/shard_map/ppermute | solution.py:121
  136.5 13.9 %all-to-all-start.2 = ((bf16[8,16,128]{2,1,0:T(8,128)(2,1)}), bf16[8,16,128]{2,1,0:T(8,128)(2,1)S(1)}, u32[]{:S(2)}, u32[]{:S(2)}) async-start(bf16[8,16,128]{2,1,0:T(8,128)(2,1)} %constant_dynamic-update-slice_fusion), calls=%async_computation.2 | async-start | bytes 65536 | tf_op jit(solution)/shard_map/all_to_all | solution.py:125

commit v3 on v2

--- a/solution.py
+++ b/solution.py
@@ -6,6 +6,7 @@
 from jax.sharding import Mesh, PartitionSpec as P
 
 ROWS = 8
+SORT = 256
 BF = jnp.bfloat16
 F32 = jnp.float32
 
@@ -32,10 +33,16 @@
     total_rows, piece = rows_ref.shape
     width = held[0].shape[0]
     parts = 2 * width // piece
-    slots = total_rows // parts
-    to_parts = moved(total_rows, total_rows, lambda i: lax.rem(i, slots) * parts + lax.div(i, slots))
-    sorted_rows = dot_f32(to_parts, rows_ref[...]).astype(BF)
-    part = [sorted_rows[i * slots:(i + 1) * slots] for i in range(parts)]
+    block = min(SORT, total_rows)
+    slots = block // parts
+    to_parts = moved(block, block, lambda i: lax.rem(i, slots) * parts + lax.div(i, slots))
+    sorted_rows = [
+        dot_f32(to_parts, rows_ref[i:i + block]).astype(BF) for i in range(0, total_rows, block)
+    ]
+    part = [
+        jnp.concatenate([rows[i * slots:(i + 1) * slots] for rows in sorted_rows], axis=0)
+        for i in range(parts)
+    ]
     inputs_rows = jnp.concatenate(part[:parts // 2], axis=1)
     grads_rows = jnp.concatenate(part[parts // 2:], axis=1)
     total = None
@@ -57,11 +64,13 @@
     total = total.astype(BF)
     back = out_ref.shape[1]
     pieces = width // back
-    stacked = jnp.concatenate([total[:, i * back:(i + 1) * back] for i in range(pieces)], axis=0)
-    to_slots = moved(
-        slots * pieces, slots * pieces, lambda i: lax.rem(i, pieces) * slots + lax.div(i, pieces)
-    )
-    out_ref[...] = dot_f32(to_slots, stacked).astype(BF)
+    block = min(SORT, out_ref.shape[0])
+    slots = block // pieces
+    to_slots = moved(block, block, lambda i: lax.rem(i, pieces) * slots + lax.div(i, pieces))
+    for at in range(out_ref.shape[0] // block):
+        rows = total[at * slots:(at + 1) * slots]
+        stacked = jnp.concatenate([rows[:, i * back:(i + 1) * back] for i in range(pieces)], axis=0)
+        out_ref[at * block:(at + 1) * block] = dot_f32(to_slots, stacked).astype(BF)
 
 
 def expert_rows(rows, weights, back):
@@ -86,35 +95,66 @@
     )(rows, *weights)
 
 
-def product_kernel(*refs):
+def product_kernel(place_ref, *refs):
     contexts, tokens_ref, out_ref = refs[:-2], refs[-2], refs[-1]
     x_size, depth, cols = tokens_ref.shape
-    tok = depth // sum(ref.shape[0] for ref in contexts)
-    total, at = None, 0
-    for ref in contexts:
-        for i in range(ref.shape[0]):
-            tokens = tokens_ref[:, at * tok:(at + 1) * tok, :].reshape(x_size * tok, cols)
-            term = dot_f32(ref[i], tokens)
-            total = term if total is None else total + term
-            at += 1
-    out_ref[...] = total.astype(BF)
-
-
-def context_product(contexts, tokens_b):
-    rows, depth = contexts[0].shape[1:]
-    groups = sum(c.shape[0] for c in contexts)
+    z_size = len(contexts)
+    tok = depth // z_size
+    z_index, y_index, y_size = place_ref[0], place_ref[1], place_ref[2]
+    total = None
+    for step, ref in enumerate(contexts):
+        at = pl.multiple_of(lax.rem(z_index + z_size - step, z_size) * tok, tok)
+        tokens = tokens_ref[:, pl.ds(at, tok), :].reshape(x_size * tok, cols)
+        term = dot_f32(ref[...], tokens)
+        total = term if total is None else total + term
+    heads = out_ref.shape[1]
+    for step in range(out_ref.shape[0]):
+        out_ref[lax.rem(y_index + y_size - step, y_size)] = total[step * heads:(step + 1) * heads].astype(BF)
+
+
+def context_product(place, contexts, tokens_b, y_size):
+    rows, depth = contexts[0].shape
+    groups = len(contexts)
     cols = tokens_b.shape[2]
     return pl.pallas_call(
         product_kernel,
-        out_shape=jax.ShapeDtypeStruct((rows, cols), BF),
-        in_specs=[pl.BlockSpec(memory_space=pltpu.VMEM)] * (len(contexts) + 1),
+        out_shape=jax.ShapeDtypeStruct((y_size, rows // y_size, cols), BF),
+        in_specs=[pl.BlockSpec(memory_space=pltpu.SMEM)] + [pl.BlockSpec(memory_space=pltpu.VMEM)] * (groups + 1),
         out_specs=pl.BlockSpec(memory_space=pltpu.VMEM),
         compiler_params=pltpu.CompilerParams(vmem_limit_bytes=16 * 2**20),
         cost_estimate=pl.CostEstimate(
             flops=2 * groups * rows * depth * cols, bytes_accessed=2 * groups * rows * depth, transcendentals=0
         ),
         name="context_product",
-    )(*contexts, tokens_b)
+    )(place, *contexts, tokens_b)
+
+
+def finish_kernel(mine_ref, came_ref, grad_ref, hidden_ref, columns_ref):
+    parts, _, width = mine_ref.shape
+    cols = columns_ref.shape[2]
+    for i in range(parts):
+        at = slice(i * width, (i + 1) * width)
+        hidden = grad_ref[:, at].astype(F32) + (mine_ref[i] + came_ref[i])
+        hidden_ref[:, at] = hidden
+        for j in range(width // cols):
+            columns_ref[i * (width // cols) + j] = hidden[:, j * cols:(j + 1) * cols].astype(BF)
+
+
+def finish(mine, came, grad_half, groups):
+    tok, width = grad_half.shape
+    vmem = pl.BlockSpec(memory_space=pltpu.VMEM)
+    return pl.pallas_call(
+        finish_kernel,
+        out_shape=(
+            jax.ShapeDtypeStruct((tok, width), F32),
+            jax.ShapeDtypeStruct((groups, tok, width // groups), BF),
+        ),
+        in_specs=[vmem] * 3,
+        out_specs=(vmem, vmem),
+        compiler_params=pltpu.CompilerParams(vmem_limit_bytes=8 * 2**20),
+        cost_estimate=pl.CostEstimate(flops=3 * tok * width, bytes_accessed=16 * tok * width, transcendentals=0),
+        name="finish",
+    )(mine, came, grad_half)
 
 
 def swap_pool(value):
@@ -125,37 +165,17 @@
     return lax.all_to_all(value, axes, split_axis=0, concat_axis=0, tiled=True)
 
 
+def shifted(value, axis, size, step):
+    return lax.ppermute(value, axis, tuple((s, (s + step) % size) for s in range(size)))
+
+
 def spread_over_y(context_t, y_index, y_size):
     wide = context_t.shape[1] // y_size
-    places = [
-        lax.dynamic_slice_in_dim(context_t, jnp.bitwise_xor(y_index, r) * wide, wide, 1)
-        for r in range(y_size)
-    ]
-    bit = 1
-    while bit < y_size:
-        crossing = [r for r in range(y_size) if r & bit]
-        came = lax.ppermute(
-            jnp.stack([places[r] for r in crossing]), "y", tuple((s, s ^ bit) for s in range(y_size))
-        )
-        for i, r in enumerate(crossing):
-            places[r] = came[i]
-        bit *= 2
-    order = jnp.bitwise_xor(y_index, jnp.arange(y_size, dtype=jnp.int32))
-    return jnp.take(jnp.stack(places), order, axis=0)
-
-
-def across_group(block, z_size, bit):
-    return lax.ppermute(block, "group", tuple((s, s ^ bit) for s in range(z_size)))
-
-
-def spread_over_group(pieces, z_index, z_size):
-    bit = z_size // 2
-    order = [0, bit]
-    while bit > 1:
-        bit //= 2
-        pieces = pieces + [across_group(jnp.concatenate(pieces, axis=0), z_size, bit)]
-        order += [r ^ bit for r in order]
-    return pieces, jnp.bitwise_xor(z_index, jnp.asarray(order, jnp.int32))
+    pieces = []
+    for step in range(y_size):
+        piece = lax.dynamic_slice_in_dim(context_t, lax.rem(y_index + step, y_size) * wide, wide, 1)
+        pieces.append(shifted(piece, "y", y_size, step) if step else piece)
+    return jnp.concatenate(pieces, axis=0)
 
 
 def per_device(moe_in, out_grad, gates, routes, w_gate, w_up, w_down, context_t):
@@ -195,12 +215,10 @@
     send, context_t, weights = lax.optimization_barrier((send, context_t, weights))
     received = exchange(send, ("y", "x"))
     other_gate, other_up, other_down = swap_pool(w_gate[0]), swap_pool(w_up[0]), swap_pool(w_down[0])
-    heads = context_t.shape[0]
-    context_y = spread_over_y(context_t, y_index, y_size).reshape(1, y_size * heads, -1)
-    z_index = lax.axis_index("group")
-    context_pair = [context_y, across_group(context_y, z_size, z_size // 2)]
-    received, context_pair = lax.optimization_barrier((received, context_pair))
-    context_all, group_order = spread_over_group(context_pair, z_index, z_size)
+    context_y = spread_over_y(context_t, y_index, y_size)
+    received, context_y = lax.optimization_barrier((received, context_y))
+    contexts = [shifted(context_y, "group", z_size, step) if step else context_y for step in range(z_size)]
+    place = jnp.stack([lax.axis_index("group"), y_index, jnp.int32(y_size)]).astype(jnp.int32)
 
     back_width = model_width * own_slots // ROWS
     back_parts = model_width // back_width
@@ -210,7 +228,7 @@
         back_width,
     ).reshape(experts, ROWS, back_width)
     returned = exchange(back, ("y", "x"))
-    returned, context_all = lax.optimization_barrier((returned, context_all))
+    returned, contexts[:6] = lax.optimization_barrier((returned, contexts[:6]))
 
     high = lax.reduce_precision(weights, 8, 7).astype(BF)
     low = (weights - high.astype(F32)).astype(BF)
@@ -224,23 +242,19 @@
     per_half = back_parts // 2
     mine = lax.dynamic_slice_in_dim(mixed, pool_index * per_half, per_half, 0)
     theirs = lax.dynamic_slice_in_dim(mixed, (1 - pool_index) * per_half, per_half, 0)
-    moe_part = mine + swap_pool(theirs)
-    moe_part = jnp.concatenate([moe_part[i] for i in range(per_half)], axis=1)
     grad_half = lax.dynamic_slice_in_dim(out_grad, pool_index * half_width, half_width, 1)
-    hidden_grad = grad_half.astype(F32) + moe_part
-    hidden_grad_b = hidden_grad.astype(BF)
+    hidden_grad, by_column = finish(mine, swap_pool(theirs), grad_half, z_size)
 
     cols = half_width // z_size
-    by_column = jnp.stack([hidden_grad_b[:, i * cols:(i + 1) * cols] for i in range(z_size)])
-    by_group = jnp.take(exchange(by_column, "group"), group_order, axis=0)
+    by_group = exchange(by_column, "group")
     gathered_b = exchange(
         jnp.broadcast_to(by_group[None], (x_size, z_size, tok_rows, cols)).reshape(
             x_size, z_size * tok_rows, cols
         ),
         "x",
     )
-    partial_wo = context_product(context_all, gathered_b)
-    terms = exchange(partial_wo.reshape(y_size, heads, cols), "y")
+    partial_wo = context_product(place, contexts, gathered_b, y_size)
+    terms = exchange(partial_wo, "y")
     wo_grad = jnp.sum(terms.astype(F32), axis=0)
     return (hidden_grad, wo_grad)
 

time: 185 us -> 183 us (0.989)
  starting transfers between devices: 82.4 us -> 113 us
  waiting for transfers between devices: 47.2 us -> 21.8 us
  local copies, waits for them, and re-layouts: 8.32 us -> 2.87 us
    ppermute x6 -> x14, starting transfers between devices: 37.5 us -> 65.8 us  [shifted(): lax.ppermute(value, axis, tuple(((s, (s + step) % size) for s in range(si...]
    ppermute x6 -> x14, waiting for transfers between devices: 38.1 us -> 20.6 us  [shifted(): lax.ppermute(value, axis, tuple(((s, (s + step) % size) for s in range(si...]
    all_to_all x3, waiting for transfers between devices: 8.02 us -> 0.01 us  [exchange(): return lax.all_to_all(value, axes, split_axis=0, concat_axis=0, tiled=True)]
    unnamed x21 -> x18, local copies, waits for them, and re-layouts: 5.05 us -> 0.95 us
    all_to_all x3, starting transfers between devices: 36.7 us -> 38.6 us  [exchange(): return lax.all_to_all(value, axes, split_axis=0, concat_axis=0, tiled=True)]
  transfers between devices with their start and end apart: 13 -> 21, of which waited for: 8 -> 9; matrix products, arithmetic and copies ran while one was open for 1% -> 0% of each run, Pallas kernels for 0% -> 0%
where the time goes in v3:
time: 183 us; the launch traced here: 182 us
  starting transfers between devices  113 us (62%)
  blocking collectives  30.2 us (17%)
  waiting for transfers between devices  21.8 us (12%)
  Pallas kernels  9.73 us (5%)
  local copies, waits for them, and re-layouts  2.87 us (2%)
    ppermute x14, starting transfers between devices, shifted(): lax.ppermute(value, axis, tuple(((s, (s + step) % size) for s in range(si...  65.8 us
    all_to_all x3, starting transfers between devices, exchange(): return lax.all_to_all(value, axes, split_axis=0, concat_axis=0, tiled=True)  38.6 us
    all_to_all x2, blocking collectives, exchange(): return lax.all_to_all(value, axes, split_axis=0, concat_axis=0, tiled=True)  30.2 us
    ppermute x14, waiting for transfers between devices, shifted(): lax.ppermute(value, axis, tuple(((s, (s + step) % size) for s in range(si...  20.6 us
    ppermute x4, starting transfers between devices, swap_pool(): return lax.ppermute(value, 'pool', ((0, 1), (1, 0)))  8.18 us
    pallas_call x1, Pallas kernels, expert_rows(): pl.pallas_call(expert_kernel, out_shape=jax.ShapeDtypeStruct((slots * wid...  8.12 us
  transfers between devices with their start and end apart: 21, of which 9 were waited for; matrix products, arithmetic and copies ran while one was open for 0% of the time, Pallas kernels for 0%

profile of v3, /device:TPU:2, one launch (start us, length us, event | category | flops | bytes accessed | tf_op | source)
XLA Modules:
  0.0 181.7 jit_solution(13323369575432524414)
XLA Ops:
  0.7 0.8 copy.23
  1.5 0.1 eq.52
  1.6 0.1 fusion.13
  1.7 0.2 reduce_window_sum.11
  1.8 0.2 select_reduce_fusion.1
  2.0 0.1 reduce_sum.39
  2.1 0.1 fusion.12
  2.2 0.1 copy.25
  2.4 0.3 broadcast_multiply_fusion
  2.6 0.3 mul.89
  3.0 0.1 copy.26
  3.0 0.1 select_reduce_fusion
  3.2 0.0 copy-start
  3.2 0.0 copy-start.2
  3.2 1.4 fusion
  4.6 17.3 %all-to-all-start = ((bf16[64,8,1024]{2,1,0:T(8,128)(2,1)}), bf16[64,8,1024]{2,1,0:T(8,128)(2,1)S(1)}, u32[]{:S(2)}, u32[]{:S(2)}) async-start(bf16[64,8,1024]{2,1,0:T(8,128)(2,1)} %fusion), calls=%async_computation | async-start | bytes 2097152 | tf_op jit(solution)/shard_map/all_to_all | solution.py:165
  21.9 1.9 %collective-permute-start.7 = (bf16[2048,384]{1,0:T(8,128)(2,1)S(1)}, bf16[2048,384]{1,0:T(8,128)(2,1)}, u32[]{:S(2)}, u32[]{:S(2)}) collective-permute-start(bf16[2048,384]{1,0:T(8,128)(2,1)S(1)} %bitcast.26), channel_id=1, source_target_pairs={{0,512},{512,0},{1,513},{513,1},{2,514},{514,2},{3,515},{515,3},{4... | collective-permute-start | bytes 4718600 | tf_op jit(solution)/shard_map/ppermute | solution.py:161
  23.8 2.4 %collective-permute-start.8 = (bf16[2048,384]{1,0:T(8,128)(2,1)}, bf16[2048,384]{1,0:T(8,128)(2,1)}, u32[]{:S(2)}, u32[]{:S(2)}) collective-permute-start(bf16[2048,384]{1,0:T(8,128)(2,1)} %bitcast.28), channel_id=1, source_target_pairs={{0,512},{512,0},{1,513},{513,1},{2,514},{514,2},{3,515},{515,3},{4... | collective-permute-start | bytes 4718600 | tf_op jit(solution)/shard_map/ppermute | solution.py:161
  26.2 1.9 %collective-permute-start.9 = (bf16[384,2048]{1,0:T(8,128)(2,1)}, bf16[384,2048]{1,0:T(8,128)(2,1)}, u32[]{:S(2)}, u32[]{:S(2)}) collective-permute-start(bf16[384,2048]{1,0:T(8,128)(2,1)} %bitcast.30), channel_id=1, source_target_pairs={{0,512},{512,0},{1,513},{513,1},{2,514},{514,2},{3,515},{515,3},{4... | collective-permute-start | bytes 4718600 | tf_op jit(solution)/shard_map/ppermute | solution.py:161
  28.2 0.1 constant_dynamic-slice_fusion.3
  28.3 3.4 %collective-permute-start = (bf16[64,128]{1,0:T(8,128)(2,1)S(1)}, bf16[64,128]{1,0:T(8,128)(2,1)S(1)}, u32[]{:S(2)}, u32[]{:S(2)}) collective-permute-start(bf16[64,128]{1,0:T(8,128)(2,1)S(1)} %get-tuple-element.38), channel_id=1, source_target_pairs={{0,8},{8,16},{16,24},{24,32},{32,40},{40,48},{48,56},{56,0},{1,9},... | collective-permute-start | bytes 49160 | tf_op jit(solution)/shard_map/ppermute | solution.py:169
  31.7 4.4 %collective-permute-start.1 = (bf16[64,128]{1,0:T(8,128)(2,1)S(1)}, bf16[64,128]{1,0:T(8,128)(2,1)S(1)}, u32[]{:S(2)}, u32[]{:S(2)}) collective-permute-start(bf16[64,128]{1,0:T(8,128)(2,1)S(1)} %get-tuple-element.37), channel_id=1, source_target_pairs={{0,16},{8,24},{16,32},{24,40},{32,48},{40,56},{48,0},{56,8},{1,17}... | collective-permute-start | bytes 49160 | tf_op jit(solution)/shard_map/ppermute | solution.py:169
  36.1 5.7 %collective-permute-done = bf16[64,128]{1,0:T(8,128)(2,1)S(1)} collective-permute-done((bf16[64,128]{1,0:T(8,128)(2,1)S(1)}, bf16[64,128]{1,0:T(8,128)(2,1)S(1)}, u32[]{:S(2)}, u32[]{:S(2)}) %collective-permute-start) | collective-permute-done | bytes 16416 | tf_op jit(solution)/shard_map/ppermute | solution.py:169
  41.8 1.9 %collective-permute-start.2 = (bf16[64,128]{1,0:T(8,128)(2,1)S(1)}, bf16[64,128]{1,0:T(8,128)(2,1)S(1)}, u32[]{:S(2)}, u32[]{:S(2)}) collective-permute-start(bf16[64,128]{1,0:T(8,128)(2,1)S(1)} %get-tuple-element.36), channel_id=1, source_target_pairs={{0,24},{8,32},{16,40},{24,48},{32,56},{40,0},{48,8},{56,16},{1,25}... | collective-permute-start | bytes 49160 | tf_op jit(solution)/shard_map/ppermute | solution.py:169
  43.8 5.8 %collective-permute-start.3 = (bf16[64,128]{1,0:T(8,128)(2,1)S(1)}, bf16[64,128]{1,0:T(8,128)(2,1)S(1)}, u32[]{:S(2)}, u32[]{:S(2)}) collective-permute-start(bf16[64,128]{1,0:T(8,128)(2,1)S(1)} %get-tuple-element.35), channel_id=1, source_target_pairs={{0,32},{8,40},{16,48},{24,56},{32,0},{40,8},{48,16},{56,24},{1,33}... | collective-permute-start | bytes 49160 | tf_op jit(solution)/shard_map/ppermute | solution.py:169
  49.6 0.9 collective-permute-done.2
  50.5 2.2 %collective-permute-start.4 = (bf16[64,128]{1,0:T(8,128)(2,1)S(1)}, bf16[64,128]{1,0:T(8,128)(2,1)S(1)}, u32[]{:S(2)}, u32[]{:S(2)}) collective-permute-start(bf16[64,128]{1,0:T(8,128)(2,1)S(1)} %get-tuple-element.34), channel_id=1, source_target_pairs={{0,40},{8,48},{16,56},{24,0},{32,8},{40,16},{48,24},{56,32},{1,41}... | collective-permute-start | bytes 49160 | tf_op jit(solution)/shard_map/ppermute | solution.py:169
  52.7 0.8 collective-permute-done.3
  53.5 4.4 %collective-permute-start.5 = (bf16[64,128]{1,0:T(8,128)(2,1)S(1)}, bf16[64,128]{1,0:T(8,128)(2,1)S(1)}, u32[]{:S(2)}, u32[]{:S(2)}) collective-permute-start(bf16[64,128]{1,0:T(8,128)(2,1)S(1)} %get-tuple-element.33), channel_id=1, source_target_pairs={{0,48},{8,56},{16,0},{24,8},{32,16},{40,24},{48,32},{56,40},{1,49}... | collective-permute-start | bytes 49160 | tf_op jit(solution)/shard_map/ppermute | solution.py:169
  57.9 0.0 collective-permute-done.4
  57.9 4.8 %collective-permute-start.6 = (bf16[64,128]{1,0:T(8,128)(2,1)S(1)}, bf16[64,128]{1,0:T(8,128)(2,1)S(1)}, u32[]{:S(2)}, u32[]{:S(2)}) collective-permute-start(bf16[64,128]{1,0:T(8,128)(2,1)S(1)} %get-tuple-element.32), channel_id=1, source_target_pairs={{0,56},{8,0},{16,8},{24,16},{32,24},{40,32},{48,40},{56,48},{1,57}... | collective-permute-start | bytes 49160 | tf_op jit(solution)/shard_map/ppermute | solution.py:169
  62.8 0.0 collective-permute-done.5
  62.8 1.7 collective-permute-done.6
  64.6 0.0 all-to-all-done
  64.6 0.0 collective-permute-done.9.refs_5_
  64.6 8.1 %expert.1 = bf16[512,512]{1,0:T(8,128)(2,1)} custom-call(bf16[512,1024]{1,0:T(8,128)(2,1)S(1)} %bitcast.25, bf16[2048,384]{1,0:T(8,128)(2,1)S(1)} %bitcast.27, bf16[2048,384]{1,0:T(8,128)(2,1)} %bitcast.29, bf16[384,2048]{1,0:T(8,128)(2,1)} %bitcast.31, bf16[2048,384]{1,0:T(8,128)(2,1)} %collective-permute-done.7.refs_3_, ...), custom_call_target="tpu_custom_call" | custom-call | flops 2013265920 | bytes 9437184 | tf_op jit(solution)/shard_map/expert/pallas_call | solution.py:82
  72.7 14.2 %all-to-all-start.1 = ((bf16[64,8,512]{2,1,0:T(8,128)(2,1)}), bf16[64,8,512]{2,1,0:T(8,128)(2,1)S(1)}, u32[]{:S(2)}, u32[]{:S(2)}) async-start(bf16[64,8,512]{2,1,0:T(8,128)(2,1)} %bitcast.9), calls=%async_computation.1 | async-start | bytes 1048576 | tf_op jit(solution)/shard_map/all_to_all | solution.py:165
  86.9 5.4 %collective-permute-start.10 = (bf16[512,128]{1,0:T(8,128)(2,1)S(1)}, bf16[512,128]{1,0:T(8,128)(2,1)S(1)}, u32[]{:S(2)}, u32[]{:S(2)}) collective-permute-start(bf16[512,128]{1,0:T(8,128)(2,1)S(1)} %constant_dynamic-update-slice_fusion.refs_0_), channel_id=1, source_target_pairs={{0,64},{64,128},{128,192},{192,256},{256,320},{320,384},{384,448},... | collective-permute-start | bytes 393224 | tf_op jit(solution)/shard_map/ppermute | solution.py:169
  92.3 7.9 %collective-permute-start.11 = (bf16[512,128]{1,0:T(8,128)(2,1)S(1)}, bf16[512,128]{1,0:T(8,128)(2,1)S(1)}, u32[]{:S(2)}, u32[]{:S(2)}) collective-permute-start(bf16[512,128]{1,0:T(8,128)(2,1)S(1)} %constant_dynamic-update-slice_fusion.refs_0_), channel_id=1, source_target_pairs={{0,128},{64,192},{128,256},{192,320},{256,384},{320,448},{384,0},{... | collective-permute-start | bytes 393224 | tf_op jit(solution)/shard_map/ppermute | solution.py:169
  100.2 10.0 %collective-permute-start.12 = (bf16[512,128]{1,0:T(8,128)(2,1)S(1)}, bf16[512,128]{1,0:T(8,128)(2,1)S(1)}, u32[]{:S(2)}, u32[]{:S(2)}) collective-permute-start(bf16[512,128]{1,0:T(8,128)(2,1)S(1)} %constant_dynamic-update-slice_fusion.refs_0_), channel_id=1, source_target_pairs={{0,192},{64,256},{128,320},{192,384},{256,448},{320,0},{384,64},{4... | collective-permute-start | bytes 393224 | tf_op jit(solution)/shard_map/ppermute | solution.py:169
  110.3 3.7 %collective-permute-start.13 = (bf16[512,128]{1,0:T(8,128)(2,1)S(1)}, bf16[512,128]{1,0:T(8,128)(2,1)S(1)}, u32[]{:S(2)}, u32[]{:S(2)}) collective-permute-start(bf16[512,128]{1,0:T(8,128)(2,1)S(1)} %constant_dynamic-update-slice_fusion.refs_0_), channel_id=1, source_target_pairs={{0,256},{64,320},{128,384},{192,448},{256,0},{320,64},{384,128},{4... | collective-permute-start | bytes 393224 | tf_op jit(solution)/shard_map/ppermute | solution.py:169
  114.0 6.9 %collective-permute-start.14 = (bf16[512,128]{1,0:T(8,128)(2,1)S(1)}, bf16[512,128]{1,0:T(8,128)(2,1)S(1)}, u32[]{:S(2)}, u32[]{:S(2)}) collective-permute-start(bf16[512,128]{1,0:T(8,128)(2,1)S(1)} %constant_dynamic-update-slice_fusion.refs_0_), channel_id=1, source_target_pairs={{0,320},{64,384},{128,448},{192,0},{256,64},{320,128},{384,192},{4... | collective-permute-start | bytes 393224 | tf_op jit(solution)/shard_map/ppermute | solution.py:169
  121.0 0.1 copy.27
  121.1 0.1 mul.90
  121.2 0.1 copy.28
  121.3 0.2 mul.94
  121.5 0.0 collective-permute-done.11.refs_2_
  121.5 1.3 collective-permute-done.13.refs_4_
  122.9 3.3 %collective-permute-done.14.refs_5_ = bf16[512,128]{1,0:T(8,128)(2,1)S(1)} collective-permute-done((bf16[512,128]{1,0:T(8,128)(2,1)S(1)}, bf16[512,128]{1,0:T(8,128)(2,1)S(1)}, u32[]{:S(2)}, u32[]{:S(2)}) %collective-permute-start.14) | collective-permute-done | bytes 131104 | tf_op jit(solution)/shard_map/ppermute | solution.py:169
  126.1 0.2 convolution_reduce_fusion
  126.4 1.9 %collective-permute-start.15 = (f32[2,16,512]{2,1,0:T(8,128)S(1)}, f32[2,16,512]{2,1,0:T(8,128)S(1)}, u32[]{:S(2)}, u32[]{:S(2)}) collective-permute-start(f32[2,16,512]{2,1,0:T(8,128)S(1)} %get-tuple-element.30), channel_id=1, source_target_pairs={{0,512},{512,0},{1,513},{513,1},{2,514},{514,2},{3,515},{515,3},{4... | collective-permute-start | bytes 196616 | tf_op jit(solution)/shard_map/ppermute | solution.py:161
  128.3 1.2 collective-permute-done.15.came_ref
  129.6 0.6 finish.1
  130.2 14.5 %all_to_all.25 = bf16[8,16,128]{2,1,0:T(8,128)(2,1)S(1)} all-to-all(bf16[8,16,128]{2,1,0:T(8,128)(2,1)S(1)} %get-tuple-element.29), channel_id=1, replica_groups=mesh['pool'=2,'group'=8,'y'=8,'x'=8] {'group'}, dimensions={0} | all-to-all | bytes 65536 | tf_op jit(solution)/shard_map/all_to_all | solution.py:165
  144.7 0.7 broadcast_in_dim.32
  145.5 7.2 %all-to-all-start.3 = ((bf16[8,128,128]{2,1,0:T(8,128)(2,1)}), bf16[8,128,128]{2,1,0:T(8,128)(2,1)S(1)}, u32[]{:S(2)}, u32[]{:S(2)}) async-start(bf16[8,128,128]{2,1,0:T(8,128)(2,1)} %broadcast_in_dim.32), calls=%async_computation.3 | async-start | bytes 524288 | tf_op jit(solution)/shard_map/all_to_all | solution.py:165
  152.7 2.4 %collective-permute-start.16 = (bf16[512,128]{1,0:T(8,128)(2,1)S(1)}, bf16[512,128]{1,0:T(8,128)(2,1)S(1)}, u32[]{:S(2)}, u32[]{:S(2)}) collective-permute-start(bf16[512,128]{1,0:T(8,128)(2,1)S(1)} %constant_dynamic-update-slice_fusion.refs_0_), channel_id=1, source_target_pairs={{0,384},{64,448},{128,0},{192,64},{256,128},{320,192},{384,256},{4... | collective-permute-start | bytes 393224 | tf_op jit(solution)/shard_map/ppermute | solution.py:169
  155.1 2.4 %collective-permute-start.17 = (bf16[512,128]{1,0:T(8,128)(2,1)S(1)}, bf16[512,128]{1,0:T(8,128)(2,1)S(1)}, u32[]{:S(2)}, u32[]{:S(2)}) collective-permute-start(bf16[512,128]{1,0:T(8,128)(2,1)S(1)} %constant_dynamic-update-slice_fusion.refs_0_), channel_id=1, source_target_pairs={{0,448},{64,0},{128,64},{192,128},{256,192},{320,256},{384,320},{4... | collective-permute-start | bytes 393224 | tf_op jit(solution)/shard_map/ppermute | solution.py:169
  157.6 0.1 pad_add_fusion.place_ref
  157.6 5.1 %collective-permute-done.16.refs_6_ = bf16[512,128]{1,0:T(8,128)(2,1)S(1)} collective-permute-done((bf16[512,128]{1,0:T(8,128)(2,1)S(1)}, bf16[512,128]{1,0:T(8,128)(2,1)S(1)}, u32[]{:S(2)}, u32[]{:S(2)}) %collective-permute-start.16) | collective-permute-done | bytes 131104 | tf_op jit(solution)/shard_map/ppermute | solution.py:169
  162.7 1.8 collective-permute-done.17.refs_7_
  164.5 1.0 context_product.1
  165.5 15.6 %all_to_all.26 = bf16[8,64,128]{2,1,0:T(8,128)(2,1)S(1)} all-to-all(bf16[8,64,128]{2,1,0:T(8,128)(2,1)S(1)} %context_product.1), channel_id=1, replica_groups=mesh['pool'=2,'group'=8,'y'=8,'x'=8] {'y'}, dimensions={0} | all-to-all | bytes 262144 | tf_op jit(solution)/shard_map/all_to_all | solution.py:165
  181.1 0.6 convert_reduce_fusion
  (30 shorter events, 0.2 us)
Async XLA Ops:
  0.6 2.3 %copy-start.4 = (f32[16,8]{0,1:T(8,128)S(1)}, f32[16,8]{0,1:T(8,128)}, u32[]{:S(2)}) copy-start(f32[16,8]{0,1:T(8,128)} %param.10) | copy-start | bytes 1540
  0.6 2.5 %copy-start.3 = (bf16[16,2048]{1,0:T(8,128)(2,1)S(1)}, bf16[16,2048]{1,0:T(8,128)(2,1)}, u32[]{:S(2)}) copy-start(bf16[16,2048]{1,0:T(8,128)(2,1)} %param.8) | copy-start | bytes 196612
  0.6 2.5 %copy-start.1 = (bf16[16,2048]{1,0:T(8,128)(2,1)S(1)}, bf16[16,2048]{1,0:T(8,128)(2,1)}, u32[]{:S(2)}) copy-start(bf16[16,2048]{1,0:T(8,128)(2,1)} %param.9) | copy-start | bytes 196612
  3.2 18.7 %copy-start = (bf16[1,2048,384]{2,1,0:T(8,128)(2,1)S(1)}, bf16[1,2048,384]{2,1,0:T(8,128)(2,1)}, u32[]{:S(2)}) copy-start(bf16[1,2048,384]{2,1,0:T(8,128)(2,1)} %param.12) | copy-start | bytes 4718596
  3.2 25.0 %copy-start.2 = (bf16[64,1024]{1,0:T(8,128)(2,1)S(1)}, bf16[64,1024]{1,0:T(8,128)(2,1)}, u32[]{:S(2)}) copy-start(bf16[64,1024]{1,0:T(8,128)(2,1)} %param.15) | copy-start | bytes 393220
  4.6 59.9 %all-to-all-start = ((bf16[64,8,1024]{2,1,0:T(8,128)(2,1)}), bf16[64,8,1024]{2,1,0:T(8,128)(2,1)S(1)}, u32[]{:S(2)}, u32[]{:S(2)}) async-start(bf16[64,8,1024]{2,1,0:T(8,128)(2,1)} %fusion), calls=%async_computation | async-start | bytes 2097152 | tf_op jit(solution)/shard_map/all_to_all | solution.py:165
  21.9 42.7 %collective-permute-start.7 = (bf16[2048,384]{1,0:T(8,128)(2,1)S(1)}, bf16[2048,384]{1,0:T(8,128)(2,1)}, u32[]{:S(2)}, u32[]{:S(2)}) collective-permute-start(bf16[2048,384]{1,0:T(8,128)(2,1)S(1)} %bitcast.26), channel_id=1, source_target_pairs={{0,512},{512,0},{1,513},{513,1},{2,514},{514,2},{3,515},{515,3},{4... | collective-permute-start | bytes 4718600 | tf_op jit(solution)/shard_map/ppermute | solution.py:161
  23.8 40.7 %collective-permute-start.8 = (bf16[2048,384]{1,0:T(8,128)(2,1)}, bf16[2048,384]{1,0:T(8,128)(2,1)}, u32[]{:S(2)}, u32[]{:S(2)}) collective-permute-start(bf16[2048,384]{1,0:T(8,128)(2,1)} %bitcast.28), channel_id=1, source_target_pairs={{0,512},{512,0},{1,513},{513,1},{2,514},{514,2},{3,515},{515,3},{4... | collective-permute-start | bytes 4718600 | tf_op jit(solution)/shard_map/ppermute | solution.py:161
  26.2 38.3 %collective-permute-start.9 = (bf16[384,2048]{1,0:T(8,128)(2,1)}, bf16[384,2048]{1,0:T(8,128)(2,1)}, u32[]{:S(2)}, u32[]{:S(2)}) collective-permute-start(bf16[384,2048]{1,0:T(8,128)(2,1)} %bitcast.30), channel_id=1, source_target_pairs={{0,512},{512,0},{1,513},{513,1},{2,514},{514,2},{3,515},{515,3},{4... | collective-permute-start | bytes 4718600 | tf_op jit(solution)/shard_map/ppermute | solution.py:161
  28.3 13.5 %collective-permute-start = (bf16[64,128]{1,0:T(8,128)(2,1)S(1)}, bf16[64,128]{1,0:T(8,128)(2,1)S(1)}, u32[]{:S(2)}, u32[]{:S(2)}) collective-permute-start(bf16[64,128]{1,0:T(8,128)(2,1)S(1)} %get-tuple-element.38), channel_id=1, source_target_pairs={{0,8},{8,16},{16,24},{24,32},{32,40},{40,48},{48,56},{56,0},{1,9},... | collective-permute-start | bytes 49160 | tf_op jit(solution)/shard_map/ppermute | solution.py:169
  31.7 12.0 %collective-permute-start.1 = (bf16[64,128]{1,0:T(8,128)(2,1)S(1)}, bf16[64,128]{1,0:T(8,128)(2,1)S(1)}, u32[]{:S(2)}, u32[]{:S(2)}) collective-permute-start(bf16[64,128]{1,0:T(8,128)(2,1)S(1)} %get-tuple-element.37), channel_id=1, source_target_pairs={{0,16},{8,24},{16,32},{24,40},{32,48},{40,56},{48,0},{56,8},{1,17}... | collective-permute-start | bytes 49160 | tf_op jit(solution)/shard_map/ppermute | solution.py:169
  41.8 8.6 %collective-permute-start.2 = (bf16[64,128]{1,0:T(8,128)(2,1)S(1)}, bf16[64,128]{1,0:T(8,128)(2,1)S(1)}, u32[]{:S(2)}, u32[]{:S(2)}) collective-permute-start(bf16[64,128]{1,0:T(8,128)(2,1)S(1)} %get-tuple-element.36), channel_id=1, source_target_pairs={{0,24},{8,32},{16,40},{24,48},{32,56},{40,0},{48,8},{56,16},{1,25}... | collective-permute-start | bytes 49160 | tf_op jit(solution)/shard_map/ppermute | solution.py:169
  43.8 9.7 %collective-permute-start.3 = (bf16[64,128]{1,0:T(8,128)(2,1)S(1)}, bf16[64,128]{1,0:T(8,128)(2,1)S(1)}, u32[]{:S(2)}, u32[]{:S(2)}) collective-permute-start(bf16[64,128]{1,0:T(8,128)(2,1)S(1)} %get-tuple-element.35), channel_id=1, source_target_pairs={{0,32},{8,40},{16,48},{24,56},{32,0},{40,8},{48,16},{56,24},{1,33}... | collective-permute-start | bytes 49160 | tf_op jit(solution)/shard_map/ppermute | solution.py:169
  50.5 7.4 %collective-permute-start.4 = (bf16[64,128]{1,0:T(8,128)(2,1)S(1)}, bf16[64,128]{1,0:T(8,128)(2,1)S(1)}, u32[]{:S(2)}, u32[]{:S(2)}) collective-permute-start(bf16[64,128]{1,0:T(8,128)(2,1)S(1)} %get-tuple-element.34), channel_id=1, source_target_pairs={{0,40},{8,48},{16,56},{24,0},{32,8},{40,16},{48,24},{56,32},{1,41}... | collective-permute-start | bytes 49160 | tf_op jit(solution)/shard_map/ppermute | solution.py:169
  53.5 9.3 %collective-permute-start.5 = (bf16[64,128]{1,0:T(8,128)(2,1)S(1)}, bf16[64,128]{1,0:T(8,128)(2,1)S(1)}, u32[]{:S(2)}, u32[]{:S(2)}) collective-permute-start(bf16[64,128]{1,0:T(8,128)(2,1)S(1)} %get-tuple-element.33), channel_id=1, source_target_pairs={{0,48},{8,56},{16,0},{24,8},{32,16},{40,24},{48,32},{56,40},{1,49}... | collective-permute-start | bytes 49160 | tf_op jit(solution)/shard_map/ppermute | solution.py:169
  57.9 6.6 %collective-permute-start.6 = (bf16[64,128]{1,0:T(8,128)(2,1)S(1)}, bf16[64,128]{1,0:T(8,128)(2,1)S(1)}, u32[]{:S(2)}, u32[]{:S(2)}) collective-permute-start(bf16[64,128]{1,0:T(8,128)(2,1)S(1)} %get-tuple-element.32), channel_id=1, source_target_pairs={{0,56},{8,0},{16,8},{24,16},{32,24},{40,32},{48,40},{56,48},{1,57}... | collective-permute-start | bytes 49160 | tf_op jit(solution)/shard_map/ppermute | solution.py:169
  72.7 53.4 %all-to-all-start.1 = ((bf16[64,8,512]{2,1,0:T(8,128)(2,1)}), bf16[64,8,512]{2,1,0:T(8,128)(2,1)S(1)}, u32[]{:S(2)}, u32[]{:S(2)}) async-start(bf16[64,8,512]{2,1,0:T(8,128)(2,1)} %bitcast.9), calls=%async_computation.1 | async-start | bytes 1048576 | tf_op jit(solution)/shard_map/all_to_all | solution.py:165
  86.9 34.6 %collective-permute-start.10 = (bf16[512,128]{1,0:T(8,128)(2,1)S(1)}, bf16[512,128]{1,0:T(8,128)(2,1)S(1)}, u32[]{:S(2)}, u32[]{:S(2)}) collective-permute-start(bf16[512,128]{1,0:T(8,128)(2,1)S(1)} %constant_dynamic-update-slice_fusion.refs_0_), channel_id=1, source_target_pairs={{0,64},{64,128},{128,192},{192,256},{256,320},{320,384},{384,448},... | collective-permute-start | bytes 393224 | tf_op jit(solution)/shard_map/ppermute | solution.py:169
  92.3 29.2 %collective-permute-start.11 = (bf16[512,128]{1,0:T(8,128)(2,1)S(1)}, bf16[512,128]{1,0:T(8,128)(2,1)S(1)}, u32[]{:S(2)}, u32[]{:S(2)}) collective-permute-start(bf16[512,128]{1,0:T(8,128)(2,1)S(1)} %constant_dynamic-update-slice_fusion.refs_0_), channel_id=1, source_target_pairs={{0,128},{64,192},{128,256},{192,320},{256,384},{320,448},{384,0},{... | collective-permute-start | bytes 393224 | tf_op jit(solution)/shard_map/ppermute | solution.py:169
  100.2 21.3 %collective-permute-start.12 = (bf16[512,128]{1,0:T(8,128)(2,1)S(1)}, bf16[512,128]{1,0:T(8,128)(2,1)S(1)}, u32[]{:S(2)}, u32[]{:S(2)}) collective-permute-start(bf16[512,128]{1,0:T(8,128)(2,1)S(1)} %constant_dynamic-update-slice_fusion.refs_0_), channel_id=1, source_target_pairs={{0,192},{64,256},{128,320},{192,384},{256,448},{320,0},{384,64},{4... | collective-permute-start | bytes 393224 | tf_op jit(solution)/shard_map/ppermute | solution.py:169
  110.3 12.6 %collective-permute-start.13 = (bf16[512,128]{1,0:T(8,128)(2,1)S(1)}, bf16[512,128]{1,0:T(8,128)(2,1)S(1)}, u32[]{:S(2)}, u32[]{:S(2)}) collective-permute-start(bf16[512,128]{1,0:T(8,128)(2,1)S(1)} %constant_dynamic-update-slice_fusion.refs_0_), channel_id=1, source_target_pairs={{0,256},{64,320},{128,384},{192,448},{256,0},{320,64},{384,128},{4... | collective-permute-start | bytes 393224 | tf_op jit(solution)/shard_map/ppermute | solution.py:169
  114.0 12.1 %collective-permute-start.14 = (bf16[512,128]{1,0:T(8,128)(2,1)S(1)}, bf16[512,128]{1,0:T(8,128)(2,1)S(1)}, u32[]{:S(2)}, u32[]{:S(2)}) collective-permute-start(bf16[512,128]{1,0:T(8,128)(2,1)S(1)} %constant_dynamic-update-slice_fusion.refs_0_), channel_id=1, source_target_pairs={{0,320},{64,384},{128,448},{192,0},{256,64},{320,128},{384,192},{4... | collective-permute-start | bytes 393224 | tf_op jit(solution)/shard_map/ppermute | solution.py:169
  126.4 3.1 %collective-permute-start.15 = (f32[2,16,512]{2,1,0:T(8,128)S(1)}, f32[2,16,512]{2,1,0:T(8,128)S(1)}, u32[]{:S(2)}, u32[]{:S(2)}) collective-permute-start(f32[2,16,512]{2,1,0:T(8,128)S(1)} %get-tuple-element.30), channel_id=1, source_target_pairs={{0,512},{512,0},{1,513},{513,1},{2,514},{514,2},{3,515},{515,3},{4... | collective-permute-start | bytes 196616 | tf_op jit(solution)/shard_map/ppermute | solution.py:161
  145.5 19.0 %all-to-all-start.3 = ((bf16[8,128,128]{2,1,0:T(8,128)(2,1)}), bf16[8,128,128]{2,1,0:T(8,128)(2,1)S(1)}, u32[]{:S(2)}, u32[]{:S(2)}) async-start(bf16[8,128,128]{2,1,0:T(8,128)(2,1)} %broadcast_in_dim.32), calls=%async_computation.3 | async-start | bytes 524288 | tf_op jit(solution)/shard_map/all_to_all | solution.py:165
  152.7 10.1 %collective-permute-start.16 = (bf16[512,128]{1,0:T(8,128)(2,1)S(1)}, bf16[512,128]{1,0:T(8,128)(2,1)S(1)}, u32[]{:S(2)}, u32[]{:S(2)}) collective-permute-start(bf16[512,128]{1,0:T(8,128)(2,1)S(1)} %constant_dynamic-update-slice_fusion.refs_0_), channel_id=1, source_target_pairs={{0,384},{64,448},{128,0},{192,64},{256,128},{320,192},{384,256},{4... | collective-permute-start | bytes 393224 | tf_op jit(solution)/shard_map/ppermute | solution.py:169
  155.1 9.4 %collective-permute-start.17 = (bf16[512,128]{1,0:T(8,128)(2,1)S(1)}, bf16[512,128]{1,0:T(8,128)(2,1)S(1)}, u32[]{:S(2)}, u32[]{:S(2)}) collective-permute-start(bf16[512,128]{1,0:T(8,128)(2,1)S(1)} %constant_dynamic-update-slice_fusion.refs_0_), channel_id=1, source_target_pairs={{0,448},{64,0},{128,64},{192,128},{256,192},{320,256},{384,320},{4... | collective-permute-start | bytes 393224 | tf_op jit(solution)/shard_map/ppermute | solution.py:169

commit v4 on v3

--- a/solution.py
+++ b/solution.py
@@ -98,28 +98,29 @@
 def product_kernel(place_ref, *refs):
     contexts, tokens_ref, out_ref = refs[:-2], refs[-2], refs[-1]
     x_size, depth, cols = tokens_ref.shape
-    z_size = len(contexts)
+    z_size = sum(ref.shape[0] for ref in contexts)
     tok = depth // z_size
-    z_index, y_index, y_size = place_ref[0], place_ref[1], place_ref[2]
+    z_index, y_index = place_ref[0], place_ref[1]
     total = None
-    for step, ref in enumerate(contexts):
-        at = pl.multiple_of(lax.rem(z_index + z_size - step, z_size) * tok, tok)
+    for (ref, i), apart in zip(((ref, i) for ref in contexts for i in range(ref.shape[0])), doubled(z_size)):
+        at = pl.multiple_of(jnp.bitwise_xor(z_index, apart) * tok, tok)
         tokens = tokens_ref[:, pl.ds(at, tok), :].reshape(x_size * tok, cols)
-        term = dot_f32(ref[...], tokens)
+        term = dot_f32(ref[i], tokens)
         total = term if total is None else total + term
     heads = out_ref.shape[1]
-    for step in range(out_ref.shape[0]):
-        out_ref[lax.rem(y_index + y_size - step, y_size)] = total[step * heads:(step + 1) * heads].astype(BF)
+    for apart in range(out_ref.shape[0]):
+        out_ref[jnp.bitwise_xor(y_index, apart)] = total[apart * heads:(apart + 1) * heads].astype(BF)
 
 
 def context_product(place, contexts, tokens_b, y_size):
-    rows, depth = contexts[0].shape
-    groups = len(contexts)
+    rows, depth = contexts[0].shape[1:]
+    groups = sum(c.shape[0] for c in contexts)
     cols = tokens_b.shape[2]
     return pl.pallas_call(
         product_kernel,
         out_shape=jax.ShapeDtypeStruct((y_size, rows // y_size, cols), BF),
-        in_specs=[pl.BlockSpec(memory_space=pltpu.SMEM)] + [pl.BlockSpec(memory_space=pltpu.VMEM)] * (groups + 1),
+        in_specs=[pl.BlockSpec(memory_space=pltpu.SMEM)]
+        + [pl.BlockSpec(memory_space=pltpu.VMEM)] * (len(contexts) + 1),
         out_specs=pl.BlockSpec(memory_space=pltpu.VMEM),
         compiler_params=pltpu.CompilerParams(vmem_limit_bytes=16 * 2**20),
         cost_estimate=pl.CostEstimate(
@@ -165,17 +166,32 @@
     return lax.all_to_all(value, axes, split_axis=0, concat_axis=0, tiled=True)
 
 
-def shifted(value, axis, size, step):
-    return lax.ppermute(value, axis, tuple((s, (s + step) % size) for s in range(size)))
+def swapped(value, axis, size, bit):
+    return lax.ppermute(value, axis, tuple((s, s ^ bit) for s in range(size)))
 
 
 def spread_over_y(context_t, y_index, y_size):
     wide = context_t.shape[1] // y_size
-    pieces = []
-    for step in range(y_size):
-        piece = lax.dynamic_slice_in_dim(context_t, lax.rem(y_index + step, y_size) * wide, wide, 1)
-        pieces.append(shifted(piece, "y", y_size, step) if step else piece)
-    return jnp.concatenate(pieces, axis=0)
+    places = [
+        lax.dynamic_slice_in_dim(context_t, jnp.bitwise_xor(y_index, r) * wide, wide, 1)
+        for r in range(y_size)
+    ]
+    bit = 1
+    while bit < y_size:
+        crossing = [r for r in range(y_size) if r & bit]
+        came = swapped(jnp.stack([places[r] for r in crossing]), "y", y_size, bit)
+        for i, r in enumerate(crossing):
+            places[r] = came[i]
+        bit *= 2
+    return jnp.concatenate(places, axis=0)[None]
+
+
+def doubled(size):
+    order, bit = [0], size // 2
+    while bit:
+        order += [r ^ bit for r in order]
+        bit //= 2
+    return order
 
 
 def per_device(moe_in, out_grad, gates, routes, w_gate, w_up, w_down, context_t):
@@ -212,13 +228,19 @@
         experts * ROWS, parts * tok_rows
     )
     send = dot_f32(spread, stacked).astype(BF).reshape(experts, ROWS, piece_width)
-    send, context_t, weights = lax.optimization_barrier((send, context_t, weights))
+    context_y = spread_over_y(context_t, y_index, y_size)
+    send, weights, context_y = lax.optimization_barrier((send, weights, context_y))
     received = exchange(send, ("y", "x"))
-    other_gate, other_up, other_down = swap_pool(w_gate[0]), swap_pool(w_up[0]), swap_pool(w_down[0])
-    context_y = spread_over_y(context_t, y_index, y_size)
-    received, context_y = lax.optimization_barrier((received, context_y))
-    contexts = [shifted(context_y, "group", z_size, step) if step else context_y for step in range(z_size)]
-    place = jnp.stack([lax.axis_index("group"), y_index, jnp.int32(y_size)]).astype(jnp.int32)
+    contexts, bit = [context_y, swapped(context_y, "group", z_size, z_size // 2)], z_size // 4
+    other_gate = swap_pool(w_gate[0])
+    up_matrix, down_matrix, contexts = lax.optimization_barrier((w_up[0], w_down[0], contexts))
+    other_up, other_down = swap_pool(up_matrix), swap_pool(down_matrix)
+    while bit:
+        contexts.append(swapped(jnp.concatenate(contexts, axis=0), "group", z_size, bit))
+        if bit > 1:
+            received, contexts = lax.optimization_barrier((received, contexts))
+        bit //= 2
+    place = jnp.stack([lax.axis_index("group"), y_index]).astype(jnp.int32)
 
     back_width = model_width * own_slots // ROWS
     back_parts = model_width // back_width
@@ -228,7 +250,7 @@
         back_width,
     ).reshape(experts, ROWS, back_width)
     returned = exchange(back, ("y", "x"))
-    returned, contexts[:6] = lax.optimization_barrier((returned, contexts[:6]))
+    returned, contexts = lax.optimization_barrier((returned, contexts))
 
     high = lax.reduce_precision(weights, 8, 7).astype(BF)
     low = (weights - high.astype(F32)).astype(BF)

time: 183 us -> 170 us (0.929)
  starting transfers between devices: 113 us -> 75.5 us
  waiting for transfers between devices: 21.8 us -> 46.6 us
    ppermute x14 -> x6, starting transfers between devices: 65.8 us -> 35.4 us  [swapped(): return lax.ppermute(value, axis, tuple(((s, s ^ bit) for s in range(size))))]
    all_to_all x3, waiting for transfers between devices: 0.01 us -> 13.8 us  [exchange(): return lax.all_to_all(value, axes, split_axis=0, concat_axis=0, tiled=True)]
    ppermute x14 -> x6, waiting for transfers between devices: 20.6 us -> 31.6 us  [swapped(): return lax.ppermute(value, axis, tuple(((s, s ^ bit) for s in range(size))))]
    all_to_all x3, starting transfers between devices: 38.6 us -> 31.9 us  [exchange(): return lax.all_to_all(value, axes, split_axis=0, concat_axis=0, tiled=True)]
  transfers between devices with their start and end apart: 21 -> 13, of which waited for: 9 -> 8; matrix products, arithmetic and copies ran while one was open for 0% -> 3% of each run, Pallas kernels for 0% -> 0%
where the time goes in v4:
time: 170 us
  starting transfers between devices  75.5 us (44%)
  waiting for transfers between devices  46.6 us (27%)
  blocking collectives  29.6 us (17%)
  Pallas kernels  9.7 us (6%)
  local copies, waits for them, and re-layouts  3.63 us (2%)
  other arithmetic  1.8 us (1%)
    ppermute x6, starting transfers between devices, swapped(): return lax.ppermute(value, axis, tuple(((s, s ^ bit) for s in range(size))))  35.4 us
    all_to_all x3, starting transfers between devices, exchange(): return lax.all_to_all(value, axes, split_axis=0, concat_axis=0, tiled=True)  31.9 us
    ppermute x6, waiting for transfers between devices, swapped(): return lax.ppermute(value, axis, tuple(((s, s ^ bit) for s in range(size))))  31.6 us
    all_to_all x2, blocking collectives, exchange(): return lax.all_to_all(value, axes, split_axis=0, concat_axis=0, tiled=True)  29.6 us
    all_to_all x3, waiting for transfers between devices, exchange(): return lax.all_to_all(value, axes, split_axis=0, concat_axis=0, tiled=True)  13.8 us
    ppermute x4, starting transfers between devices, swap_pool(): return lax.ppermute(value, 'pool', ((0, 1), (1, 0)))  8.16 us
    pallas_call x1, Pallas kernels, expert_rows(): pl.pallas_call(expert_kernel, out_shape=jax.ShapeDtypeStruct((slots * wid...  8.1 us
  transfers between devices with their start and end apart: 13, of which 8 were waited for; matrix products, arithmetic and copies ran while one was open for 3% of the time, Pallas kernels for 0%

profile of v4, /device:TPU:2, one launch (start us, length us, event | category | flops | bytes accessed | tf_op | source)
XLA Modules:
  0.0 169.5 jit_solution(8573065005246655326)
XLA Ops:
  0.6 0.0 copy-start.3
  0.6 0.0 copy-start.1
  0.7 0.0 copy-start.2
  0.7 0.9 dynamic-slice_bitcast_fusion
  1.6 3.6 %collective-permute-start = (bf16[4,64,128]{2,1,0:T(8,128)(2,1)S(1)}, bf16[4,64,128]{2,1,0:T(8,128)(2,1)S(1)}, u32[]{:S(2)}, u32[]{:S(2)}) collective-permute-start(bf16[4,64,128]{2,1,0:T(8,128)(2,1)S(1)} %pad_maximum_fusion.2), channel_id=1, source_target_pairs={{0,8},{8,0},{16,24},{24,16},{32,40},{40,32},{48,56},{56,48},{1,9},... | collective-permute-start | bytes 196616 | tf_op jit(solution)/shard_map/ppermute | solution.py:170
  5.2 0.8 copy.23
  6.0 0.1 eq.52
  6.1 0.1 fusion.13
  6.2 0.2 reduce_window_sum.11
  6.3 0.2 select_reduce_fusion.1
  6.5 0.1 reduce_sum.39
  6.6 0.1 fusion.12
  6.7 0.1 copy.25
  6.9 0.3 broadcast_multiply_fusion
  7.2 0.3 mul.89
  7.4 0.0 copy-done.3
  7.5 0.1 copy.26
  7.5 0.0 copy-done.1
  7.5 0.0 copy-done.2
  7.5 1.4 fusion
  9.0 0.0 copy-start
  9.0 0.1 select_reduce_fusion
  9.1 0.0 collective-permute-done
  9.1 4.9 %collective-permute-start.1 = (bf16[4,64,128]{2,1,0:T(8,128)(2,1)S(1)}, bf16[4,64,128]{2,1,0:T(8,128)(2,1)S(1)}, u32[]{:S(2)}, u32[]{:S(2)}) collective-permute-start(bf16[4,64,128]{2,1,0:T(8,128)(2,1)S(1)} %pad_maximum_fusion.3), channel_id=1, source_target_pairs={{0,16},{8,24},{16,0},{24,8},{32,48},{40,56},{48,32},{56,40},{1,17}... | collective-permute-start | bytes 196616 | tf_op jit(solution)/shard_map/ppermute | solution.py:170
  14.0 3.0 %collective-permute-done.1 = bf16[4,64,128]{2,1,0:T(8,128)(2,1)S(1)} collective-permute-done((bf16[4,64,128]{2,1,0:T(8,128)(2,1)S(1)}, bf16[4,64,128]{2,1,0:T(8,128)(2,1)S(1)}, u32[]{:S(2)}, u32[]{:S(2)}) %collective-permute-start.1) | collective-permute-done | bytes 65568 | tf_op jit(solution)/shard_map/ppermute | solution.py:170
  17.0 6.7 %collective-permute-start.2 = (bf16[4,64,128]{2,1,0:T(8,128)(2,1)S(1)}, bf16[4,64,128]{2,1,0:T(8,128)(2,1)S(1)}, u32[]{:S(2)}, u32[]{:S(2)}) collective-permute-start(bf16[4,64,128]{2,1,0:T(8,128)(2,1)S(1)} %pad_maximum_fusion.4), channel_id=1, source_target_pairs={{0,32},{8,40},{16,48},{24,56},{32,0},{40,8},{48,16},{56,24},{1,33}... | collective-permute-start | bytes 196616 | tf_op jit(solution)/shard_map/ppermute | solution.py:170
  23.7 4.1 %collective-permute-done.2 = bf16[4,64,128]{2,1,0:T(8,128)(2,1)S(1)} collective-permute-done((bf16[4,64,128]{2,1,0:T(8,128)(2,1)S(1)}, bf16[4,64,128]{2,1,0:T(8,128)(2,1)S(1)}, u32[]{:S(2)}, u32[]{:S(2)}) %collective-permute-start.2) | collective-permute-done | bytes 65568 | tf_op jit(solution)/shard_map/ppermute | solution.py:170
  27.8 14.7 %all-to-all-start = ((bf16[64,8,1024]{2,1,0:T(8,128)(2,1)}), bf16[64,8,1024]{2,1,0:T(8,128)(2,1)S(1)}, u32[]{:S(2)}, u32[]{:S(2)}) async-start(bf16[64,8,1024]{2,1,0:T(8,128)(2,1)} %fusion), calls=%async_computation | async-start | bytes 2097152 | tf_op jit(solution)/shard_map/all_to_all | solution.py:166
  42.5 11.5 %collective-permute-start.3 = (bf16[1,512,128]{2,1,0:T(8,128)(2,1)S(1)}, bf16[1,512,128]{2,1,0:T(8,128)(2,1)S(1)}, u32[]{:S(2)}, u32[]{:S(2)}) collective-permute-start(bf16[1,512,128]{2,1,0:T(8,128)(2,1)S(1)} %bitcast.71), channel_id=1, source_target_pairs={{0,256},{64,320},{128,384},{192,448},{256,0},{320,64},{384,128},{4... | collective-permute-start | bytes 393224 | tf_op jit(solution)/shard_map/ppermute | solution.py:170
  54.0 0.0 copy-done
  54.0 1.9 %collective-permute-start.5 = (bf16[2048,384]{1,0:T(8,128)(2,1)S(1)}, bf16[2048,384]{1,0:T(8,128)(2,1)}, u32[]{:S(2)}, u32[]{:S(2)}) collective-permute-start(bf16[2048,384]{1,0:T(8,128)(2,1)S(1)} %bitcast.69), channel_id=1, source_target_pairs={{0,512},{512,0},{1,513},{513,1},{2,514},{514,2},{3,515},{515,3},{4... | collective-permute-start | bytes 4718600 | tf_op jit(solution)/shard_map/ppermute | solution.py:162
  55.9 1.0 collective-permute-done.3.refs_1_
  56.9 1.9 %collective-permute-start.6 = (bf16[2048,384]{1,0:T(8,128)(2,1)}, bf16[2048,384]{1,0:T(8,128)(2,1)}, u32[]{:S(2)}, u32[]{:S(2)}) collective-permute-start(bf16[2048,384]{1,0:T(8,128)(2,1)} %bitcast.75), channel_id=1, source_target_pairs={{0,512},{512,0},{1,513},{513,1},{2,514},{514,2},{3,515},{515,3},{4... | collective-permute-start | bytes 4718600 | tf_op jit(solution)/shard_map/ppermute | solution.py:162
  58.8 2.4 %collective-permute-start.7 = (bf16[384,2048]{1,0:T(8,128)(2,1)}, bf16[384,2048]{1,0:T(8,128)(2,1)}, u32[]{:S(2)}, u32[]{:S(2)}) collective-permute-start(bf16[384,2048]{1,0:T(8,128)(2,1)} %bitcast.77), channel_id=1, source_target_pairs={{0,512},{512,0},{1,513},{513,1},{2,514},{514,2},{3,515},{515,3},{4... | collective-permute-start | bytes 4718600 | tf_op jit(solution)/shard_map/ppermute | solution.py:162
  61.3 6.2 %collective-permute-start.4 = (bf16[2,512,128]{2,1,0:T(8,128)(2,1)S(1)}, bf16[2,512,128]{2,1,0:T(8,128)(2,1)S(1)}, u32[]{:S(2)}, u32[]{:S(2)}) collective-permute-start(bf16[2,512,128]{2,1,0:T(8,128)(2,1)S(1)} %pad_maximum_fusion.1), channel_id=1, source_target_pairs={{0,128},{64,192},{128,0},{192,64},{256,384},{320,448},{384,256},{4... | collective-permute-start | bytes 786440 | tf_op jit(solution)/shard_map/ppermute | solution.py:170
  67.5 12.1 %collective-permute-done.4.refs_2_ = bf16[2,512,128]{2,1,0:T(8,128)(2,1)S(1)} collective-permute-done((bf16[2,512,128]{2,1,0:T(8,128)(2,1)S(1)}, bf16[2,512,128]{2,1,0:T(8,128)(2,1)S(1)}, u32[]{:S(2)}, u32[]{:S(2)}) %collective-permute-start.4) | collective-permute-done | bytes 262176 | tf_op jit(solution)/shard_map/ppermute | solution.py:170
  79.6 0.0 all-to-all-done
  79.6 0.0 collective-permute-done.5.refs_3_
  79.6 0.0 collective-permute-done.6.refs_4_
  79.6 0.0 collective-permute-done.7.refs_5_
  79.6 8.1 %expert.1 = bf16[512,512]{1,0:T(8,128)(2,1)} custom-call(bf16[512,1024]{1,0:T(8,128)(2,1)S(1)} %bitcast.68, bf16[2048,384]{1,0:T(8,128)(2,1)S(1)} %bitcast.70, bf16[2048,384]{1,0:T(8,128)(2,1)} %bitcast.76, bf16[384,2048]{1,0:T(8,128)(2,1)} %bitcast.78, bf16[2048,384]{1,0:T(8,128)(2,1)} %collective-permute-done.5.refs_3_, ...), custom_call_target="tpu_custom_call" | custom-call | flops 2013265920 | bytes 9437184 | tf_op jit(solution)/shard_map/expert/pallas_call | solution.py:82
  87.7 12.7 %all-to-all-start.1 = ((bf16[64,8,512]{2,1,0:T(8,128)(2,1)}), bf16[64,8,512]{2,1,0:T(8,128)(2,1)S(1)}, u32[]{:S(2)}, u32[]{:S(2)}) async-start(bf16[64,8,512]{2,1,0:T(8,128)(2,1)} %bitcast.24), calls=%async_computation.1 | async-start | bytes 1048576 | tf_op jit(solution)/shard_map/all_to_all | solution.py:166
  100.4 0.1 pad_maximum_fusion
  100.5 2.6 %collective-permute-start.8 = (bf16[4,512,128]{2,1,0:T(8,128)(2,1)S(1)}, bf16[4,512,128]{2,1,0:T(8,128)(2,1)S(1)}, u32[]{:S(2)}, u32[]{:S(2)}) collective-permute-start(bf16[4,512,128]{2,1,0:T(8,128)(2,1)S(1)} %pad_maximum_fusion), channel_id=1, source_target_pairs={{0,64},{64,0},{128,192},{192,128},{256,320},{320,256},{384,448},{4... | collective-permute-start | bytes 1572872 | tf_op jit(solution)/shard_map/ppermute | solution.py:170
  103.2 0.2 mul.102
  103.4 0.1 copy.27
  103.5 0.1 mul.98
  103.6 0.1 copy.28
  103.7 11.5 %collective-permute-done.8.refs_3_ = bf16[4,512,128]{2,1,0:T(8,128)(2,1)S(1)} collective-permute-done((bf16[4,512,128]{2,1,0:T(8,128)(2,1)S(1)}, bf16[4,512,128]{2,1,0:T(8,128)(2,1)S(1)}, u32[]{:S(2)}, u32[]{:S(2)}) %collective-permute-start.8) | collective-permute-done | bytes 524320 | tf_op jit(solution)/shard_map/ppermute | solution.py:170
  115.2 4.5 %all-to-all-done.1 = bf16[64,8,512]{2,1,0:T(8,128)(2,1)S(1)} async-done(((bf16[64,8,512]{2,1,0:T(8,128)(2,1)}), bf16[64,8,512]{2,1,0:T(8,128)(2,1)S(1)}, u32[]{:S(2)}, u32[]{:S(2)}) %all-to-all-start.1) | async-done | bytes 524320 | tf_op jit(solution)/shard_map/all_to_all | solution.py:166
  119.6 0.2 convolution_reduce_fusion
  119.9 1.9 %collective-permute-start.9 = (f32[2,16,512]{2,1,0:T(8,128)S(1)}, f32[2,16,512]{2,1,0:T(8,128)S(1)}, u32[]{:S(2)}, u32[]{:S(2)}) collective-permute-start(f32[2,16,512]{2,1,0:T(8,128)S(1)} %get-tuple-element.38), channel_id=1, source_target_pairs={{0,512},{512,0},{1,513},{513,1},{2,514},{514,2},{3,515},{515,3},{4... | collective-permute-start | bytes 196616 | tf_op jit(solution)/shard_map/ppermute | solution.py:162
  121.8 1.2 collective-permute-done.9.came_ref
  123.0 0.6 finish.1
  123.7 15.5 %all_to_all.25 = bf16[8,16,128]{2,1,0:T(8,128)(2,1)S(1)} all-to-all(bf16[8,16,128]{2,1,0:T(8,128)(2,1)S(1)} %get-tuple-element.37), channel_id=1, replica_groups=mesh['pool'=2,'group'=8,'y'=8,'x'=8] {'group'}, dimensions={0} | all-to-all | bytes 65536 | tf_op jit(solution)/shard_map/all_to_all | solution.py:166
  139.2 0.7 broadcast_in_dim.36
  139.9 4.5 %all-to-all-start.3 = ((bf16[8,128,128]{2,1,0:T(8,128)(2,1)}), bf16[8,128,128]{2,1,0:T(8,128)(2,1)S(1)}, u32[]{:S(2)}, u32[]{:S(2)}) async-start(bf16[8,128,128]{2,1,0:T(8,128)(2,1)} %broadcast_in_dim.36), calls=%async_computation.3 | async-start | bytes 524288 | tf_op jit(solution)/shard_map/all_to_all | solution.py:166
  144.4 0.1 pad_add_fusion.place_ref
  144.5 9.3 %all-to-all-done.3.refs_4_ = bf16[8,128,128]{2,1,0:T(8,128)(2,1)S(1)} async-done(((bf16[8,128,128]{2,1,0:T(8,128)(2,1)}), bf16[8,128,128]{2,1,0:T(8,128)(2,1)S(1)}, u32[]{:S(2)}, u32[]{:S(2)}) %all-to-all-start.3) | async-done | bytes 262176 | tf_op jit(solution)/shard_map/all_to_all | solution.py:166
  153.8 1.0 context_product.1
  154.8 14.1 %all_to_all.26 = bf16[8,64,128]{2,1,0:T(8,128)(2,1)S(1)} all-to-all(bf16[8,64,128]{2,1,0:T(8,128)(2,1)S(1)} %context_product.1), channel_id=1, replica_groups=mesh['pool'=2,'group'=8,'y'=8,'x'=8] {'y'}, dimensions={0} | all-to-all | bytes 262144 | tf_op jit(solution)/shard_map/all_to_all | solution.py:166
  168.9 0.6 convert_reduce_fusion
  (21 shorter events, 0.3 us)
Async XLA Ops:
  0.6 6.8 %copy-start.3 = (f32[16,8]{0,1:T(8,128)S(1)}, f32[16,8]{0,1:T(8,128)}, u32[]{:S(2)}) copy-start(f32[16,8]{0,1:T(8,128)} %param.10) | copy-start | bytes 1540
  0.6 6.9 %copy-start.1 = (bf16[16,2048]{1,0:T(8,128)(2,1)S(1)}, bf16[16,2048]{1,0:T(8,128)(2,1)}, u32[]{:S(2)}) copy-start(bf16[16,2048]{1,0:T(8,128)(2,1)} %param.9) | copy-start | bytes 196612
  0.7 6.9 %copy-start.2 = (bf16[16,2048]{1,0:T(8,128)(2,1)S(1)}, bf16[16,2048]{1,0:T(8,128)(2,1)}, u32[]{:S(2)}) copy-start(bf16[16,2048]{1,0:T(8,128)(2,1)} %param.8) | copy-start | bytes 196612
  1.6 7.5 %collective-permute-start = (bf16[4,64,128]{2,1,0:T(8,128)(2,1)S(1)}, bf16[4,64,128]{2,1,0:T(8,128)(2,1)S(1)}, u32[]{:S(2)}, u32[]{:S(2)}) collective-permute-start(bf16[4,64,128]{2,1,0:T(8,128)(2,1)S(1)} %pad_maximum_fusion.2), channel_id=1, source_target_pairs={{0,8},{8,0},{16,24},{24,16},{32,40},{40,32},{48,56},{56,48},{1,9},... | collective-permute-start | bytes 196616 | tf_op jit(solution)/shard_map/ppermute | solution.py:170
  9.0 45.0 %copy-start = (bf16[1,2048,384]{2,1,0:T(8,128)(2,1)S(1)}, bf16[1,2048,384]{2,1,0:T(8,128)(2,1)}, u32[]{:S(2)}) copy-start(bf16[1,2048,384]{2,1,0:T(8,128)(2,1)} %param.12) | copy-start | bytes 4718596
  9.1 7.8 %collective-permute-start.1 = (bf16[4,64,128]{2,1,0:T(8,128)(2,1)S(1)}, bf16[4,64,128]{2,1,0:T(8,128)(2,1)S(1)}, u32[]{:S(2)}, u32[]{:S(2)}) collective-permute-start(bf16[4,64,128]{2,1,0:T(8,128)(2,1)S(1)} %pad_maximum_fusion.3), channel_id=1, source_target_pairs={{0,16},{8,24},{16,0},{24,8},{32,48},{40,56},{48,32},{56,40},{1,17}... | collective-permute-start | bytes 196616 | tf_op jit(solution)/shard_map/ppermute | solution.py:170
  17.0 10.8 %collective-permute-start.2 = (bf16[4,64,128]{2,1,0:T(8,128)(2,1)S(1)}, bf16[4,64,128]{2,1,0:T(8,128)(2,1)S(1)}, u32[]{:S(2)}, u32[]{:S(2)}) collective-permute-start(bf16[4,64,128]{2,1,0:T(8,128)(2,1)S(1)} %pad_maximum_fusion.4), channel_id=1, source_target_pairs={{0,32},{8,40},{16,48},{24,56},{32,0},{40,8},{48,16},{56,24},{1,33}... | collective-permute-start | bytes 196616 | tf_op jit(solution)/shard_map/ppermute | solution.py:170
  27.8 51.8 %all-to-all-start = ((bf16[64,8,1024]{2,1,0:T(8,128)(2,1)}), bf16[64,8,1024]{2,1,0:T(8,128)(2,1)S(1)}, u32[]{:S(2)}, u32[]{:S(2)}) async-start(bf16[64,8,1024]{2,1,0:T(8,128)(2,1)} %fusion), calls=%async_computation | async-start | bytes 2097152 | tf_op jit(solution)/shard_map/all_to_all | solution.py:166
  42.5 14.4 %collective-permute-start.3 = (bf16[1,512,128]{2,1,0:T(8,128)(2,1)S(1)}, bf16[1,512,128]{2,1,0:T(8,128)(2,1)S(1)}, u32[]{:S(2)}, u32[]{:S(2)}) collective-permute-start(bf16[1,512,128]{2,1,0:T(8,128)(2,1)S(1)} %bitcast.71), channel_id=1, source_target_pairs={{0,256},{64,320},{128,384},{192,448},{256,0},{320,64},{384,128},{4... | collective-permute-start | bytes 393224 | tf_op jit(solution)/shard_map/ppermute | solution.py:170
  54.0 25.6 %collective-permute-start.5 = (bf16[2048,384]{1,0:T(8,128)(2,1)S(1)}, bf16[2048,384]{1,0:T(8,128)(2,1)}, u32[]{:S(2)}, u32[]{:S(2)}) collective-permute-start(bf16[2048,384]{1,0:T(8,128)(2,1)S(1)} %bitcast.69), channel_id=1, source_target_pairs={{0,512},{512,0},{1,513},{513,1},{2,514},{514,2},{3,515},{515,3},{4... | collective-permute-start | bytes 4718600 | tf_op jit(solution)/shard_map/ppermute | solution.py:162
  56.9 22.7 %collective-permute-start.6 = (bf16[2048,384]{1,0:T(8,128)(2,1)}, bf16[2048,384]{1,0:T(8,128)(2,1)}, u32[]{:S(2)}, u32[]{:S(2)}) collective-permute-start(bf16[2048,384]{1,0:T(8,128)(2,1)} %bitcast.75), channel_id=1, source_target_pairs={{0,512},{512,0},{1,513},{513,1},{2,514},{514,2},{3,515},{515,3},{4... | collective-permute-start | bytes 4718600 | tf_op jit(solution)/shard_map/ppermute | solution.py:162
  58.8 20.8 %collective-permute-start.7 = (bf16[384,2048]{1,0:T(8,128)(2,1)}, bf16[384,2048]{1,0:T(8,128)(2,1)}, u32[]{:S(2)}, u32[]{:S(2)}) collective-permute-start(bf16[384,2048]{1,0:T(8,128)(2,1)} %bitcast.77), channel_id=1, source_target_pairs={{0,512},{512,0},{1,513},{513,1},{2,514},{514,2},{3,515},{515,3},{4... | collective-permute-start | bytes 4718600 | tf_op jit(solution)/shard_map/ppermute | solution.py:162
  61.3 18.3 %collective-permute-start.4 = (bf16[2,512,128]{2,1,0:T(8,128)(2,1)S(1)}, bf16[2,512,128]{2,1,0:T(8,128)(2,1)S(1)}, u32[]{:S(2)}, u32[]{:S(2)}) collective-permute-start(bf16[2,512,128]{2,1,0:T(8,128)(2,1)S(1)} %pad_maximum_fusion.1), channel_id=1, source_target_pairs={{0,128},{64,192},{128,0},{192,64},{256,384},{320,448},{384,256},{4... | collective-permute-start | bytes 786440 | tf_op jit(solution)/shard_map/ppermute | solution.py:170
  87.7 31.9 %all-to-all-start.1 = ((bf16[64,8,512]{2,1,0:T(8,128)(2,1)}), bf16[64,8,512]{2,1,0:T(8,128)(2,1)S(1)}, u32[]{:S(2)}, u32[]{:S(2)}) async-start(bf16[64,8,512]{2,1,0:T(8,128)(2,1)} %bitcast.24), calls=%async_computation.1 | async-start | bytes 1048576 | tf_op jit(solution)/shard_map/all_to_all | solution.py:166
  100.5 14.7 %collective-permute-start.8 = (bf16[4,512,128]{2,1,0:T(8,128)(2,1)S(1)}, bf16[4,512,128]{2,1,0:T(8,128)(2,1)S(1)}, u32[]{:S(2)}, u32[]{:S(2)}) collective-permute-start(bf16[4,512,128]{2,1,0:T(8,128)(2,1)S(1)} %pad_maximum_fusion), channel_id=1, source_target_pairs={{0,64},{64,0},{128,192},{192,128},{256,320},{320,256},{384,448},{4... | collective-permute-start | bytes 1572872 | tf_op jit(solution)/shard_map/ppermute | solution.py:170
  119.9 3.1 %collective-permute-start.9 = (f32[2,16,512]{2,1,0:T(8,128)S(1)}, f32[2,16,512]{2,1,0:T(8,128)S(1)}, u32[]{:S(2)}, u32[]{:S(2)}) collective-permute-start(f32[2,16,512]{2,1,0:T(8,128)S(1)} %get-tuple-element.38), channel_id=1, source_target_pairs={{0,512},{512,0},{1,513},{513,1},{2,514},{514,2},{3,515},{515,3},{4... | collective-permute-start | bytes 196616 | tf_op jit(solution)/shard_map/ppermute | solution.py:162
  139.9 13.9 %all-to-all-start.3 = ((bf16[8,128,128]{2,1,0:T(8,128)(2,1)}), bf16[8,128,128]{2,1,0:T(8,128)(2,1)S(1)}, u32[]{:S(2)}, u32[]{:S(2)}) async-start(bf16[8,128,128]{2,1,0:T(8,128)(2,1)} %broadcast_in_dim.36), calls=%async_computation.3 | async-start | bytes 524288 | tf_op jit(solution)/shard_map/all_to_all | solution.py:166

commit v5 on v3

--- a/solution.py
+++ b/solution.py
@@ -7,6 +7,7 @@
 
 ROWS = 8
 SORT = 256
+Z_BLOCKS = 4
 BF = jnp.bfloat16
 F32 = jnp.float32
 
@@ -97,64 +98,71 @@
 
 def product_kernel(place_ref, *refs):
     contexts, tokens_ref, out_ref = refs[:-2], refs[-2], refs[-1]
-    x_size, depth, cols = tokens_ref.shape
-    z_size = len(contexts)
-    tok = depth // z_size
-    z_index, y_index, y_size = place_ref[0], place_ref[1], place_ref[2]
+    peers, depth, width = tokens_ref.shape
+    tok = depth // len(contexts)
     total = None
-    for step, ref in enumerate(contexts):
-        at = pl.multiple_of(lax.rem(z_index + z_size - step, z_size) * tok, tok)
-        tokens = tokens_ref[:, pl.ds(at, tok), :].reshape(x_size * tok, cols)
+    for i, ref in enumerate(contexts):
+        tokens = tokens_ref[:, i * tok:(i + 1) * tok, :].reshape(peers * tok, width)
         term = dot_f32(ref[...], tokens)
         total = term if total is None else total + term
-    heads = out_ref.shape[1]
-    for step in range(out_ref.shape[0]):
-        out_ref[lax.rem(y_index + y_size - step, y_size)] = total[step * heads:(step + 1) * heads].astype(BF)
-
-
-def context_product(place, contexts, tokens_b, y_size):
+    blocks, heads, cols = out_ref.shape
+    z_blocks = width // cols
+    y_blocks = blocks // z_blocks
+    yh_index = place_ref[0]
+    for z in range(z_blocks):
+        for apart in range(y_blocks):
+            out_ref[z * y_blocks + jnp.bitwise_xor(yh_index, apart)] = total[
+                apart * heads:(apart + 1) * heads, z * cols:(z + 1) * cols
+            ].astype(BF)
+
+
+def context_product(yh_index, contexts, tokens_b, y_blocks, z_blocks):
     rows, depth = contexts[0].shape
-    groups = len(contexts)
-    cols = tokens_b.shape[2]
+    width = tokens_b.shape[2]
     return pl.pallas_call(
         product_kernel,
-        out_shape=jax.ShapeDtypeStruct((y_size, rows // y_size, cols), BF),
-        in_specs=[pl.BlockSpec(memory_space=pltpu.SMEM)] + [pl.BlockSpec(memory_space=pltpu.VMEM)] * (groups + 1),
+        out_shape=jax.ShapeDtypeStruct((z_blocks * y_blocks, rows // y_blocks, width // z_blocks), BF),
+        in_specs=[pl.BlockSpec(memory_space=pltpu.SMEM)]
+        + [pl.BlockSpec(memory_space=pltpu.VMEM)] * (len(contexts) + 1),
         out_specs=pl.BlockSpec(memory_space=pltpu.VMEM),
         compiler_params=pltpu.CompilerParams(vmem_limit_bytes=16 * 2**20),
         cost_estimate=pl.CostEstimate(
-            flops=2 * groups * rows * depth * cols, bytes_accessed=2 * groups * rows * depth, transcendentals=0
+            flops=2 * len(contexts) * rows * depth * width,
+            bytes_accessed=2 * len(contexts) * depth * (rows + width),
+            transcendentals=0,
         ),
         name="context_product",
-    )(place, *contexts, tokens_b)
-
-
-def finish_kernel(mine_ref, came_ref, grad_ref, hidden_ref, columns_ref):
+    )(yh_index.astype(jnp.int32).reshape(1), *contexts, tokens_b)
+
+
+def finish_kernel(zl_ref, mine_ref, came_ref, grad_ref, hidden_ref, keep_ref, send_ref):
     parts, _, width = mine_ref.shape
-    cols = columns_ref.shape[2]
     for i in range(parts):
         at = slice(i * width, (i + 1) * width)
-        hidden = grad_ref[:, at].astype(F32) + (mine_ref[i] + came_ref[i])
-        hidden_ref[:, at] = hidden
-        for j in range(width // cols):
-            columns_ref[i * (width // cols) + j] = hidden[:, j * cols:(j + 1) * cols].astype(BF)
-
-
-def finish(mine, came, grad_half, groups):
+        hidden_ref[:, at] = grad_ref[:, at].astype(F32) + (mine_ref[i] + came_ref[i])
+    first = zl_ref[0] == 0
+    cols = hidden_ref.shape[1] // (2 * Z_BLOCKS)
+    for z in range(Z_BLOCKS):
+        even = hidden_ref[:, 2 * z * cols:(2 * z + 1) * cols]
+        odd = hidden_ref[:, (2 * z + 1) * cols:(2 * z + 2) * cols]
+        at = slice(z * cols, (z + 1) * cols)
+        keep_ref[:, at] = jnp.where(first, even, odd).astype(BF)
+        send_ref[:, at] = jnp.where(first, odd, even).astype(BF)
+
+
+def finish(zl_index, mine, came, grad_half):
     tok, width = grad_half.shape
     vmem = pl.BlockSpec(memory_space=pltpu.VMEM)
+    half = jax.ShapeDtypeStruct((tok, width // 2), BF)
     return pl.pallas_call(
         finish_kernel,
-        out_shape=(
-            jax.ShapeDtypeStruct((tok, width), F32),
-            jax.ShapeDtypeStruct((groups, tok, width // groups), BF),
-        ),
-        in_specs=[vmem] * 3,
-        out_specs=(vmem, vmem),
+        out_shape=(jax.ShapeDtypeStruct((tok, width), F32), half, half),
+        in_specs=[pl.BlockSpec(memory_space=pltpu.SMEM)] + [vmem] * 3,
+        out_specs=(vmem,) * 3,
         compiler_params=pltpu.CompilerParams(vmem_limit_bytes=8 * 2**20),
         cost_estimate=pl.CostEstimate(flops=3 * tok * width, bytes_accessed=16 * tok * width, transcendentals=0),
         name="finish",
-    )(mine, came, grad_half)
+    )(zl_index.astype(jnp.int32).reshape(1), mine, came, grad_half)
 
 
 def swap_pool(value):
@@ -165,28 +173,40 @@
     return lax.all_to_all(value, axes, split_axis=0, concat_axis=0, tiled=True)
 
 
-def shifted(value, axis, size, step):
-    return lax.ppermute(value, axis, tuple((s, (s + step) % size) for s in range(size)))
-
-
-def spread_over_y(context_t, y_index, y_size):
-    wide = context_t.shape[1] // y_size
-    pieces = []
-    for step in range(y_size):
-        piece = lax.dynamic_slice_in_dim(context_t, lax.rem(y_index + step, y_size) * wide, wide, 1)
-        pieces.append(shifted(piece, "y", y_size, step) if step else piece)
-    return jnp.concatenate(pieces, axis=0)
+def swapped(value, axis, size, bit):
+    return lax.ppermute(value, axis, tuple((s, s ^ bit) for s in range(size)))
+
+
+def spread_over_yh(context_t, yh_index, y_blocks, others):
+    wide = context_t.shape[1] // y_blocks
+    places = [
+        lax.dynamic_slice_in_dim(context_t, jnp.bitwise_xor(yh_index, r) * wide, wide, 1)
+        for r in range(y_blocks)
+    ]
+    bit = 1
+    while bit < y_blocks:
+        crossing = [r for r in range(y_blocks) if r & bit]
+        came = swapped(jnp.concatenate([places[r] for r in crossing], axis=0), "yh", y_blocks, bit)
+        if bit == 1:
+            came, others = lax.optimization_barrier((came, others))
+        heads = context_t.shape[0]
+        for i, r in enumerate(crossing):
+            places[r] = came[i * heads:(i + 1) * heads]
+        bit *= 2
+    return jnp.concatenate(places, axis=0), others
 
 
 def per_device(moe_in, out_grad, gates, routes, w_gate, w_up, w_down, context_t):
     tok_rows, model_width = moe_in.shape
     top_count = routes.shape[1]
-    y_size, x_size, z_size = lax.axis_size("y"), lax.axis_size("x"), lax.axis_size("group")
-    experts = y_size * x_size
+    plane = ("yh", "yl", "x")
+    experts = lax.axis_size(plane)
+    y_blocks, z_blocks = lax.axis_size("yh"), lax.axis_size("zh")
+    peers = experts // y_blocks
     capacity = 2 * tok_rows * top_count // experts
     own_slots = capacity // 2
     pool_index = lax.axis_index("pool")
-    y_index = lax.axis_index("y")
+    yh_index, zl_index = lax.axis_index("yh"), lax.axis_index("zl")
     half_width = model_width // 2
     pair_count = tok_rows * top_count
 
@@ -212,13 +232,12 @@
         experts * ROWS, parts * tok_rows
     )
     send = dot_f32(spread, stacked).astype(BF).reshape(experts, ROWS, piece_width)
-    send, context_t, weights = lax.optimization_barrier((send, context_t, weights))
-    received = exchange(send, ("y", "x"))
-    other_gate, other_up, other_down = swap_pool(w_gate[0]), swap_pool(w_up[0]), swap_pool(w_down[0])
-    context_y = spread_over_y(context_t, y_index, y_size)
+    send, weights, context_t = lax.optimization_barrier((send, weights, context_t))
+    received = exchange(send, plane)
+    other_gate = swap_pool(w_gate[0])
+    context_y, (up_matrix, down_matrix) = spread_over_yh(context_t, yh_index, y_blocks, (w_up[0], w_down[0]))
+    other_up, other_down = swap_pool(up_matrix), swap_pool(down_matrix)
     received, context_y = lax.optimization_barrier((received, context_y))
-    contexts = [shifted(context_y, "group", z_size, step) if step else context_y for step in range(z_size)]
-    place = jnp.stack([lax.axis_index("group"), y_index, jnp.int32(y_size)]).astype(jnp.int32)
 
     back_width = model_width * own_slots // ROWS
     back_parts = model_width // back_width
@@ -227,8 +246,9 @@
         (w_gate[0], w_up[0], w_down[0], other_gate, other_up, other_down),
         back_width,
     ).reshape(experts, ROWS, back_width)
-    returned = exchange(back, ("y", "x"))
-    returned, contexts[:6] = lax.optimization_barrier((returned, contexts[:6]))
+    returned = exchange(back, plane)
+    contexts = [context_y, swapped(context_y, "zl", 2, 1)]
+    returned, contexts = lax.optimization_barrier((returned, contexts))
 
     high = lax.reduce_precision(weights, 8, 7).astype(BF)
     low = (weights - high.astype(F32)).astype(BF)
@@ -243,27 +263,25 @@
     mine = lax.dynamic_slice_in_dim(mixed, pool_index * per_half, per_half, 0)
     theirs = lax.dynamic_slice_in_dim(mixed, (1 - pool_index) * per_half, per_half, 0)
     grad_half = lax.dynamic_slice_in_dim(out_grad, pool_index * half_width, half_width, 1)
-    hidden_grad, by_column = finish(mine, swap_pool(theirs), grad_half, z_size)
-
-    cols = half_width // z_size
-    by_group = exchange(by_column, "group")
-    gathered_b = exchange(
-        jnp.broadcast_to(by_group[None], (x_size, z_size, tok_rows, cols)).reshape(
-            x_size, z_size * tok_rows, cols
-        ),
-        "x",
-    )
-    partial_wo = context_product(place, contexts, gathered_b, y_size)
-    terms = exchange(partial_wo, "y")
+    hidden_grad, keep, give = finish(zl_index, mine, swap_pool(theirs), grad_half)
+    pair = jnp.concatenate((keep, swapped(give, "zl", 2, 1)), axis=0)
+    gathered_b = exchange(jnp.broadcast_to(pair[None], (peers, *pair.shape)), ("yl", "x"))
+    terms = exchange(
+        context_product(yh_index, contexts, gathered_b, y_blocks, z_blocks), ("zh", "yh")
+    )
     wo_grad = jnp.sum(terms.astype(F32), axis=0)
     return (hidden_grad, wo_grad)
 
 
 def solution(mesh):
     pool, group, ep = (mesh.shape[name] for name in ("pool", "group", "ep"))
-    y_size = 8
-    grid = Mesh(mesh.devices.reshape(pool, group, y_size, ep // y_size), ("pool", "group", "y", "x"))
-    tokens = ("group", "y", "x")
+    y_blocks, x_size = 4, 8
+    grid = Mesh(
+        mesh.devices.reshape(pool, Z_BLOCKS, group // Z_BLOCKS, y_blocks, ep // (y_blocks * x_size), x_size),
+        ("pool", "zh", "zl", "yh", "yl", "x"),
+    )
+    group, plane = ("zh", "zl"), ("yh", "yl", "x")
+    tokens = group + plane
     return jax.shard_map(
         per_device,
         mesh=grid,
@@ -272,11 +290,11 @@
             P(tokens, None),
             P(tokens, None),
             P(tokens, None),
-            P(("y", "x"), None, "pool"),
-            P(("y", "x"), None, "pool"),
-            P(("y", "x"), "pool", None),
-            P(("y", "x"), "group"),
+            P(plane, None, "pool"),
+            P(plane, None, "pool"),
+            P(plane, "pool", None),
+            P(plane, group),
         ),
-        out_specs=(P(tokens, "pool"), P(("y", "x"), ("pool", "group"))),
+        out_specs=(P(tokens, "pool"), P(plane, ("pool",) + group)),
         check_vma=False,
     )

time: 183 us -> 159 us (0.87)
  starting transfers between devices: 113 us -> 55.7 us
  waiting for transfers between devices: 21.8 us -> 39.7 us
  blocking collectives: 30.2 us -> 47.9 us
    ppermute x14 -> x4, starting transfers between devices: 65.8 us -> 20.5 us  [swapped(): return lax.ppermute(value, axis, tuple(((s, s ^ bit) for s in range(size))))]
    all_to_all x2, blocking collectives: 30.2 us -> 47.9 us  [exchange(): return lax.all_to_all(value, axes, split_axis=0, concat_axis=0, tiled=True)]
    all_to_all x3 -> x2, starting transfers between devices: 38.6 us -> 27 us  [exchange(): return lax.all_to_all(value, axes, split_axis=0, concat_axis=0, tiled=True)]
    all_to_all x3 -> x2, waiting for transfers between devices: 0.01 us -> 11.1 us  [exchange(): return lax.all_to_all(value, axes, split_axis=0, concat_axis=0, tiled=True)]
    ppermute x14 -> x4, waiting for transfers between devices: 20.6 us -> 27.4 us  [swapped(): return lax.ppermute(value, axis, tuple(((s, s ^ bit) for s in range(size))))]
  transfers between devices with their start and end apart: 21 -> 10, of which waited for: 9 -> 6; matrix products, arithmetic and copies ran while one was open for 0% -> 0% of each run, Pallas kernels for 0% -> 0%
where the time goes in v5:
time: 159 us
  starting transfers between devices  55.7 us (35%)
  blocking collectives  47.9 us (30%)
  waiting for transfers between devices  39.7 us (25%)
  Pallas kernels  9.07 us (6%)
  local copies, waits for them, and re-layouts  2.1 us (1%)
  other arithmetic  1.66 us (1%)
  matrix products  1.65 us (1%)
    all_to_all x2, blocking collectives, exchange(): return lax.all_to_all(value, axes, split_axis=0, concat_axis=0, tiled=True)  47.9 us
    ppermute x4, waiting for transfers between devices, swapped(): return lax.ppermute(value, axis, tuple(((s, s ^ bit) for s in range(size))))  27.4 us
    all_to_all x2, starting transfers between devices, exchange(): return lax.all_to_all(value, axes, split_axis=0, concat_axis=0, tiled=True)  27 us
    ppermute x4, starting transfers between devices, swapped(): return lax.ppermute(value, axis, tuple(((s, s ^ bit) for s in range(size))))  20.5 us
    all_to_all x2, waiting for transfers between devices, exchange(): return lax.all_to_all(value, axes, split_axis=0, concat_axis=0, tiled=True)  11.1 us
    ppermute x4, starting transfers between devices, swap_pool(): return lax.ppermute(value, 'pool', ((0, 1), (1, 0)))  8.16 us
    pallas_call x1, Pallas kernels, expert_rows(): pl.pallas_call(expert_kernel, out_shape=jax.ShapeDtypeStruct((slots * wid...  8.12 us
  transfers between devices with their start and end apart: 10, of which 6 were waited for; matrix products, arithmetic and copies ran while one was open for 0% of the time, Pallas kernels for 0%

profile of v5, /device:TPU:2, one launch (start us, length us, event | category | flops | bytes accessed | tf_op | source)
XLA Modules:
  0.0 158.8 jit_solution(9711412116141515062)
XLA Ops:
  0.6 0.0 copy-start.4
  0.6 0.0 copy-start.3
  0.6 0.0 copy-start.1
  0.7 0.8 copy.23
  1.5 0.1 eq.52
  1.6 0.1 fusion.13
  1.7 0.2 reduce_window_sum.11
  1.8 0.2 select_reduce_fusion.1
  2.0 0.1 reduce_sum.39
  2.1 0.1 fusion.12
  2.2 0.1 copy.25
  2.4 0.3 broadcast_multiply_fusion
  2.6 0.3 mul.77
  2.9 0.0 copy-done.4
  2.9 0.1 copy.26
  3.0 0.1 select_reduce_fusion
  3.1 0.0 copy-done.3
  3.1 0.0 copy-done.1
  3.2 0.0 copy-start.2
  3.2 1.4 fusion
  4.6 0.0 copy-start
  4.6 17.4 %all-to-all-start = ((bf16[64,8,1024]{2,1,0:T(8,128)(2,1)}), bf16[64,8,1024]{2,1,0:T(8,128)(2,1)S(1)}, u32[]{:S(2)}, u32[]{:S(2)}) async-start(bf16[64,8,1024]{2,1,0:T(8,128)(2,1)} %fusion), calls=%async_computation | async-start | bytes 2097152 | tf_op jit(solution)/shard_map/all_to_all | solution.py:173
  22.1 0.0 copy-done.2
  22.1 4.4 %collective-permute-start = (bf16[128,256]{1,0:T(8,128)(2,1)S(1)}, bf16[128,256]{1,0:T(8,128)(2,1)S(1)}, u32[]{:S(2)}, u32[]{:S(2)}) collective-permute-start(bf16[128,256]{1,0:T(8,128)(2,1)S(1)} %pad_maximum_fusion.1), channel_id=1, source_target_pairs={{0,16},{16,0},{32,48},{48,32},{1,17},{17,1},{33,49},{49,33},{2,18}... | collective-permute-start | bytes 196616 | tf_op jit(solution)/shard_map/ppermute | solution.py:177
  26.5 0.0 copy-done
  26.5 1.9 %collective-permute-start.2 = (bf16[2048,384]{1,0:T(8,128)(2,1)S(1)}, bf16[2048,384]{1,0:T(8,128)(2,1)}, u32[]{:S(2)}, u32[]{:S(2)}) collective-permute-start(bf16[2048,384]{1,0:T(8,128)(2,1)S(1)} %bitcast.25), channel_id=1, source_target_pairs={{0,512},{512,0},{1,513},{513,1},{2,514},{514,2},{3,515},{515,3},{4... | collective-permute-start | bytes 4718600 | tf_op jit(solution)/shard_map/ppermute | solution.py:169
  28.4 17.9 %collective-permute-done = bf16[128,256]{1,0:T(8,128)(2,1)S(1)} collective-permute-done((bf16[128,256]{1,0:T(8,128)(2,1)S(1)}, bf16[128,256]{1,0:T(8,128)(2,1)S(1)}, u32[]{:S(2)}, u32[]{:S(2)}) %collective-permute-start) | collective-permute-done | bytes 65568 | tf_op jit(solution)/shard_map/ppermute | solution.py:177
  46.3 1.9 %collective-permute-start.3 = (bf16[2048,384]{1,0:T(8,128)(2,1)}, bf16[2048,384]{1,0:T(8,128)(2,1)}, u32[]{:S(2)}, u32[]{:S(2)}) collective-permute-start(bf16[2048,384]{1,0:T(8,128)(2,1)} %bitcast.27), channel_id=1, source_target_pairs={{0,512},{512,0},{1,513},{513,1},{2,514},{514,2},{3,515},{515,3},{4... | collective-permute-start | bytes 4718600 | tf_op jit(solution)/shard_map/ppermute | solution.py:169
  48.2 2.4 %collective-permute-start.4 = (bf16[384,2048]{1,0:T(8,128)(2,1)}, bf16[384,2048]{1,0:T(8,128)(2,1)}, u32[]{:S(2)}, u32[]{:S(2)}) collective-permute-start(bf16[384,2048]{1,0:T(8,128)(2,1)} %bitcast.29), channel_id=1, source_target_pairs={{0,512},{512,0},{1,513},{513,1},{2,514},{514,2},{3,515},{515,3},{4... | collective-permute-start | bytes 4718600 | tf_op jit(solution)/shard_map/ppermute | solution.py:169
  50.7 5.7 %collective-permute-start.1 = (bf16[128,256]{1,0:T(8,128)(2,1)S(1)}, bf16[128,256]{1,0:T(8,128)(2,1)S(1)}, u32[]{:S(2)}, u32[]{:S(2)}) collective-permute-start(bf16[128,256]{1,0:T(8,128)(2,1)S(1)} %pad_maximum_fusion.2), channel_id=1, source_target_pairs={{0,32},{16,48},{32,0},{48,16},{1,33},{17,49},{33,1},{49,17},{2,34}... | collective-permute-start | bytes 196616 | tf_op jit(solution)/shard_map/ppermute | solution.py:177
  56.4 5.5 %collective-permute-done.1 = bf16[128,256]{1,0:T(8,128)(2,1)S(1)} collective-permute-done((bf16[128,256]{1,0:T(8,128)(2,1)S(1)}, bf16[128,256]{1,0:T(8,128)(2,1)S(1)}, u32[]{:S(2)}, u32[]{:S(2)}) %collective-permute-start.1) | collective-permute-done | bytes 65568 | tf_op jit(solution)/shard_map/ppermute | solution.py:177
  61.9 0.0 all-to-all-done
  61.9 0.0 collective-permute-done.2.refs_3_
  61.9 0.0 collective-permute-done.3.refs_4_
  61.9 0.0 collective-permute-done.4.refs_5_
  62.0 8.1 %expert.1 = bf16[512,512]{1,0:T(8,128)(2,1)} custom-call(bf16[512,1024]{1,0:T(8,128)(2,1)S(1)} %bitcast.24, bf16[2048,384]{1,0:T(8,128)(2,1)S(1)} %bitcast.26, bf16[2048,384]{1,0:T(8,128)(2,1)} %bitcast.28, bf16[384,2048]{1,0:T(8,128)(2,1)} %bitcast.30, bf16[2048,384]{1,0:T(8,128)(2,1)} %collective-permute-done.2.refs_3_, ...), custom_call_target="tpu_custom_call" | custom-call | flops 2013265920 | bytes 9437184 | tf_op jit(solution)/shard_map/expert/pallas_call | solution.py:83
  70.1 9.6 %all-to-all-start.1 = ((bf16[64,8,512]{2,1,0:T(8,128)(2,1)}), bf16[64,8,512]{2,1,0:T(8,128)(2,1)S(1)}, u32[]{:S(2)}, u32[]{:S(2)}) async-start(bf16[64,8,512]{2,1,0:T(8,128)(2,1)} %bitcast.10), calls=%async_computation.1 | async-start | bytes 1048576 | tf_op jit(solution)/shard_map/all_to_all | solution.py:173
  79.7 5.2 %collective-permute-start.5 = (bf16[256,256]{1,0:T(8,128)(2,1)S(1)}, bf16[256,256]{1,0:T(8,128)(2,1)S(1)}, u32[]{:S(2)}, u32[]{:S(2)}) collective-permute-start(bf16[256,256]{1,0:T(8,128)(2,1)S(1)} %pad_maximum_fusion.refs_0_), channel_id=1, source_target_pairs={{0,64},{64,0},{1,65},{65,1},{2,66},{66,2},{3,67},{67,3},{4,68},{68... | collective-permute-start | bytes 393224 | tf_op jit(solution)/shard_map/ppermute | solution.py:177
  84.9 0.1 copy.27
  85.0 0.1 mul.78
  85.1 0.1 copy.28
  85.3 0.2 mul.82
  85.5 2.4 %collective-permute-done.5.refs_1_ = bf16[256,256]{1,0:T(8,128)(2,1)S(1)} collective-permute-done((bf16[256,256]{1,0:T(8,128)(2,1)S(1)}, bf16[256,256]{1,0:T(8,128)(2,1)S(1)}, u32[]{:S(2)}, u32[]{:S(2)}) %collective-permute-start.5) | collective-permute-done | bytes 131104 | tf_op jit(solution)/shard_map/ppermute | solution.py:177
  87.8 11.1 %all-to-all-done.1 = bf16[64,8,512]{2,1,0:T(8,128)(2,1)S(1)} async-done(((bf16[64,8,512]{2,1,0:T(8,128)(2,1)}), bf16[64,8,512]{2,1,0:T(8,128)(2,1)S(1)}, u32[]{:S(2)}, u32[]{:S(2)}) %all-to-all-start.1) | async-done | bytes 524320 | tf_op jit(solution)/shard_map/all_to_all | solution.py:173
  98.9 0.2 convolution_reduce_fusion
  99.1 1.9 %collective-permute-start.6 = (f32[2,16,512]{2,1,0:T(8,128)S(1)}, f32[2,16,512]{2,1,0:T(8,128)S(1)}, u32[]{:S(2)}, u32[]{:S(2)}) collective-permute-start(f32[2,16,512]{2,1,0:T(8,128)S(1)} %get-tuple-element.30), channel_id=1, source_target_pairs={{0,512},{512,0},{1,513},{513,1},{2,514},{514,2},{3,515},{515,3},{4... | collective-permute-start | bytes 196616 | tf_op jit(solution)/shard_map/ppermute | solution.py:169
  101.1 1.2 collective-permute-done.6.came_ref
  102.3 0.6 finish.1
  102.9 5.2 %collective-permute-start.7 = (bf16[16,512]{1,0:T(8,128)(2,1)S(1)}, bf16[16,512]{1,0:T(8,128)(2,1)S(1)}, u32[]{:S(2)}, u32[]{:S(2)}) collective-permute-start(bf16[16,512]{1,0:T(8,128)(2,1)S(1)} %get-tuple-element.29), channel_id=1, source_target_pairs={{0,64},{64,0},{1,65},{65,1},{2,66},{66,2},{3,67},{67,3},{4,68},{68... | collective-permute-start | bytes 49160 | tf_op jit(solution)/shard_map/ppermute | solution.py:177
  108.1 1.7 %collective-permute-done.7 = bf16[16,512]{1,0:T(8,128)(2,1)S(1)} collective-permute-done((bf16[16,512]{1,0:T(8,128)(2,1)S(1)}, bf16[16,512]{1,0:T(8,128)(2,1)S(1)}, u32[]{:S(2)}, u32[]{:S(2)}) %collective-permute-start.7) | collective-permute-done | bytes 16416 | tf_op jit(solution)/shard_map/ppermute | solution.py:177
  109.9 18.8 %all_to_all.20.refs_2_ = bf16[16,32,512]{2,1,0:T(8,128)(2,1)S(1)} all-to-all(bf16[16,32,512]{2,1,0:T(8,128)(2,1)S(1)} %broadcast_in_dim.18), channel_id=1, replica_groups=mesh['pool'=2,'zh'=4,'zl'=2,'yh'=4,'yl'=2,'x'=8] {'yl','x'}, dimensions={0} | all-to-all | bytes 1048576 | tf_op jit(solution)/shard_map/all_to_all | solution.py:173
  128.7 0.3 context_product.1
  129.0 29.1 %all_to_all.21 = bf16[16,64,128]{2,1,0:T(8,128)(2,1)S(1)} all-to-all(bf16[16,64,128]{2,1,0:T(8,128)(2,1)S(1)} %context_product.1), channel_id=1, replica_groups=mesh['pool'=2,'zh'=4,'zl'=2,'yh'=4,'yl'=2,'x'=8] {'zh','yh'}, dimensions={0} | all-to-all | bytes 524288 | tf_op jit(solution)/shard_map/all_to_all | solution.py:173
  158.1 0.7 convert_reduce_fusion
  (15 shorter events, 0.2 us)
Async XLA Ops:
  0.6 2.3 %copy-start.4 = (f32[16,8]{0,1:T(8,128)S(1)}, f32[16,8]{0,1:T(8,128)}, u32[]{:S(2)}) copy-start(f32[16,8]{0,1:T(8,128)} %param.10) | copy-start | bytes 1540
  0.6 2.5 %copy-start.3 = (bf16[16,2048]{1,0:T(8,128)(2,1)S(1)}, bf16[16,2048]{1,0:T(8,128)(2,1)}, u32[]{:S(2)}) copy-start(bf16[16,2048]{1,0:T(8,128)(2,1)} %param.8) | copy-start | bytes 196612
  0.6 2.5 %copy-start.1 = (bf16[16,2048]{1,0:T(8,128)(2,1)S(1)}, bf16[16,2048]{1,0:T(8,128)(2,1)}, u32[]{:S(2)}) copy-start(bf16[16,2048]{1,0:T(8,128)(2,1)} %param.9) | copy-start | bytes 196612
  3.2 18.9 %copy-start.2 = (bf16[64,1024]{1,0:T(8,128)(2,1)S(1)}, bf16[64,1024]{1,0:T(8,128)(2,1)}, u32[]{:S(2)}) copy-start(bf16[64,1024]{1,0:T(8,128)(2,1)} %param.15) | copy-start | bytes 393220
  4.6 21.9 %copy-start = (bf16[1,2048,384]{2,1,0:T(8,128)(2,1)S(1)}, bf16[1,2048,384]{2,1,0:T(8,128)(2,1)}, u32[]{:S(2)}) copy-start(bf16[1,2048,384]{2,1,0:T(8,128)(2,1)} %param.12) | copy-start | bytes 4718596
  4.6 57.3 %all-to-all-start = ((bf16[64,8,1024]{2,1,0:T(8,128)(2,1)}), bf16[64,8,1024]{2,1,0:T(8,128)(2,1)S(1)}, u32[]{:S(2)}, u32[]{:S(2)}) async-start(bf16[64,8,1024]{2,1,0:T(8,128)(2,1)} %fusion), calls=%async_computation | async-start | bytes 2097152 | tf_op jit(solution)/shard_map/all_to_all | solution.py:173
  22.1 24.2 %collective-permute-start = (bf16[128,256]{1,0:T(8,128)(2,1)S(1)}, bf16[128,256]{1,0:T(8,128)(2,1)S(1)}, u32[]{:S(2)}, u32[]{:S(2)}) collective-permute-start(bf16[128,256]{1,0:T(8,128)(2,1)S(1)} %pad_maximum_fusion.1), channel_id=1, source_target_pairs={{0,16},{16,0},{32,48},{48,32},{1,17},{17,1},{33,49},{49,33},{2,18}... | collective-permute-start | bytes 196616 | tf_op jit(solution)/shard_map/ppermute | solution.py:177
  26.5 35.4 %collective-permute-start.2 = (bf16[2048,384]{1,0:T(8,128)(2,1)S(1)}, bf16[2048,384]{1,0:T(8,128)(2,1)}, u32[]{:S(2)}, u32[]{:S(2)}) collective-permute-start(bf16[2048,384]{1,0:T(8,128)(2,1)S(1)} %bitcast.25), channel_id=1, source_target_pairs={{0,512},{512,0},{1,513},{513,1},{2,514},{514,2},{3,515},{515,3},{4... | collective-permute-start | bytes 4718600 | tf_op jit(solution)/shard_map/ppermute | solution.py:169
  46.3 15.6 %collective-permute-start.3 = (bf16[2048,384]{1,0:T(8,128)(2,1)}, bf16[2048,384]{1,0:T(8,128)(2,1)}, u32[]{:S(2)}, u32[]{:S(2)}) collective-permute-start(bf16[2048,384]{1,0:T(8,128)(2,1)} %bitcast.27), channel_id=1, source_target_pairs={{0,512},{512,0},{1,513},{513,1},{2,514},{514,2},{3,515},{515,3},{4... | collective-permute-start | bytes 4718600 | tf_op jit(solution)/shard_map/ppermute | solution.py:169
  48.2 13.7 %collective-permute-start.4 = (bf16[384,2048]{1,0:T(8,128)(2,1)}, bf16[384,2048]{1,0:T(8,128)(2,1)}, u32[]{:S(2)}, u32[]{:S(2)}) collective-permute-start(bf16[384,2048]{1,0:T(8,128)(2,1)} %bitcast.29), channel_id=1, source_target_pairs={{0,512},{512,0},{1,513},{513,1},{2,514},{514,2},{3,515},{515,3},{4... | collective-permute-start | bytes 4718600 | tf_op jit(solution)/shard_map/ppermute | solution.py:169
  50.7 11.2 %collective-permute-start.1 = (bf16[128,256]{1,0:T(8,128)(2,1)S(1)}, bf16[128,256]{1,0:T(8,128)(2,1)S(1)}, u32[]{:S(2)}, u32[]{:S(2)}) collective-permute-start(bf16[128,256]{1,0:T(8,128)(2,1)S(1)} %pad_maximum_fusion.2), channel_id=1, source_target_pairs={{0,32},{16,48},{32,0},{48,16},{1,33},{17,49},{33,1},{49,17},{2,34}... | collective-permute-start | bytes 196616 | tf_op jit(solution)/shard_map/ppermute | solution.py:177
  70.1 28.8 %all-to-all-start.1 = ((bf16[64,8,512]{2,1,0:T(8,128)(2,1)}), bf16[64,8,512]{2,1,0:T(8,128)(2,1)S(1)}, u32[]{:S(2)}, u32[]{:S(2)}) async-start(bf16[64,8,512]{2,1,0:T(8,128)(2,1)} %bitcast.10), calls=%async_computation.1 | async-start | bytes 1048576 | tf_op jit(solution)/shard_map/all_to_all | solution.py:173
  79.7 8.1 %collective-permute-start.5 = (bf16[256,256]{1,0:T(8,128)(2,1)S(1)}, bf16[256,256]{1,0:T(8,128)(2,1)S(1)}, u32[]{:S(2)}, u32[]{:S(2)}) collective-permute-start(bf16[256,256]{1,0:T(8,128)(2,1)S(1)} %pad_maximum_fusion.refs_0_), channel_id=1, source_target_pairs={{0,64},{64,0},{1,65},{65,1},{2,66},{66,2},{3,67},{67,3},{4,68},{68... | collective-permute-start | bytes 393224 | tf_op jit(solution)/shard_map/ppermute | solution.py:177
  99.1 3.1 %collective-permute-start.6 = (f32[2,16,512]{2,1,0:T(8,128)S(1)}, f32[2,16,512]{2,1,0:T(8,128)S(1)}, u32[]{:S(2)}, u32[]{:S(2)}) collective-permute-start(f32[2,16,512]{2,1,0:T(8,128)S(1)} %get-tuple-element.30), channel_id=1, source_target_pairs={{0,512},{512,0},{1,513},{513,1},{2,514},{514,2},{3,515},{515,3},{4... | collective-permute-start | bytes 196616 | tf_op jit(solution)/shard_map/ppermute | solution.py:169
  102.9 6.9 %collective-permute-start.7 = (bf16[16,512]{1,0:T(8,128)(2,1)S(1)}, bf16[16,512]{1,0:T(8,128)(2,1)S(1)}, u32[]{:S(2)}, u32[]{:S(2)}) collective-permute-start(bf16[16,512]{1,0:T(8,128)(2,1)S(1)} %get-tuple-element.29), channel_id=1, source_target_pairs={{0,64},{64,0},{1,65},{65,1},{2,66},{66,2},{3,67},{67,3},{4,68},{68... | collective-permute-start | bytes 49160 | tf_op jit(solution)/shard_map/ppermute | solution.py:177

commit v6 on v5

--- a/solution.py
+++ b/solution.py
@@ -177,8 +177,8 @@
     return lax.ppermute(value, axis, tuple((s, s ^ bit) for s in range(size)))
 
 
-def spread_over_yh(context_t, yh_index, y_blocks, others):
-    wide = context_t.shape[1] // y_blocks
+def spread_over_yh(context_t, yh_index, y_blocks):
+    wide, heads = context_t.shape[1] // y_blocks, context_t.shape[0]
     places = [
         lax.dynamic_slice_in_dim(context_t, jnp.bitwise_xor(yh_index, r) * wide, wide, 1)
         for r in range(y_blocks)
@@ -187,13 +187,11 @@
     while bit < y_blocks:
         crossing = [r for r in range(y_blocks) if r & bit]
         came = swapped(jnp.concatenate([places[r] for r in crossing], axis=0), "yh", y_blocks, bit)
-        if bit == 1:
-            came, others = lax.optimization_barrier((came, others))
-        heads = context_t.shape[0]
+        places = list(places)
         for i, r in enumerate(crossing):
             places[r] = came[i * heads:(i + 1) * heads]
+        places = yield places
         bit *= 2
-    return jnp.concatenate(places, axis=0), others
 
 
 def per_device(moe_in, out_grad, gates, routes, w_gate, w_up, w_down, context_t):
@@ -232,11 +230,16 @@
         experts * ROWS, parts * tok_rows
     )
     send = dot_f32(spread, stacked).astype(BF).reshape(experts, ROWS, piece_width)
-    send, weights, context_t = lax.optimization_barrier((send, weights, context_t))
+    swaps = spread_over_yh(context_t, yh_index, y_blocks)
+    places = next(swaps)
+    send, weights, places = lax.optimization_barrier((send, weights, places))
     received = exchange(send, plane)
-    other_gate = swap_pool(w_gate[0])
-    context_y, (up_matrix, down_matrix) = spread_over_yh(context_t, yh_index, y_blocks, (w_up[0], w_down[0]))
-    other_up, other_down = swap_pool(up_matrix), swap_pool(down_matrix)
+    other_gate, other_up, other_down = swap_pool(w_gate[0]), swap_pool(w_up[0]), swap_pool(w_down[0])
+    try:
+        while True:
+            places = swaps.send(places)
+    except StopIteration:
+        context_y = jnp.concatenate(places, axis=0)
     received, context_y = lax.optimization_barrier((received, context_y))
 
     back_width = model_width * own_slots // ROWS

time: 159 us -> 150 us (0.943)
  waiting for transfers between devices: 39.7 us -> 31.9 us
  starting transfers between devices: 55.7 us -> 52.8 us
    ppermute x4, waiting for transfers between devices: 27.4 us -> 19.3 us  [swapped(): return lax.ppermute(value, axis, tuple(((s, s ^ bit) for s in range(size))))]
    all_to_all x2, starting transfers between devices: 27 us -> 22.7 us  [exchange(): return lax.all_to_all(value, axes, split_axis=0, concat_axis=0, tiled=True)]
  transfers between devices with their start and end apart: 10 -> 10, of which waited for: 6 -> 5; matrix products, arithmetic and copies ran while one was open for 0% -> 3% of each run, Pallas kernels for 0% -> 0%
where the time goes in v6:
time: 150 us; the launch traced here: 149 us
  starting transfers between devices  52.8 us (35%)
  blocking collectives  48 us (32%)
  waiting for transfers between devices  31.9 us (21%)
  Pallas kernels  9.07 us (6%)
  local copies, waits for them, and re-layouts  2.88 us (2%)
  other arithmetic  1.66 us (1%)
  matrix products  1.66 us (1%)
    all_to_all x2, blocking collectives, exchange(): return lax.all_to_all(value, axes, split_axis=0, concat_axis=0, tiled=True)  48 us
    all_to_all x2, starting transfers between devices, exchange(): return lax.all_to_all(value, axes, split_axis=0, concat_axis=0, tiled=True)  22.7 us
    ppermute x4, starting transfers between devices, swapped(): return lax.ppermute(value, axis, tuple(((s, s ^ bit) for s in range(size))))  21.9 us
    ppermute x4, waiting for transfers between devices, swapped(): return lax.ppermute(value, axis, tuple(((s, s ^ bit) for s in range(size))))  19.3 us
    all_to_all x2, waiting for transfers between devices, exchange(): return lax.all_to_all(value, axes, split_axis=0, concat_axis=0, tiled=True)  11.3 us
    ppermute x4, starting transfers between devices, swap_pool(): return lax.ppermute(value, 'pool', ((0, 1), (1, 0)))  8.18 us
    pallas_call x1, Pallas kernels, expert_rows(): pl.pallas_call(expert_kernel, out_shape=jax.ShapeDtypeStruct((slots * wid...  8.12 us
  transfers between devices with their start and end apart: 10, of which 5 were waited for; matrix products, arithmetic and copies ran while one was open for 3% of the time, Pallas kernels for 0%

profile of v6, /device:TPU:2, one launch (start us, length us, event | category | flops | bytes accessed | tf_op | source)
XLA Modules:
  0.0 149.0 jit_solution(5241295580089400514)
XLA Ops:
  0.6 0.0 copy-start.3
  0.6 0.0 copy-start.2
  0.7 0.0 copy-start.1
  0.7 0.9 constant_dynamic-slice_fusion.2
  1.6 4.7 %collective-permute-start = (bf16[128,256]{1,0:T(8,128)(2,1)S(1)}, bf16[128,256]{1,0:T(8,128)(2,1)S(1)}, u32[]{:S(2)}, u32[]{:S(2)}) collective-permute-start(bf16[128,256]{1,0:T(8,128)(2,1)S(1)} %pad_maximum_fusion.1), channel_id=1, source_target_pairs={{0,16},{16,0},{32,48},{48,32},{1,17},{17,1},{33,49},{49,33},{2,18}... | collective-permute-start | bytes 196616 | tf_op jit(solution)/shard_map/ppermute | solution.py:177
  6.3 0.8 copy.23
  7.1 0.1 eq.52
  7.2 0.1 fusion.13
  7.3 0.2 reduce_window_sum.11
  7.4 0.2 select_reduce_fusion.1
  7.6 0.1 reduce_sum.39
  7.7 0.1 fusion.12
  7.8 0.1 copy.25
  8.0 0.3 broadcast_multiply_fusion
  8.2 0.3 mul.77
  8.5 0.0 copy-done.3
  8.5 0.1 copy.26
  8.6 0.0 copy-done.2
  8.6 0.0 copy-done.1
  8.6 0.0 copy-start
  8.6 1.4 fusion
  10.1 0.1 select_reduce_fusion
  10.2 0.0 collective-permute-done
  10.2 15.7 %all-to-all-start = ((bf16[64,8,1024]{2,1,0:T(8,128)(2,1)}), bf16[64,8,1024]{2,1,0:T(8,128)(2,1)S(1)}, u32[]{:S(2)}, u32[]{:S(2)}) async-start(bf16[64,8,1024]{2,1,0:T(8,128)(2,1)} %fusion), calls=%async_computation | async-start | bytes 2097152 | tf_op jit(solution)/shard_map/all_to_all | solution.py:173
  25.9 0.0 copy-done
  25.9 1.9 %collective-permute-start.2 = (bf16[2048,384]{1,0:T(8,128)(2,1)S(1)}, bf16[2048,384]{1,0:T(8,128)(2,1)}, u32[]{:S(2)}, u32[]{:S(2)}) collective-permute-start(bf16[2048,384]{1,0:T(8,128)(2,1)S(1)} %bitcast.25), channel_id=1, source_target_pairs={{0,512},{512,0},{1,513},{513,1},{2,514},{514,2},{3,515},{515,3},{4... | collective-permute-start | bytes 4718600 | tf_op jit(solution)/shard_map/ppermute | solution.py:169
  27.8 2.4 %collective-permute-start.3 = (bf16[2048,384]{1,0:T(8,128)(2,1)}, bf16[2048,384]{1,0:T(8,128)(2,1)}, u32[]{:S(2)}, u32[]{:S(2)}) collective-permute-start(bf16[2048,384]{1,0:T(8,128)(2,1)} %bitcast.27), channel_id=1, source_target_pairs={{0,512},{512,0},{1,513},{513,1},{2,514},{514,2},{3,515},{515,3},{4... | collective-permute-start | bytes 4718600 | tf_op jit(solution)/shard_map/ppermute | solution.py:169
  30.3 1.9 %collective-permute-start.4 = (bf16[384,2048]{1,0:T(8,128)(2,1)}, bf16[384,2048]{1,0:T(8,128)(2,1)}, u32[]{:S(2)}, u32[]{:S(2)}) collective-permute-start(bf16[384,2048]{1,0:T(8,128)(2,1)} %bitcast.29), channel_id=1, source_target_pairs={{0,512},{512,0},{1,513},{513,1},{2,514},{514,2},{3,515},{515,3},{4... | collective-permute-start | bytes 4718600 | tf_op jit(solution)/shard_map/ppermute | solution.py:169
  32.2 7.5 %collective-permute-start.1 = (bf16[128,256]{1,0:T(8,128)(2,1)S(1)}, bf16[128,256]{1,0:T(8,128)(2,1)S(1)}, u32[]{:S(2)}, u32[]{:S(2)}) collective-permute-start(bf16[128,256]{1,0:T(8,128)(2,1)S(1)} %pad_maximum_fusion.2), channel_id=1, source_target_pairs={{0,32},{16,48},{32,0},{48,16},{1,33},{17,49},{33,1},{49,17},{2,34}... | collective-permute-start | bytes 196616 | tf_op jit(solution)/shard_map/ppermute | solution.py:177
  39.7 15.0 %collective-permute-done.1 = bf16[128,256]{1,0:T(8,128)(2,1)S(1)} collective-permute-done((bf16[128,256]{1,0:T(8,128)(2,1)S(1)}, bf16[128,256]{1,0:T(8,128)(2,1)S(1)}, u32[]{:S(2)}, u32[]{:S(2)}) %collective-permute-start.1) | collective-permute-done | bytes 65568 | tf_op jit(solution)/shard_map/ppermute | solution.py:177
  54.7 0.0 all-to-all-done
  54.8 0.0 collective-permute-done.2.refs_3_
  54.8 0.0 collective-permute-done.3.refs_4_
  54.8 0.0 collective-permute-done.4.refs_5_
  54.8 8.1 %expert.1 = bf16[512,512]{1,0:T(8,128)(2,1)} custom-call(bf16[512,1024]{1,0:T(8,128)(2,1)S(1)} %bitcast.24, bf16[2048,384]{1,0:T(8,128)(2,1)S(1)} %bitcast.26, bf16[2048,384]{1,0:T(8,128)(2,1)} %bitcast.28, bf16[384,2048]{1,0:T(8,128)(2,1)} %bitcast.30, bf16[2048,384]{1,0:T(8,128)(2,1)} %collective-permute-done.2.refs_3_, ...), custom_call_target="tpu_custom_call" | custom-call | flops 2013265920 | bytes 9437184 | tf_op jit(solution)/shard_map/expert/pallas_call | solution.py:83
  62.9 7.0 %all-to-all-start.1 = ((bf16[64,8,512]{2,1,0:T(8,128)(2,1)}), bf16[64,8,512]{2,1,0:T(8,128)(2,1)S(1)}, u32[]{:S(2)}, u32[]{:S(2)}) async-start(bf16[64,8,512]{2,1,0:T(8,128)(2,1)} %bitcast.10), calls=%async_computation.1 | async-start | bytes 1048576 | tf_op jit(solution)/shard_map/all_to_all | solution.py:173
  70.0 0.2 mul.86
  70.2 5.0 %collective-permute-start.5 = (bf16[256,256]{1,0:T(8,128)(2,1)S(1)}, bf16[256,256]{1,0:T(8,128)(2,1)S(1)}, u32[]{:S(2)}, u32[]{:S(2)}) collective-permute-start(bf16[256,256]{1,0:T(8,128)(2,1)S(1)} %pad_maximum_fusion.refs_0_), channel_id=1, source_target_pairs={{0,64},{64,0},{1,65},{65,1},{2,66},{66,2},{3,67},{67,3},{4,68},{68... | collective-permute-start | bytes 393224 | tf_op jit(solution)/shard_map/ppermute | solution.py:177
  75.2 0.1 copy.27
  75.3 0.1 mul.82
  75.4 0.1 copy.28
  75.5 2.6 %collective-permute-done.5.refs_1_ = bf16[256,256]{1,0:T(8,128)(2,1)S(1)} collective-permute-done((bf16[256,256]{1,0:T(8,128)(2,1)S(1)}, bf16[256,256]{1,0:T(8,128)(2,1)S(1)}, u32[]{:S(2)}, u32[]{:S(2)}) %collective-permute-start.5) | collective-permute-done | bytes 131104 | tf_op jit(solution)/shard_map/ppermute | solution.py:177
  78.1 11.3 %all-to-all-done.1 = bf16[64,8,512]{2,1,0:T(8,128)(2,1)S(1)} async-done(((bf16[64,8,512]{2,1,0:T(8,128)(2,1)}), bf16[64,8,512]{2,1,0:T(8,128)(2,1)S(1)}, u32[]{:S(2)}, u32[]{:S(2)}) %all-to-all-start.1) | async-done | bytes 524320 | tf_op jit(solution)/shard_map/all_to_all | solution.py:173
  89.5 0.2 convolution_reduce_fusion
  89.7 1.9 %collective-permute-start.6 = (f32[2,16,512]{2,1,0:T(8,128)S(1)}, f32[2,16,512]{2,1,0:T(8,128)S(1)}, u32[]{:S(2)}, u32[]{:S(2)}) collective-permute-start(f32[2,16,512]{2,1,0:T(8,128)S(1)} %get-tuple-element.30), channel_id=1, source_target_pairs={{0,512},{512,0},{1,513},{513,1},{2,514},{514,2},{3,515},{515,3},{4... | collective-permute-start | bytes 196616 | tf_op jit(solution)/shard_map/ppermute | solution.py:169
  91.7 1.2 collective-permute-done.6.came_ref
  92.9 0.6 finish.1
  93.5 4.7 %collective-permute-start.7 = (bf16[16,512]{1,0:T(8,128)(2,1)S(1)}, bf16[16,512]{1,0:T(8,128)(2,1)S(1)}, u32[]{:S(2)}, u32[]{:S(2)}) collective-permute-start(bf16[16,512]{1,0:T(8,128)(2,1)S(1)} %get-tuple-element.29), channel_id=1, source_target_pairs={{0,64},{64,0},{1,65},{65,1},{2,66},{66,2},{3,67},{67,3},{4,68},{68... | collective-permute-start | bytes 49160 | tf_op jit(solution)/shard_map/ppermute | solution.py:177
  98.2 1.7 %collective-permute-done.7 = bf16[16,512]{1,0:T(8,128)(2,1)S(1)} collective-permute-done((bf16[16,512]{1,0:T(8,128)(2,1)S(1)}, bf16[16,512]{1,0:T(8,128)(2,1)S(1)}, u32[]{:S(2)}, u32[]{:S(2)}) %collective-permute-start.7) | collective-permute-done | bytes 16416 | tf_op jit(solution)/shard_map/ppermute | solution.py:177
  100.0 18.9 %all_to_all.20.refs_2_ = bf16[16,32,512]{2,1,0:T(8,128)(2,1)S(1)} all-to-all(bf16[16,32,512]{2,1,0:T(8,128)(2,1)S(1)} %broadcast_in_dim.18), channel_id=1, replica_groups=mesh['pool'=2,'zh'=4,'zl'=2,'yh'=4,'yl'=2,'x'=8] {'yl','x'}, dimensions={0} | all-to-all | bytes 1048576 | tf_op jit(solution)/shard_map/all_to_all | solution.py:173
  118.9 0.3 context_product.1
  119.2 29.1 %all_to_all.21 = bf16[16,64,128]{2,1,0:T(8,128)(2,1)S(1)} all-to-all(bf16[16,64,128]{2,1,0:T(8,128)(2,1)S(1)} %context_product.1), channel_id=1, replica_groups=mesh['pool'=2,'zh'=4,'zl'=2,'yh'=4,'yl'=2,'x'=8] {'zh','yh'}, dimensions={0} | all-to-all | bytes 524288 | tf_op jit(solution)/shard_map/all_to_all | solution.py:173
  148.3 0.7 convert_reduce_fusion
  (14 shorter events, 0.2 us)
Async XLA Ops:
  0.6 7.9 %copy-start.3 = (f32[16,8]{0,1:T(8,128)S(1)}, f32[16,8]{0,1:T(8,128)}, u32[]{:S(2)}) copy-start(f32[16,8]{0,1:T(8,128)} %param.10) | copy-start | bytes 1540
  0.6 8.0 %copy-start.2 = (bf16[16,2048]{1,0:T(8,128)(2,1)S(1)}, bf16[16,2048]{1,0:T(8,128)(2,1)}, u32[]{:S(2)}) copy-start(bf16[16,2048]{1,0:T(8,128)(2,1)} %param.8) | copy-start | bytes 196612
  0.7 8.0 %copy-start.1 = (bf16[16,2048]{1,0:T(8,128)(2,1)S(1)}, bf16[16,2048]{1,0:T(8,128)(2,1)}, u32[]{:S(2)}) copy-start(bf16[16,2048]{1,0:T(8,128)(2,1)} %param.9) | copy-start | bytes 196612
  1.6 8.6 %collective-permute-start = (bf16[128,256]{1,0:T(8,128)(2,1)S(1)}, bf16[128,256]{1,0:T(8,128)(2,1)S(1)}, u32[]{:S(2)}, u32[]{:S(2)}) collective-permute-start(bf16[128,256]{1,0:T(8,128)(2,1)S(1)} %pad_maximum_fusion.1), channel_id=1, source_target_pairs={{0,16},{16,0},{32,48},{48,32},{1,17},{17,1},{33,49},{49,33},{2,18}... | collective-permute-start | bytes 196616 | tf_op jit(solution)/shard_map/ppermute | solution.py:177
  8.6 17.3 %copy-start = (bf16[1,2048,384]{2,1,0:T(8,128)(2,1)S(1)}, bf16[1,2048,384]{2,1,0:T(8,128)(2,1)}, u32[]{:S(2)}) copy-start(bf16[1,2048,384]{2,1,0:T(8,128)(2,1)} %param.12) | copy-start | bytes 4718596
  10.2 44.5 %all-to-all-start = ((bf16[64,8,1024]{2,1,0:T(8,128)(2,1)}), bf16[64,8,1024]{2,1,0:T(8,128)(2,1)S(1)}, u32[]{:S(2)}, u32[]{:S(2)}) async-start(bf16[64,8,1024]{2,1,0:T(8,128)(2,1)} %fusion), calls=%async_computation | async-start | bytes 2097152 | tf_op jit(solution)/shard_map/all_to_all | solution.py:173
  25.9 28.8 %collective-permute-start.2 = (bf16[2048,384]{1,0:T(8,128)(2,1)S(1)}, bf16[2048,384]{1,0:T(8,128)(2,1)}, u32[]{:S(2)}, u32[]{:S(2)}) collective-permute-start(bf16[2048,384]{1,0:T(8,128)(2,1)S(1)} %bitcast.25), channel_id=1, source_target_pairs={{0,512},{512,0},{1,513},{513,1},{2,514},{514,2},{3,515},{515,3},{4... | collective-permute-start | bytes 4718600 | tf_op jit(solution)/shard_map/ppermute | solution.py:169
  27.8 26.9 %collective-permute-start.3 = (bf16[2048,384]{1,0:T(8,128)(2,1)}, bf16[2048,384]{1,0:T(8,128)(2,1)}, u32[]{:S(2)}, u32[]{:S(2)}) collective-permute-start(bf16[2048,384]{1,0:T(8,128)(2,1)} %bitcast.27), channel_id=1, source_target_pairs={{0,512},{512,0},{1,513},{513,1},{2,514},{514,2},{3,515},{515,3},{4... | collective-permute-start | bytes 4718600 | tf_op jit(solution)/shard_map/ppermute | solution.py:169
  30.3 24.5 %collective-permute-start.4 = (bf16[384,2048]{1,0:T(8,128)(2,1)}, bf16[384,2048]{1,0:T(8,128)(2,1)}, u32[]{:S(2)}, u32[]{:S(2)}) collective-permute-start(bf16[384,2048]{1,0:T(8,128)(2,1)} %bitcast.29), channel_id=1, source_target_pairs={{0,512},{512,0},{1,513},{513,1},{2,514},{514,2},{3,515},{515,3},{4... | collective-permute-start | bytes 4718600 | tf_op jit(solution)/shard_map/ppermute | solution.py:169
  32.2 22.5 %collective-permute-start.1 = (bf16[128,256]{1,0:T(8,128)(2,1)S(1)}, bf16[128,256]{1,0:T(8,128)(2,1)S(1)}, u32[]{:S(2)}, u32[]{:S(2)}) collective-permute-start(bf16[128,256]{1,0:T(8,128)(2,1)S(1)} %pad_maximum_fusion.2), channel_id=1, source_target_pairs={{0,32},{16,48},{32,0},{48,16},{1,33},{17,49},{33,1},{49,17},{2,34}... | collective-permute-start | bytes 196616 | tf_op jit(solution)/shard_map/ppermute | solution.py:177
  62.9 26.5 %all-to-all-start.1 = ((bf16[64,8,512]{2,1,0:T(8,128)(2,1)}), bf16[64,8,512]{2,1,0:T(8,128)(2,1)S(1)}, u32[]{:S(2)}, u32[]{:S(2)}) async-start(bf16[64,8,512]{2,1,0:T(8,128)(2,1)} %bitcast.10), calls=%async_computation.1 | async-start | bytes 1048576 | tf_op jit(solution)/shard_map/all_to_all | solution.py:173
  70.2 7.9 %collective-permute-start.5 = (bf16[256,256]{1,0:T(8,128)(2,1)S(1)}, bf16[256,256]{1,0:T(8,128)(2,1)S(1)}, u32[]{:S(2)}, u32[]{:S(2)}) collective-permute-start(bf16[256,256]{1,0:T(8,128)(2,1)S(1)} %pad_maximum_fusion.refs_0_), channel_id=1, source_target_pairs={{0,64},{64,0},{1,65},{65,1},{2,66},{66,2},{3,67},{67,3},{4,68},{68... | collective-permute-start | bytes 393224 | tf_op jit(solution)/shard_map/ppermute | solution.py:177
  89.7 3.1 %collective-permute-start.6 = (f32[2,16,512]{2,1,0:T(8,128)S(1)}, f32[2,16,512]{2,1,0:T(8,128)S(1)}, u32[]{:S(2)}, u32[]{:S(2)}) collective-permute-start(f32[2,16,512]{2,1,0:T(8,128)S(1)} %get-tuple-element.30), channel_id=1, source_target_pairs={{0,512},{512,0},{1,513},{513,1},{2,514},{514,2},{3,515},{515,3},{4... | collective-permute-start | bytes 196616 | tf_op jit(solution)/shard_map/ppermute | solution.py:169
  93.5 6.4 %collective-permute-start.7 = (bf16[16,512]{1,0:T(8,128)(2,1)S(1)}, bf16[16,512]{1,0:T(8,128)(2,1)S(1)}, u32[]{:S(2)}, u32[]{:S(2)}) collective-permute-start(bf16[16,512]{1,0:T(8,128)(2,1)S(1)} %get-tuple-element.29), channel_id=1, source_target_pairs={{0,64},{64,0},{1,65},{65,1},{2,66},{66,2},{3,67},{67,3},{4,68},{68... | collective-permute-start | bytes 49160 | tf_op jit(solution)/shard_map/ppermute | solution.py:177

commit v7 on v5

--- a/solution.py
+++ b/solution.py
@@ -111,7 +111,7 @@
     yh_index = place_ref[0]
     for z in range(z_blocks):
         for apart in range(y_blocks):
-            out_ref[z * y_blocks + jnp.bitwise_xor(yh_index, apart)] = total[
+            out_ref[jnp.bitwise_xor(yh_index, apart) * z_blocks + z] = total[
                 apart * heads:(apart + 1) * heads, z * cols:(z + 1) * cols
             ].astype(BF)
 
@@ -121,7 +121,7 @@
     width = tokens_b.shape[2]
     return pl.pallas_call(
         product_kernel,
-        out_shape=jax.ShapeDtypeStruct((z_blocks * y_blocks, rows // y_blocks, width // z_blocks), BF),
+        out_shape=jax.ShapeDtypeStruct((y_blocks * z_blocks, rows // y_blocks, width // z_blocks), BF),
         in_specs=[pl.BlockSpec(memory_space=pltpu.SMEM)]
         + [pl.BlockSpec(memory_space=pltpu.VMEM)] * (len(contexts) + 1),
         out_specs=pl.BlockSpec(memory_space=pltpu.VMEM),
@@ -177,23 +177,22 @@
     return lax.ppermute(value, axis, tuple((s, s ^ bit) for s in range(size)))
 
 
-def spread_over_yh(context_t, yh_index, y_blocks, others):
+def context_blocks(context_t, yh_index, y_blocks):
     wide = context_t.shape[1] // y_blocks
-    places = [
+    return [
         lax.dynamic_slice_in_dim(context_t, jnp.bitwise_xor(yh_index, r) * wide, wide, 1)
         for r in range(y_blocks)
     ]
-    bit = 1
-    while bit < y_blocks:
-        crossing = [r for r in range(y_blocks) if r & bit]
-        came = swapped(jnp.concatenate([places[r] for r in crossing], axis=0), "yh", y_blocks, bit)
-        if bit == 1:
-            came, others = lax.optimization_barrier((came, others))
-        heads = context_t.shape[0]
-        for i, r in enumerate(crossing):
-            places[r] = came[i * heads:(i + 1) * heads]
-        bit *= 2
-    return jnp.concatenate(places, axis=0), others
+
+
+def swap_places(pieces, bit):
+    y_blocks, heads = len(pieces[0]), pieces[0][0].shape[0]
+    crossing = [(i, r) for i in range(len(pieces)) for r in range(y_blocks) if r & bit]
+    came = swapped(jnp.concatenate([pieces[i][r] for i, r in crossing], axis=0), "yh", y_blocks, bit)
+    pieces = [list(places) for places in pieces]
+    for at, (i, r) in enumerate(crossing):
+        pieces[i][r] = came[at * heads:(at + 1) * heads]
+    return pieces
 
 
 def per_device(moe_in, out_grad, gates, routes, w_gate, w_up, w_down, context_t):
@@ -232,12 +231,14 @@
         experts * ROWS, parts * tok_rows
     )
     send = dot_f32(spread, stacked).astype(BF).reshape(experts, ROWS, piece_width)
-    send, weights, context_t = lax.optimization_barrier((send, weights, context_t))
+    heads = context_t.shape[0]
+    [places] = swap_places([context_blocks(context_t, yh_index, y_blocks)], 2)
+    send, weights, places = lax.optimization_barrier((send, weights, places))
     received = exchange(send, plane)
-    other_gate = swap_pool(w_gate[0])
-    context_y, (up_matrix, down_matrix) = spread_over_yh(context_t, yh_index, y_blocks, (w_up[0], w_down[0]))
-    other_up, other_down = swap_pool(up_matrix), swap_pool(down_matrix)
-    received, context_y = lax.optimization_barrier((received, context_y))
+    other_gate, other_up, other_down = swap_pool(w_gate[0]), swap_pool(w_up[0]), swap_pool(w_down[0])
+    beside = swapped(jnp.concatenate(places, axis=0), "zl", 2, 1)
+    received, beside = lax.optimization_barrier((received, beside))
+    pieces = [places, [beside[r * heads:(r + 1) * heads] for r in range(y_blocks)]]
 
     back_width = model_width * own_slots // ROWS
     back_parts = model_width // back_width
@@ -247,7 +248,7 @@
         back_width,
     ).reshape(experts, ROWS, back_width)
     returned = exchange(back, plane)
-    contexts = [context_y, swapped(context_y, "zl", 2, 1)]
+    contexts = [jnp.concatenate(piece, axis=0) for piece in swap_places(pieces, 1)]
     returned, contexts = lax.optimization_barrier((returned, contexts))
 
     high = lax.reduce_precision(weights, 8, 7).astype(BF)
@@ -267,7 +268,7 @@
     pair = jnp.concatenate((keep, swapped(give, "zl", 2, 1)), axis=0)
     gathered_b = exchange(jnp.broadcast_to(pair[None], (peers, *pair.shape)), ("yl", "x"))
     terms = exchange(
-        context_product(yh_index, contexts, gathered_b, y_blocks, z_blocks), ("zh", "yh")
+        context_product(yh_index, contexts, gathered_b, y_blocks, z_blocks), ("yh", "zh")
     )
     wo_grad = jnp.sum(terms.astype(F32), axis=0)
     return (hidden_grad, wo_grad)

time: 159 us -> 151 us (0.950)
  waiting for transfers between devices: 39.7 us -> 30.1 us
  blocking collectives: 47.9 us -> 52.3 us
  starting transfers between devices: 55.7 us -> 51.9 us
    ppermute x4, waiting for transfers between devices: 27.4 us -> 17.9 us  [swapped(): return lax.ppermute(value, axis, tuple(((s, s ^ bit) for s in range(size))))]
    all_to_all x2, starting transfers between devices: 27 us -> 21.5 us  [exchange(): return lax.all_to_all(value, axes, split_axis=0, concat_axis=0, tiled=True)]
    all_to_all x2, blocking collectives: 47.9 us -> 52.3 us  [exchange(): return lax.all_to_all(value, axes, split_axis=0, concat_axis=0, tiled=True)]
    ppermute x4, starting transfers between devices: 20.5 us -> 22.2 us  [swapped(): return lax.ppermute(value, axis, tuple(((s, s ^ bit) for s in range(size))))]
  transfers between devices with their start and end apart: 10 -> 10, of which waited for: 6 -> 5; matrix products, arithmetic and copies ran while one was open for 0% -> 3% of each run, Pallas kernels for 0% -> 0%
where the time goes in v7:
time: 151 us
  blocking collectives  52.3 us (35%)
  starting transfers between devices  51.9 us (34%)
  waiting for transfers between devices  30.1 us (20%)
  Pallas kernels  9.07 us (6%)
  local copies, waits for them, and re-layouts  2.9 us (2%)
  other arithmetic  1.69 us (1%)
  matrix products  1.65 us (1%)
    all_to_all x2, blocking collectives, exchange(): return lax.all_to_all(value, axes, split_axis=0, concat_axis=0, tiled=True)  52.3 us
    ppermute x4, starting transfers between devices, swapped(): return lax.ppermute(value, axis, tuple(((s, s ^ bit) for s in range(size))))  22.2 us
    all_to_all x2, starting transfers between devices, exchange(): return lax.all_to_all(value, axes, split_axis=0, concat_axis=0, tiled=True)  21.5 us
    ppermute x4, waiting for transfers between devices, swapped(): return lax.ppermute(value, axis, tuple(((s, s ^ bit) for s in range(size))))  17.9 us
    all_to_all x2, waiting for transfers between devices, exchange(): return lax.all_to_all(value, axes, split_axis=0, concat_axis=0, tiled=True)  11 us
    ppermute x4, starting transfers between devices, swap_pool(): return lax.ppermute(value, 'pool', ((0, 1), (1, 0)))  8.18 us
    pallas_call x1, Pallas kernels, expert_rows(): pl.pallas_call(expert_kernel, out_shape=jax.ShapeDtypeStruct((slots * wid...  8.12 us
  transfers between devices with their start and end apart: 10, of which 5 were waited for; matrix products, arithmetic and copies ran while one was open for 3% of the time, Pallas kernels for 0%

profile of v7, /device:TPU:2, one launch (start us, length us, event | category | flops | bytes accessed | tf_op | source)
XLA Modules:
  0.0 150.6 jit_solution(5299575576154534174)
XLA Ops:
  0.6 0.0 copy-start.3
  0.6 0.0 copy-start.2
  0.7 0.0 copy-start.1
  0.7 0.9 constant_dynamic-slice_fusion.3
  1.6 8.2 %collective-permute-start = (bf16[128,256]{1,0:T(8,128)(2,1)S(1)}, bf16[128,256]{1,0:T(8,128)(2,1)S(1)}, u32[]{:S(2)}, u32[]{:S(2)}) collective-permute-start(bf16[128,256]{1,0:T(8,128)(2,1)S(1)} %pad_maximum_fusion.6), channel_id=1, source_target_pairs={{0,32},{16,48},{32,0},{48,16},{1,33},{17,49},{33,1},{49,17},{2,34}... | collective-permute-start | bytes 196616 | tf_op jit(solution)/shard_map/ppermute | solution.py:177
  9.8 0.8 copy.23
  10.5 0.1 eq.52
  10.6 0.1 fusion.15
  10.7 0.2 reduce_window_sum.11
  10.9 0.2 select_reduce_fusion.1
  11.1 0.1 reduce_sum.39
  11.2 0.1 fusion.14
  11.3 0.1 copy.25
  11.4 0.3 broadcast_multiply_fusion
  11.7 0.3 mul.77
  12.0 0.0 copy-done.3
  12.0 0.1 copy.26
  12.1 0.0 copy-done.2
  12.1 0.0 copy-done.1
  12.1 0.0 copy-start
  12.1 1.4 fusion
  13.5 0.1 select_reduce_fusion
  13.7 0.0 collective-permute-done
  13.7 15.2 %all-to-all-start = ((bf16[64,8,1024]{2,1,0:T(8,128)(2,1)}), bf16[64,8,1024]{2,1,0:T(8,128)(2,1)S(1)}, u32[]{:S(2)}, u32[]{:S(2)}) async-start(bf16[64,8,1024]{2,1,0:T(8,128)(2,1)} %fusion), calls=%async_computation | async-start | bytes 2097152 | tf_op jit(solution)/shard_map/all_to_all | solution.py:173
  28.9 0.0 copy-done
  28.9 1.9 %collective-permute-start.2 = (bf16[2048,384]{1,0:T(8,128)(2,1)S(1)}, bf16[2048,384]{1,0:T(8,128)(2,1)}, u32[]{:S(2)}, u32[]{:S(2)}) collective-permute-start(bf16[2048,384]{1,0:T(8,128)(2,1)S(1)} %bitcast.25), channel_id=1, source_target_pairs={{0,512},{512,0},{1,513},{513,1},{2,514},{514,2},{3,515},{515,3},{4... | collective-permute-start | bytes 4718600 | tf_op jit(solution)/shard_map/ppermute | solution.py:169
  30.8 2.4 %collective-permute-start.3 = (bf16[2048,384]{1,0:T(8,128)(2,1)}, bf16[2048,384]{1,0:T(8,128)(2,1)}, u32[]{:S(2)}, u32[]{:S(2)}) collective-permute-start(bf16[2048,384]{1,0:T(8,128)(2,1)} %bitcast.27), channel_id=1, source_target_pairs={{0,512},{512,0},{1,513},{513,1},{2,514},{514,2},{3,515},{515,3},{4... | collective-permute-start | bytes 4718600 | tf_op jit(solution)/shard_map/ppermute | solution.py:169
  33.3 1.9 %collective-permute-start.4 = (bf16[384,2048]{1,0:T(8,128)(2,1)}, bf16[384,2048]{1,0:T(8,128)(2,1)}, u32[]{:S(2)}, u32[]{:S(2)}) collective-permute-start(bf16[384,2048]{1,0:T(8,128)(2,1)} %bitcast.29), channel_id=1, source_target_pairs={{0,512},{512,0},{1,513},{513,1},{2,514},{514,2},{3,515},{515,3},{4... | collective-permute-start | bytes 4718600 | tf_op jit(solution)/shard_map/ppermute | solution.py:169
  35.2 2.6 %collective-permute-start.1 = (bf16[256,256]{1,0:T(8,128)(2,1)S(1)}, bf16[256,256]{1,0:T(8,128)(2,1)S(1)}, u32[]{:S(2)}, u32[]{:S(2)}) collective-permute-start(bf16[256,256]{1,0:T(8,128)(2,1)S(1)} %fusion.2), channel_id=1, source_target_pairs={{0,64},{64,0},{1,65},{65,1},{2,66},{66,2},{3,67},{67,3},{4,68},{68... | collective-permute-start | bytes 393224 | tf_op jit(solution)/shard_map/ppermute | solution.py:177
  37.8 0.2 mul.86
  38.0 5.0 %collective-permute-done.1 = bf16[256,256]{1,0:T(8,128)(2,1)S(1)} collective-permute-done((bf16[256,256]{1,0:T(8,128)(2,1)S(1)}, bf16[256,256]{1,0:T(8,128)(2,1)S(1)}, u32[]{:S(2)}, u32[]{:S(2)}) %collective-permute-start.1) | collective-permute-done | bytes 131104 | tf_op jit(solution)/shard_map/ppermute | solution.py:177
  43.0 11.0 %all-to-all-done = bf16[64,8,1024]{2,1,0:T(8,128)(2,1)S(1)} async-done(((bf16[64,8,1024]{2,1,0:T(8,128)(2,1)}), bf16[64,8,1024]{2,1,0:T(8,128)(2,1)S(1)}, u32[]{:S(2)}, u32[]{:S(2)}) %all-to-all-start) | async-done | bytes 1048608 | tf_op jit(solution)/shard_map/all_to_all | solution.py:173
  54.0 0.0 collective-permute-done.2.refs_3_
  54.0 0.0 collective-permute-done.3.refs_4_
  54.0 0.0 collective-permute-done.4.refs_5_
  54.1 8.1 %expert.1 = bf16[512,512]{1,0:T(8,128)(2,1)} custom-call(bf16[512,1024]{1,0:T(8,128)(2,1)S(1)} %bitcast.24, bf16[2048,384]{1,0:T(8,128)(2,1)S(1)} %bitcast.26, bf16[2048,384]{1,0:T(8,128)(2,1)} %bitcast.28, bf16[384,2048]{1,0:T(8,128)(2,1)} %bitcast.30, bf16[2048,384]{1,0:T(8,128)(2,1)} %collective-permute-done.2.refs_3_, ...), custom_call_target="tpu_custom_call" | custom-call | flops 2013265920 | bytes 9437184 | tf_op jit(solution)/shard_map/expert/pallas_call | solution.py:83
  62.2 6.3 %all-to-all-start.1 = ((bf16[64,8,512]{2,1,0:T(8,128)(2,1)}), bf16[64,8,512]{2,1,0:T(8,128)(2,1)S(1)}, u32[]{:S(2)}, u32[]{:S(2)}) async-start(bf16[64,8,512]{2,1,0:T(8,128)(2,1)} %bitcast.10), calls=%async_computation.1 | async-start | bytes 1048576 | tf_op jit(solution)/shard_map/all_to_all | solution.py:173
  68.5 4.3 %collective-permute-start.5 = (bf16[256,256]{1,0:T(8,128)(2,1)S(1)}, bf16[256,256]{1,0:T(8,128)(2,1)S(1)}, u32[]{:S(2)}, u32[]{:S(2)}) collective-permute-start(bf16[256,256]{1,0:T(8,128)(2,1)S(1)} %pad_maximum_fusion.4), channel_id=1, source_target_pairs={{0,16},{16,0},{32,48},{48,32},{1,17},{17,1},{33,49},{49,33},{2,18}... | collective-permute-start | bytes 393224 | tf_op jit(solution)/shard_map/ppermute | solution.py:177
  72.8 0.1 copy.27
  73.0 0.1 mul.82
  73.0 0.1 copy.28
  73.1 11.1 %collective-permute-done.5 = bf16[256,256]{1,0:T(8,128)(2,1)S(1)} collective-permute-done((bf16[256,256]{1,0:T(8,128)(2,1)S(1)}, bf16[256,256]{1,0:T(8,128)(2,1)S(1)}, u32[]{:S(2)}, u32[]{:S(2)}) %collective-permute-start.5) | collective-permute-done | bytes 131104 | tf_op jit(solution)/shard_map/ppermute | solution.py:177
  84.3 0.0 all-to-all-done.1
  84.3 0.2 convolution_reduce_fusion
  84.6 1.9 %collective-permute-start.6 = (f32[2,16,512]{2,1,0:T(8,128)S(1)}, f32[2,16,512]{2,1,0:T(8,128)S(1)}, u32[]{:S(2)}, u32[]{:S(2)}) collective-permute-start(f32[2,16,512]{2,1,0:T(8,128)S(1)} %get-tuple-element.30), channel_id=1, source_target_pairs={{0,512},{512,0},{1,513},{513,1},{2,514},{514,2},{3,515},{515,3},{4... | collective-permute-start | bytes 196616 | tf_op jit(solution)/shard_map/ppermute | solution.py:169
  86.5 1.2 collective-permute-done.6.came_ref
  87.8 0.6 finish.1
  88.4 7.2 %collective-permute-start.7 = (bf16[16,512]{1,0:T(8,128)(2,1)S(1)}, bf16[16,512]{1,0:T(8,128)(2,1)S(1)}, u32[]{:S(2)}, u32[]{:S(2)}) collective-permute-start(bf16[16,512]{1,0:T(8,128)(2,1)S(1)} %get-tuple-element.29), channel_id=1, source_target_pairs={{0,64},{64,0},{1,65},{65,1},{2,66},{66,2},{3,67},{67,3},{4,68},{68... | collective-permute-start | bytes 49160 | tf_op jit(solution)/shard_map/ppermute | solution.py:177
  95.6 1.7 %collective-permute-done.7 = bf16[16,512]{1,0:T(8,128)(2,1)S(1)} collective-permute-done((bf16[16,512]{1,0:T(8,128)(2,1)S(1)}, bf16[16,512]{1,0:T(8,128)(2,1)S(1)}, u32[]{:S(2)}, u32[]{:S(2)}) %collective-permute-start.7) | collective-permute-done | bytes 16416 | tf_op jit(solution)/shard_map/ppermute | solution.py:177
  97.4 20.9 %all_to_all.20.refs_2_ = bf16[16,32,512]{2,1,0:T(8,128)(2,1)S(1)} all-to-all(bf16[16,32,512]{2,1,0:T(8,128)(2,1)S(1)} %broadcast_in_dim.18), channel_id=1, replica_groups=mesh['pool'=2,'zh'=4,'zl'=2,'yh'=4,'yl'=2,'x'=8] {'yl','x'}, dimensions={0} | all-to-all | bytes 1048576 | tf_op jit(solution)/shard_map/all_to_all | solution.py:173
  118.2 0.3 context_product.1
  118.5 31.4 %all_to_all.21 = bf16[16,64,128]{2,1,0:T(8,128)(2,1)S(1)} all-to-all(bf16[16,64,128]{2,1,0:T(8,128)(2,1)S(1)} %context_product.1), channel_id=1, replica_groups=mesh['pool'=2,'zh'=4,'zl'=2,'yh'=4,'yl'=2,'x'=8] {'yh','zh'}, dimensions={0} | all-to-all | bytes 524288 | tf_op jit(solution)/shard_map/all_to_all | solution.py:173
  149.9 0.7 convert_reduce_fusion
  (18 shorter events, 0.2 us)
Async XLA Ops:
  0.6 11.4 %copy-start.3 = (f32[16,8]{0,1:T(8,128)S(1)}, f32[16,8]{0,1:T(8,128)}, u32[]{:S(2)}) copy-start(f32[16,8]{0,1:T(8,128)} %param.10) | copy-start | bytes 1540
  0.6 11.4 %copy-start.2 = (bf16[16,2048]{1,0:T(8,128)(2,1)S(1)}, bf16[16,2048]{1,0:T(8,128)(2,1)}, u32[]{:S(2)}) copy-start(bf16[16,2048]{1,0:T(8,128)(2,1)} %param.8) | copy-start | bytes 196612
  0.7 11.4 %copy-start.1 = (bf16[16,2048]{1,0:T(8,128)(2,1)S(1)}, bf16[16,2048]{1,0:T(8,128)(2,1)}, u32[]{:S(2)}) copy-start(bf16[16,2048]{1,0:T(8,128)(2,1)} %param.9) | copy-start | bytes 196612
  1.6 12.1 %collective-permute-start = (bf16[128,256]{1,0:T(8,128)(2,1)S(1)}, bf16[128,256]{1,0:T(8,128)(2,1)S(1)}, u32[]{:S(2)}, u32[]{:S(2)}) collective-permute-start(bf16[128,256]{1,0:T(8,128)(2,1)S(1)} %pad_maximum_fusion.6), channel_id=1, source_target_pairs={{0,32},{16,48},{32,0},{48,16},{1,33},{17,49},{33,1},{49,17},{2,34}... | collective-permute-start | bytes 196616 | tf_op jit(solution)/shard_map/ppermute | solution.py:177
  12.1 16.8 %copy-start = (bf16[1,2048,384]{2,1,0:T(8,128)(2,1)S(1)}, bf16[1,2048,384]{2,1,0:T(8,128)(2,1)}, u32[]{:S(2)}) copy-start(bf16[1,2048,384]{2,1,0:T(8,128)(2,1)} %param.12) | copy-start | bytes 4718596
  13.7 40.4 %all-to-all-start = ((bf16[64,8,1024]{2,1,0:T(8,128)(2,1)}), bf16[64,8,1024]{2,1,0:T(8,128)(2,1)S(1)}, u32[]{:S(2)}, u32[]{:S(2)}) async-start(bf16[64,8,1024]{2,1,0:T(8,128)(2,1)} %fusion), calls=%async_computation | async-start | bytes 2097152 | tf_op jit(solution)/shard_map/all_to_all | solution.py:173
  28.9 25.1 %collective-permute-start.2 = (bf16[2048,384]{1,0:T(8,128)(2,1)S(1)}, bf16[2048,384]{1,0:T(8,128)(2,1)}, u32[]{:S(2)}, u32[]{:S(2)}) collective-permute-start(bf16[2048,384]{1,0:T(8,128)(2,1)S(1)} %bitcast.25), channel_id=1, source_target_pairs={{0,512},{512,0},{1,513},{513,1},{2,514},{514,2},{3,515},{515,3},{4... | collective-permute-start | bytes 4718600 | tf_op jit(solution)/shard_map/ppermute | solution.py:169
  30.8 23.2 %collective-permute-start.3 = (bf16[2048,384]{1,0:T(8,128)(2,1)}, bf16[2048,384]{1,0:T(8,128)(2,1)}, u32[]{:S(2)}, u32[]{:S(2)}) collective-permute-start(bf16[2048,384]{1,0:T(8,128)(2,1)} %bitcast.27), channel_id=1, source_target_pairs={{0,512},{512,0},{1,513},{513,1},{2,514},{514,2},{3,515},{515,3},{4... | collective-permute-start | bytes 4718600 | tf_op jit(solution)/shard_map/ppermute | solution.py:169
  33.3 20.8 %collective-permute-start.4 = (bf16[384,2048]{1,0:T(8,128)(2,1)}, bf16[384,2048]{1,0:T(8,128)(2,1)}, u32[]{:S(2)}, u32[]{:S(2)}) collective-permute-start(bf16[384,2048]{1,0:T(8,128)(2,1)} %bitcast.29), channel_id=1, source_target_pairs={{0,512},{512,0},{1,513},{513,1},{2,514},{514,2},{3,515},{515,3},{4... | collective-permute-start | bytes 4718600 | tf_op jit(solution)/shard_map/ppermute | solution.py:169
  35.2 7.8 %collective-permute-start.1 = (bf16[256,256]{1,0:T(8,128)(2,1)S(1)}, bf16[256,256]{1,0:T(8,128)(2,1)S(1)}, u32[]{:S(2)}, u32[]{:S(2)}) collective-permute-start(bf16[256,256]{1,0:T(8,128)(2,1)S(1)} %fusion.2), channel_id=1, source_target_pairs={{0,64},{64,0},{1,65},{65,1},{2,66},{66,2},{3,67},{67,3},{4,68},{68... | collective-permute-start | bytes 393224 | tf_op jit(solution)/shard_map/ppermute | solution.py:177
  62.2 22.2 %all-to-all-start.1 = ((bf16[64,8,512]{2,1,0:T(8,128)(2,1)}), bf16[64,8,512]{2,1,0:T(8,128)(2,1)S(1)}, u32[]{:S(2)}, u32[]{:S(2)}) async-start(bf16[64,8,512]{2,1,0:T(8,128)(2,1)} %bitcast.10), calls=%async_computation.1 | async-start | bytes 1048576 | tf_op jit(solution)/shard_map/all_to_all | solution.py:173
  68.5 15.8 %collective-permute-start.5 = (bf16[256,256]{1,0:T(8,128)(2,1)S(1)}, bf16[256,256]{1,0:T(8,128)(2,1)S(1)}, u32[]{:S(2)}, u32[]{:S(2)}) collective-permute-start(bf16[256,256]{1,0:T(8,128)(2,1)S(1)} %pad_maximum_fusion.4), channel_id=1, source_target_pairs={{0,16},{16,0},{32,48},{48,32},{1,17},{17,1},{33,49},{49,33},{2,18}... | collective-permute-start | bytes 393224 | tf_op jit(solution)/shard_map/ppermute | solution.py:177
  84.6 3.1 %collective-permute-start.6 = (f32[2,16,512]{2,1,0:T(8,128)S(1)}, f32[2,16,512]{2,1,0:T(8,128)S(1)}, u32[]{:S(2)}, u32[]{:S(2)}) collective-permute-start(f32[2,16,512]{2,1,0:T(8,128)S(1)} %get-tuple-element.30), channel_id=1, source_target_pairs={{0,512},{512,0},{1,513},{513,1},{2,514},{514,2},{3,515},{515,3},{4... | collective-permute-start | bytes 196616 | tf_op jit(solution)/shard_map/ppermute | solution.py:169
  88.4 8.9 %collective-permute-start.7 = (bf16[16,512]{1,0:T(8,128)(2,1)S(1)}, bf16[16,512]{1,0:T(8,128)(2,1)S(1)}, u32[]{:S(2)}, u32[]{:S(2)}) collective-permute-start(bf16[16,512]{1,0:T(8,128)(2,1)S(1)} %get-tuple-element.29), channel_id=1, source_target_pairs={{0,64},{64,0},{1,65},{65,1},{2,66},{66,2},{3,67},{67,3},{4,68},{68... | collective-permute-start | bytes 49160 | tf_op jit(solution)/shard_map/ppermute | solution.py:177

commit v8 on v7

--- a/solution.py
+++ b/solution.py
@@ -98,17 +98,17 @@
 
 def product_kernel(place_ref, *refs):
     contexts, tokens_ref, out_ref = refs[:-2], refs[-2], refs[-1]
-    peers, depth, width = tokens_ref.shape
-    tok = depth // len(contexts)
+    peers, tok, width = tokens_ref.shape
+    peers //= len(contexts)
+    yh_index, zl_index = place_ref[0], place_ref[1]
     total = None
-    for i, ref in enumerate(contexts):
-        tokens = tokens_ref[:, i * tok:(i + 1) * tok, :].reshape(peers * tok, width)
-        term = dot_f32(ref[...], tokens)
+    for apart, ref in enumerate(contexts):
+        tokens = tokens_ref[pl.ds(jnp.bitwise_xor(zl_index, apart) * peers, peers)]
+        term = dot_f32(ref[...], tokens.reshape(peers * tok, width))
         total = term if total is None else total + term
     blocks, heads, cols = out_ref.shape
     z_blocks = width // cols
     y_blocks = blocks // z_blocks
-    yh_index = place_ref[0]
     for z in range(z_blocks):
         for apart in range(y_blocks):
             out_ref[jnp.bitwise_xor(yh_index, apart) * z_blocks + z] = total[
@@ -116,7 +116,7 @@
             ].astype(BF)
 
 
-def context_product(yh_index, contexts, tokens_b, y_blocks, z_blocks):
+def context_product(place, contexts, tokens_b, y_blocks, z_blocks):
     rows, depth = contexts[0].shape
     width = tokens_b.shape[2]
     return pl.pallas_call(
@@ -132,37 +132,42 @@
             transcendentals=0,
         ),
         name="context_product",
-    )(yh_index.astype(jnp.int32).reshape(1), *contexts, tokens_b)
-
-
-def finish_kernel(zl_ref, mine_ref, came_ref, grad_ref, hidden_ref, keep_ref, send_ref):
+    )(place, *contexts, tokens_b)
+
+
+def finish_kernel(mine_ref, came_ref, grad_ref, hidden_ref, spread_ref):
     parts, _, width = mine_ref.shape
     for i in range(parts):
         at = slice(i * width, (i + 1) * width)
         hidden_ref[:, at] = grad_ref[:, at].astype(F32) + (mine_ref[i] + came_ref[i])
-    first = zl_ref[0] == 0
-    cols = hidden_ref.shape[1] // (2 * Z_BLOCKS)
+    blocks, _, held = spread_ref.shape
+    cols = held // Z_BLOCKS
+    pair = hidden_ref.shape[1] // held
     for z in range(Z_BLOCKS):
-        even = hidden_ref[:, 2 * z * cols:(2 * z + 1) * cols]
-        odd = hidden_ref[:, (2 * z + 1) * cols:(2 * z + 2) * cols]
-        at = slice(z * cols, (z + 1) * cols)
-        keep_ref[:, at] = jnp.where(first, even, odd).astype(BF)
-        send_ref[:, at] = jnp.where(first, odd, even).astype(BF)
-
-
-def finish(zl_index, mine, came, grad_half):
+        for of in range(pair):
+            at = (pair * z + of) * cols
+            rounded = hidden_ref[:, at:at + cols].astype(BF)
+            for peer in range(blocks // pair):
+                spread_ref[of * (blocks // pair) + peer, :, z * cols:(z + 1) * cols] = rounded
+
+
+def finish(mine, came, grad_half, peers):
     tok, width = grad_half.shape
     vmem = pl.BlockSpec(memory_space=pltpu.VMEM)
-    half = jax.ShapeDtypeStruct((tok, width // 2), BF)
     return pl.pallas_call(
         finish_kernel,
-        out_shape=(jax.ShapeDtypeStruct((tok, width), F32), half, half),
-        in_specs=[pl.BlockSpec(memory_space=pltpu.SMEM)] + [vmem] * 3,
-        out_specs=(vmem,) * 3,
+        out_shape=(
+            jax.ShapeDtypeStruct((tok, width), F32),
+            jax.ShapeDtypeStruct((2 * peers, tok, width // 2), BF),
+        ),
+        in_specs=[vmem] * 3,
+        out_specs=(vmem,) * 2,
         compiler_params=pltpu.CompilerParams(vmem_limit_bytes=8 * 2**20),
-        cost_estimate=pl.CostEstimate(flops=3 * tok * width, bytes_accessed=16 * tok * width, transcendentals=0),
+        cost_estimate=pl.CostEstimate(
+            flops=3 * tok * width, bytes_accessed=(16 + 2 * peers) * tok * width, transcendentals=0
+        ),
         name="finish",
-    )(zl_index.astype(jnp.int32).reshape(1), mine, came, grad_half)
+    )(mine, came, grad_half)
 
 
 def swap_pool(value):
@@ -232,7 +237,7 @@
     )
     send = dot_f32(spread, stacked).astype(BF).reshape(experts, ROWS, piece_width)
     heads = context_t.shape[0]
-    [places] = swap_places([context_blocks(context_t, yh_index, y_blocks)], 2)
+    [places] = swap_places([context_blocks(context_t, yh_index, y_blocks)], 1)
     send, weights, places = lax.optimization_barrier((send, weights, places))
     received = exchange(send, plane)
     other_gate, other_up, other_down = swap_pool(w_gate[0]), swap_pool(w_up[0]), swap_pool(w_down[0])
@@ -248,7 +253,7 @@
         back_width,
     ).reshape(experts, ROWS, back_width)
     returned = exchange(back, plane)
-    contexts = [jnp.concatenate(piece, axis=0) for piece in swap_places(pieces, 1)]
+    contexts = [jnp.concatenate(piece, axis=0) for piece in swap_places(pieces, 2)]
     returned, contexts = lax.optimization_barrier((returned, contexts))
 
     high = lax.reduce_precision(weights, 8, 7).astype(BF)
@@ -264,11 +269,11 @@
     mine = lax.dynamic_slice_in_dim(mixed, pool_index * per_half, per_half, 0)
     theirs = lax.dynamic_slice_in_dim(mixed, (1 - pool_index) * per_half, per_half, 0)
     grad_half = lax.dynamic_slice_in_dim(out_grad, pool_index * half_width, half_width, 1)
-    hidden_grad, keep, give = finish(zl_index, mine, swap_pool(theirs), grad_half)
-    pair = jnp.concatenate((keep, swapped(give, "zl", 2, 1)), axis=0)
-    gathered_b = exchange(jnp.broadcast_to(pair[None], (peers, *pair.shape)), ("yl", "x"))
+    hidden_grad, columns = finish(mine, swap_pool(theirs), grad_half, peers)
+    gathered_b = exchange(columns, ("zl", "yl", "x"))
+    place = jnp.stack([yh_index, zl_index]).astype(jnp.int32)
     terms = exchange(
-        context_product(yh_index, contexts, gathered_b, y_blocks, z_blocks), ("yh", "zh")
+        context_product(place, contexts, gathered_b, y_blocks, z_blocks), ("yh", "zh")
     )
     wo_grad = jnp.sum(terms.astype(F32), axis=0)
     return (hidden_grad, wo_grad)

time: 151 us -> 152 us (level)
  blocking collectives: 52.3 us -> 29.5 us
  waiting for transfers between devices: 30.1 us -> 46.1 us
  starting transfers between devices: 51.9 us -> 58.3 us
    all_to_all x2 -> x1, blocking collectives: 52.3 us -> 29.5 us  [exchange(): return lax.all_to_all(value, axes, split_axis=0, concat_axis=0, tiled=True)]
    all_to_all x2 -> x3, waiting for transfers between devices: 11 us -> 29.6 us  [exchange(): return lax.all_to_all(value, axes, split_axis=0, concat_axis=0, tiled=True)]
    all_to_all x2 -> x3, starting transfers between devices: 21.5 us -> 35.5 us  [exchange(): return lax.all_to_all(value, axes, split_axis=0, concat_axis=0, tiled=True)]
    ppermute x4 -> x3, starting transfers between devices: 22.2 us -> 14.6 us  [swapped(): return lax.ppermute(value, axis, tuple(((s, s ^ bit) for s in range(size))))]
    ppermute x4 -> x3, waiting for transfers between devices: 17.9 us -> 15.2 us  [swapped(): return lax.ppermute(value, axis, tuple(((s, s ^ bit) for s in range(size))))]
where the time goes in v8:
time: 152 us; the launch traced here: 151 us
  starting transfers between devices  58.3 us (38%)
  waiting for transfers between devices  46.1 us (30%)
  blocking collectives  29.5 us (19%)
  Pallas kernels  9.85 us (6%)
  local copies, waits for them, and re-layouts  2.86 us (2%)
  other arithmetic  1.76 us (1%)
  matrix products  1.64 us (1%)
    all_to_all x3, starting transfers between devices, exchange(): return lax.all_to_all(value, axes, split_axis=0, concat_axis=0, tiled=True)  35.5 us
    all_to_all x3, waiting for transfers between devices, exchange(): return lax.all_to_all(value, axes, split_axis=0, concat_axis=0, tiled=True)  29.6 us
    all_to_all x1, blocking collectives, exchange(): return lax.all_to_all(value, axes, split_axis=0, concat_axis=0, tiled=True)  29.5 us
    ppermute x3, waiting for transfers between devices, swapped(): return lax.ppermute(value, axis, tuple(((s, s ^ bit) for s in range(size))))  15.2 us
    ppermute x3, starting transfers between devices, swapped(): return lax.ppermute(value, axis, tuple(((s, s ^ bit) for s in range(size))))  14.6 us
    ppermute x4, starting transfers between devices, swap_pool(): return lax.ppermute(value, 'pool', ((0, 1), (1, 0)))  8.18 us
    pallas_call x1, Pallas kernels, expert_rows(): pl.pallas_call(expert_kernel, out_shape=jax.ShapeDtypeStruct((slots * wid...  8.1 us
  transfers between devices with their start and end apart: 10, of which 5 were waited for; matrix products, arithmetic and copies ran while one was open for 3% of the time, Pallas kernels for 0%

profile of v8, /device:TPU:2, one launch (start us, length us, event | category | flops | bytes accessed | tf_op | source)
XLA Modules:
  0.0 151.0 jit_solution(16794158491077746521)
XLA Ops:
  0.6 0.0 copy-start.3
  0.6 0.0 copy-start.2
  0.7 0.0 copy-start.1
  0.7 0.9 constant_dynamic-slice_fusion.3
  1.6 4.7 %collective-permute-start = (bf16[128,256]{1,0:T(8,128)(2,1)S(1)}, bf16[128,256]{1,0:T(8,128)(2,1)S(1)}, u32[]{:S(2)}, u32[]{:S(2)}) collective-permute-start(bf16[128,256]{1,0:T(8,128)(2,1)S(1)} %pad_maximum_fusion.5), channel_id=1, source_target_pairs={{0,16},{16,0},{32,48},{48,32},{1,17},{17,1},{33,49},{49,33},{2,18}... | collective-permute-start | bytes 196616 | tf_op jit(solution)/shard_map/ppermute | solution.py:182
  6.3 0.8 copy.23
  7.1 0.1 eq.52
  7.2 0.1 fusion.13
  7.3 0.2 reduce_window_sum.11
  7.4 0.2 select_reduce_fusion.1
  7.6 0.1 reduce_sum.39
  7.7 0.1 fusion.12
  7.8 0.1 copy.25
  8.0 0.3 broadcast_multiply_fusion
  8.2 0.3 mul.77
  8.5 0.0 copy-done.3
  8.5 0.1 copy.26
  8.6 0.0 copy-done.2
  8.6 0.0 copy-done.1
  8.6 0.0 copy-start
  8.6 1.4 fusion
  10.1 0.1 select_reduce_fusion
  10.2 0.0 collective-permute-done
  10.2 15.7 %all-to-all-start = ((bf16[64,8,1024]{2,1,0:T(8,128)(2,1)}), bf16[64,8,1024]{2,1,0:T(8,128)(2,1)S(1)}, u32[]{:S(2)}, u32[]{:S(2)}) async-start(bf16[64,8,1024]{2,1,0:T(8,128)(2,1)} %fusion), calls=%async_computation | async-start | bytes 2097152 | tf_op jit(solution)/shard_map/all_to_all | solution.py:178
  25.9 0.0 copy-done
  25.9 1.9 %collective-permute-start.2 = (bf16[2048,384]{1,0:T(8,128)(2,1)S(1)}, bf16[2048,384]{1,0:T(8,128)(2,1)}, u32[]{:S(2)}, u32[]{:S(2)}) collective-permute-start(bf16[2048,384]{1,0:T(8,128)(2,1)S(1)} %bitcast.25), channel_id=1, source_target_pairs={{0,512},{512,0},{1,513},{513,1},{2,514},{514,2},{3,515},{515,3},{4... | collective-permute-start | bytes 4718600 | tf_op jit(solution)/shard_map/ppermute | solution.py:174
  27.8 2.4 %collective-permute-start.3 = (bf16[2048,384]{1,0:T(8,128)(2,1)}, bf16[2048,384]{1,0:T(8,128)(2,1)}, u32[]{:S(2)}, u32[]{:S(2)}) collective-permute-start(bf16[2048,384]{1,0:T(8,128)(2,1)} %bitcast.27), channel_id=1, source_target_pairs={{0,512},{512,0},{1,513},{513,1},{2,514},{514,2},{3,515},{515,3},{4... | collective-permute-start | bytes 4718600 | tf_op jit(solution)/shard_map/ppermute | solution.py:174
  30.3 1.9 %collective-permute-start.4 = (bf16[384,2048]{1,0:T(8,128)(2,1)}, bf16[384,2048]{1,0:T(8,128)(2,1)}, u32[]{:S(2)}, u32[]{:S(2)}) collective-permute-start(bf16[384,2048]{1,0:T(8,128)(2,1)} %bitcast.29), channel_id=1, source_target_pairs={{0,512},{512,0},{1,513},{513,1},{2,514},{514,2},{3,515},{515,3},{4... | collective-permute-start | bytes 4718600 | tf_op jit(solution)/shard_map/ppermute | solution.py:174
  32.2 2.5 %collective-permute-start.1 = (bf16[256,256]{1,0:T(8,128)(2,1)S(1)}, bf16[256,256]{1,0:T(8,128)(2,1)S(1)}, u32[]{:S(2)}, u32[]{:S(2)}) collective-permute-start(bf16[256,256]{1,0:T(8,128)(2,1)S(1)} %pad_maximum_fusion), channel_id=1, source_target_pairs={{0,64},{64,0},{1,65},{65,1},{2,66},{66,2},{3,67},{67,3},{4,68},{68... | collective-permute-start | bytes 393224 | tf_op jit(solution)/shard_map/ppermute | solution.py:182
  34.7 0.2 mul.86
  34.9 5.1 %collective-permute-done.1 = bf16[256,256]{1,0:T(8,128)(2,1)S(1)} collective-permute-done((bf16[256,256]{1,0:T(8,128)(2,1)S(1)}, bf16[256,256]{1,0:T(8,128)(2,1)S(1)}, u32[]{:S(2)}, u32[]{:S(2)}) %collective-permute-start.1) | collective-permute-done | bytes 131104 | tf_op jit(solution)/shard_map/ppermute | solution.py:182
  40.0 12.9 %all-to-all-done = bf16[64,8,1024]{2,1,0:T(8,128)(2,1)S(1)} async-done(((bf16[64,8,1024]{2,1,0:T(8,128)(2,1)}), bf16[64,8,1024]{2,1,0:T(8,128)(2,1)S(1)}, u32[]{:S(2)}, u32[]{:S(2)}) %all-to-all-start) | async-done | bytes 1048608 | tf_op jit(solution)/shard_map/all_to_all | solution.py:178
  52.9 0.0 collective-permute-done.2.refs_3_
  52.9 0.0 collective-permute-done.3.refs_4_
  52.9 0.0 collective-permute-done.4.refs_5_
  52.9 8.1 %expert.1 = bf16[512,512]{1,0:T(8,128)(2,1)} custom-call(bf16[512,1024]{1,0:T(8,128)(2,1)S(1)} %bitcast.24, bf16[2048,384]{1,0:T(8,128)(2,1)S(1)} %bitcast.26, bf16[2048,384]{1,0:T(8,128)(2,1)} %bitcast.28, bf16[384,2048]{1,0:T(8,128)(2,1)} %bitcast.30, bf16[2048,384]{1,0:T(8,128)(2,1)} %collective-permute-done.2.refs_3_, ...), custom_call_target="tpu_custom_call" | custom-call | flops 2013265920 | bytes 9437184 | tf_op jit(solution)/shard_map/expert/pallas_call | solution.py:83
  61.0 6.3 %all-to-all-start.1 = ((bf16[64,8,512]{2,1,0:T(8,128)(2,1)}), bf16[64,8,512]{2,1,0:T(8,128)(2,1)S(1)}, u32[]{:S(2)}, u32[]{:S(2)}) async-start(bf16[64,8,512]{2,1,0:T(8,128)(2,1)} %bitcast.9), calls=%async_computation.1 | async-start | bytes 1048576 | tf_op jit(solution)/shard_map/all_to_all | solution.py:178
  67.4 7.4 %collective-permute-start.5 = (bf16[256,256]{1,0:T(8,128)(2,1)S(1)}, bf16[256,256]{1,0:T(8,128)(2,1)S(1)}, u32[]{:S(2)}, u32[]{:S(2)}) collective-permute-start(bf16[256,256]{1,0:T(8,128)(2,1)S(1)} %pad_maximum_fusion.2), channel_id=1, source_target_pairs={{0,32},{16,48},{32,0},{48,16},{1,33},{17,49},{33,1},{49,17},{2,34}... | collective-permute-start | bytes 393224 | tf_op jit(solution)/shard_map/ppermute | solution.py:182
  74.8 0.1 copy.27
  74.9 0.1 mul.82
  75.0 0.1 copy.28
  75.1 10.1 %collective-permute-done.5 = bf16[256,256]{1,0:T(8,128)(2,1)S(1)} collective-permute-done((bf16[256,256]{1,0:T(8,128)(2,1)S(1)}, bf16[256,256]{1,0:T(8,128)(2,1)S(1)}, u32[]{:S(2)}, u32[]{:S(2)}) %collective-permute-start.5) | collective-permute-done | bytes 131104 | tf_op jit(solution)/shard_map/ppermute | solution.py:182
  85.2 0.0 all-to-all-done.1
  85.2 0.2 convolution_reduce_fusion
  85.5 1.9 %collective-permute-start.6 = (f32[2,16,512]{2,1,0:T(8,128)S(1)}, f32[2,16,512]{2,1,0:T(8,128)S(1)}, u32[]{:S(2)}, u32[]{:S(2)}) collective-permute-start(f32[2,16,512]{2,1,0:T(8,128)S(1)} %get-tuple-element.28), channel_id=1, source_target_pairs={{0,512},{512,0},{1,513},{513,1},{2,514},{514,2},{3,515},{515,3},{4... | collective-permute-start | bytes 196616 | tf_op jit(solution)/shard_map/ppermute | solution.py:174
  87.4 1.2 collective-permute-done.6.came_ref
  88.6 0.9 finish.1
  89.5 13.6 %all-to-all-start.2 = ((bf16[32,16,512]{2,1,0:T(8,128)(2,1)}), bf16[32,16,512]{2,1,0:T(8,128)(2,1)S(1)}, u32[]{:S(2)}, u32[]{:S(2)}) async-start(bf16[32,16,512]{2,1,0:T(8,128)(2,1)} %get-tuple-element.27), calls=%async_computation.2 | async-start | bytes 1048576 | tf_op jit(solution)/shard_map/all_to_all | solution.py:178
  103.1 0.1 pad_add_fusion.place_ref
  103.2 16.7 %all-to-all-done.2.refs_2_ = bf16[32,16,512]{2,1,0:T(8,128)(2,1)S(1)} async-done(((bf16[32,16,512]{2,1,0:T(8,128)(2,1)}), bf16[32,16,512]{2,1,0:T(8,128)(2,1)S(1)}, u32[]{:S(2)}, u32[]{:S(2)}) %all-to-all-start.2) | async-done | bytes 524320 | tf_op jit(solution)/shard_map/all_to_all | solution.py:178
  119.9 0.9 context_product.1
  120.8 29.5 %all_to_all.20 = bf16[16,64,128]{2,1,0:T(8,128)(2,1)S(1)} all-to-all(bf16[16,64,128]{2,1,0:T(8,128)(2,1)S(1)} %context_product.1), channel_id=1, replica_groups=mesh['pool'=2,'zh'=4,'zl'=2,'yh'=4,'yl'=2,'x'=8] {'yh','zh'}, dimensions={0} | all-to-all | bytes 524288 | tf_op jit(solution)/shard_map/all_to_all | solution.py:178
  150.3 0.7 convert_reduce_fusion
  (16 shorter events, 0.2 us)
Async XLA Ops:
  0.6 7.9 %copy-start.3 = (f32[16,8]{0,1:T(8,128)S(1)}, f32[16,8]{0,1:T(8,128)}, u32[]{:S(2)}) copy-start(f32[16,8]{0,1:T(8,128)} %param.10) | copy-start | bytes 1540
  0.6 8.0 %copy-start.2 = (bf16[16,2048]{1,0:T(8,128)(2,1)S(1)}, bf16[16,2048]{1,0:T(8,128)(2,1)}, u32[]{:S(2)}) copy-start(bf16[16,2048]{1,0:T(8,128)(2,1)} %param.8) | copy-start | bytes 196612
  0.7 8.0 %copy-start.1 = (bf16[16,2048]{1,0:T(8,128)(2,1)S(1)}, bf16[16,2048]{1,0:T(8,128)(2,1)}, u32[]{:S(2)}) copy-start(bf16[16,2048]{1,0:T(8,128)(2,1)} %param.9) | copy-start | bytes 196612
  1.6 8.6 %collective-permute-start = (bf16[128,256]{1,0:T(8,128)(2,1)S(1)}, bf16[128,256]{1,0:T(8,128)(2,1)S(1)}, u32[]{:S(2)}, u32[]{:S(2)}) collective-permute-start(bf16[128,256]{1,0:T(8,128)(2,1)S(1)} %pad_maximum_fusion.5), channel_id=1, source_target_pairs={{0,16},{16,0},{32,48},{48,32},{1,17},{17,1},{33,49},{49,33},{2,18}... | collective-permute-start | bytes 196616 | tf_op jit(solution)/shard_map/ppermute | solution.py:182
  8.6 17.3 %copy-start = (bf16[1,2048,384]{2,1,0:T(8,128)(2,1)S(1)}, bf16[1,2048,384]{2,1,0:T(8,128)(2,1)}, u32[]{:S(2)}) copy-start(bf16[1,2048,384]{2,1,0:T(8,128)(2,1)} %param.12) | copy-start | bytes 4718596
  10.2 42.7 %all-to-all-start = ((bf16[64,8,1024]{2,1,0:T(8,128)(2,1)}), bf16[64,8,1024]{2,1,0:T(8,128)(2,1)S(1)}, u32[]{:S(2)}, u32[]{:S(2)}) async-start(bf16[64,8,1024]{2,1,0:T(8,128)(2,1)} %fusion), calls=%async_computation | async-start | bytes 2097152 | tf_op jit(solution)/shard_map/all_to_all | solution.py:178
  25.9 27.0 %collective-permute-start.2 = (bf16[2048,384]{1,0:T(8,128)(2,1)S(1)}, bf16[2048,384]{1,0:T(8,128)(2,1)}, u32[]{:S(2)}, u32[]{:S(2)}) collective-permute-start(bf16[2048,384]{1,0:T(8,128)(2,1)S(1)} %bitcast.25), channel_id=1, source_target_pairs={{0,512},{512,0},{1,513},{513,1},{2,514},{514,2},{3,515},{515,3},{4... | collective-permute-start | bytes 4718600 | tf_op jit(solution)/shard_map/ppermute | solution.py:174
  27.8 25.1 %collective-permute-start.3 = (bf16[2048,384]{1,0:T(8,128)(2,1)}, bf16[2048,384]{1,0:T(8,128)(2,1)}, u32[]{:S(2)}, u32[]{:S(2)}) collective-permute-start(bf16[2048,384]{1,0:T(8,128)(2,1)} %bitcast.27), channel_id=1, source_target_pairs={{0,512},{512,0},{1,513},{513,1},{2,514},{514,2},{3,515},{515,3},{4... | collective-permute-start | bytes 4718600 | tf_op jit(solution)/shard_map/ppermute | solution.py:174
  30.3 22.7 %collective-permute-start.4 = (bf16[384,2048]{1,0:T(8,128)(2,1)}, bf16[384,2048]{1,0:T(8,128)(2,1)}, u32[]{:S(2)}, u32[]{:S(2)}) collective-permute-start(bf16[384,2048]{1,0:T(8,128)(2,1)} %bitcast.29), channel_id=1, source_target_pairs={{0,512},{512,0},{1,513},{513,1},{2,514},{514,2},{3,515},{515,3},{4... | collective-permute-start | bytes 4718600 | tf_op jit(solution)/shard_map/ppermute | solution.py:174
  32.2 7.8 %collective-permute-start.1 = (bf16[256,256]{1,0:T(8,128)(2,1)S(1)}, bf16[256,256]{1,0:T(8,128)(2,1)S(1)}, u32[]{:S(2)}, u32[]{:S(2)}) collective-permute-start(bf16[256,256]{1,0:T(8,128)(2,1)S(1)} %pad_maximum_fusion), channel_id=1, source_target_pairs={{0,64},{64,0},{1,65},{65,1},{2,66},{66,2},{3,67},{67,3},{4,68},{68... | collective-permute-start | bytes 393224 | tf_op jit(solution)/shard_map/ppermute | solution.py:182
  61.0 24.2 %all-to-all-start.1 = ((bf16[64,8,512]{2,1,0:T(8,128)(2,1)}), bf16[64,8,512]{2,1,0:T(8,128)(2,1)S(1)}, u32[]{:S(2)}, u32[]{:S(2)}) async-start(bf16[64,8,512]{2,1,0:T(8,128)(2,1)} %bitcast.9), calls=%async_computation.1 | async-start | bytes 1048576 | tf_op jit(solution)/shard_map/all_to_all | solution.py:178
  67.4 17.8 %collective-permute-start.5 = (bf16[256,256]{1,0:T(8,128)(2,1)S(1)}, bf16[256,256]{1,0:T(8,128)(2,1)S(1)}, u32[]{:S(2)}, u32[]{:S(2)}) collective-permute-start(bf16[256,256]{1,0:T(8,128)(2,1)S(1)} %pad_maximum_fusion.2), channel_id=1, source_target_pairs={{0,32},{16,48},{32,0},{48,16},{1,33},{17,49},{33,1},{49,17},{2,34}... | collective-permute-start | bytes 393224 | tf_op jit(solution)/shard_map/ppermute | solution.py:182
  85.5 3.1 %collective-permute-start.6 = (f32[2,16,512]{2,1,0:T(8,128)S(1)}, f32[2,16,512]{2,1,0:T(8,128)S(1)}, u32[]{:S(2)}, u32[]{:S(2)}) collective-permute-start(f32[2,16,512]{2,1,0:T(8,128)S(1)} %get-tuple-element.28), channel_id=1, source_target_pairs={{0,512},{512,0},{1,513},{513,1},{2,514},{514,2},{3,515},{515,3},{4... | collective-permute-start | bytes 196616 | tf_op jit(solution)/shard_map/ppermute | solution.py:174
  89.5 30.4 %all-to-all-start.2 = ((bf16[32,16,512]{2,1,0:T(8,128)(2,1)}), bf16[32,16,512]{2,1,0:T(8,128)(2,1)S(1)}, u32[]{:S(2)}, u32[]{:S(2)}) async-start(bf16[32,16,512]{2,1,0:T(8,128)(2,1)} %get-tuple-element.27), calls=%async_computation.2 | async-start | bytes 1048576 | tf_op jit(solution)/shard_map/all_to_all | solution.py:178

commit v9 on v8

--- a/solution.py
+++ b/solution.py
@@ -236,14 +236,11 @@
         experts * ROWS, parts * tok_rows
     )
     send = dot_f32(spread, stacked).astype(BF).reshape(experts, ROWS, piece_width)
-    heads = context_t.shape[0]
-    [places] = swap_places([context_blocks(context_t, yh_index, y_blocks)], 1)
-    send, weights, places = lax.optimization_barrier((send, weights, places))
+    send, weights, context_t = lax.optimization_barrier((send, weights, context_t))
     received = exchange(send, plane)
     other_gate, other_up, other_down = swap_pool(w_gate[0]), swap_pool(w_up[0]), swap_pool(w_down[0])
-    beside = swapped(jnp.concatenate(places, axis=0), "zl", 2, 1)
+    beside = swapped(context_t, "zl", 2, 1)
     received, beside = lax.optimization_barrier((received, beside))
-    pieces = [places, [beside[r * heads:(r + 1) * heads] for r in range(y_blocks)]]
 
     back_width = model_width * own_slots // ROWS
     back_parts = model_width // back_width
@@ -253,8 +250,9 @@
         back_width,
     ).reshape(experts, ROWS, back_width)
     returned = exchange(back, plane)
-    contexts = [jnp.concatenate(piece, axis=0) for piece in swap_places(pieces, 2)]
-    returned, contexts = lax.optimization_barrier((returned, contexts))
+    pieces = [context_blocks(piece, yh_index, y_blocks) for piece in (context_t, beside)]
+    pieces = swap_places(pieces, 1)
+    returned, pieces = lax.optimization_barrier((returned, pieces))
 
     high = lax.reduce_precision(weights, 8, 7).astype(BF)
     low = (weights - high.astype(F32)).astype(BF)
@@ -271,6 +269,7 @@
     grad_half = lax.dynamic_slice_in_dim(out_grad, pool_index * half_width, half_width, 1)
     hidden_grad, columns = finish(mine, swap_pool(theirs), grad_half, peers)
     gathered_b = exchange(columns, ("zl", "yl", "x"))
+    contexts = [jnp.concatenate(piece, axis=0) for piece in swap_places(pieces, 2)]
     place = jnp.stack([yh_index, zl_index]).astype(jnp.int32)
     terms = exchange(
         context_product(place, contexts, gathered_b, y_blocks, z_blocks), ("yh", "zh")

time: 152 us -> 148 us (0.974)
  the two profiles are of different devices: /device:TPU:2 before, /device:TPU:16 now
where the time goes in v9:
time: 148 us; the launch traced here: 147 us
  starting transfers between devices  56.7 us (38%)
  waiting for transfers between devices  41.3 us (28%)
  blocking collectives  32.6 us (22%)
  Pallas kernels  9.87 us (7%)
  local copies, waits for them, and re-layouts  2.1 us (1%)
  other arithmetic  1.75 us (1%)
  matrix products  1.64 us (1%)
    all_to_all x3, starting transfers between devices, exchange(): return lax.all_to_all(value, axes, split_axis=0, concat_axis=0, tiled=True)  37.2 us
    all_to_all x1, blocking collectives, exchange(): return lax.all_to_all(value, axes, split_axis=0, concat_axis=0, tiled=True)  32.6 us
    ppermute x3, waiting for transfers between devices, swapped(): return lax.ppermute(value, axis, tuple(((s, s ^ bit) for s in range(size))))  28.6 us
    all_to_all x3, waiting for transfers between devices, exchange(): return lax.all_to_all(value, axes, split_axis=0, concat_axis=0, tiled=True)  11.5 us
    ppermute x3, starting transfers between devices, swapped(): return lax.ppermute(value, axis, tuple(((s, s ^ bit) for s in range(size))))  11.3 us
    ppermute x4, starting transfers between devices, swap_pool(): return lax.ppermute(value, 'pool', ((0, 1), (1, 0)))  8.18 us
    pallas_call x1, Pallas kernels, expert_rows(): pl.pallas_call(expert_kernel, out_shape=jax.ShapeDtypeStruct((slots * wid...  8.1 us
  transfers between devices with their start and end apart: 10, of which 6 were waited for; matrix products, arithmetic and copies ran while one was open for 0% of the time, Pallas kernels for 0%

profile of v9, /device:TPU:16, one launch (start us, length us, event | category | flops | bytes accessed | tf_op | source)
XLA Modules:
  0.0 147.0 jit_solution(5337610840099757979)
XLA Ops:
  0.6 0.0 copy-start.4
  0.6 0.0 copy-start.1
  0.6 0.0 copy-start.3
  0.7 0.8 copy.23
  1.5 0.1 eq.52
  1.6 0.1 fusion.13
  1.7 0.2 reduce_window_sum.11
  1.8 0.2 select_reduce_fusion.1
  2.0 0.1 reduce_sum.39
  2.1 0.1 fusion.12
  2.2 0.1 copy.25
  2.4 0.3 broadcast_multiply_fusion
  2.6 0.3 mul.81
  2.9 0.0 copy-done.4
  2.9 0.1 copy.26
  3.0 0.1 select_reduce_fusion
  3.1 0.0 copy-done.1
  3.1 0.0 copy-done.3
  3.2 0.0 copy-start
  3.2 0.0 copy-start.2
  3.2 1.4 fusion
  4.6 17.1 %all-to-all-start = ((bf16[64,8,1024]{2,1,0:T(8,128)(2,1)}), bf16[64,8,1024]{2,1,0:T(8,128)(2,1)S(1)}, u32[]{:S(2)}, u32[]{:S(2)}) async-start(bf16[64,8,1024]{2,1,0:T(8,128)(2,1)} %fusion), calls=%async_computation | async-start | bytes 2097152 | tf_op jit(solution)/shard_map/all_to_all | solution.py:178
  21.7 0.0 copy-done
  21.8 1.9 %collective-permute-start.1 = (bf16[2048,384]{1,0:T(8,128)(2,1)S(1)}, bf16[2048,384]{1,0:T(8,128)(2,1)}, u32[]{:S(2)}, u32[]{:S(2)}) collective-permute-start(bf16[2048,384]{1,0:T(8,128)(2,1)S(1)} %bitcast.25), channel_id=1, source_target_pairs={{0,512},{512,0},{1,513},{513,1},{2,514},{514,2},{3,515},{515,3},{4... | collective-permute-start | bytes 4718600 | tf_op jit(solution)/shard_map/ppermute | solution.py:174
  23.7 2.4 %collective-permute-start.2 = (bf16[2048,384]{1,0:T(8,128)(2,1)}, bf16[2048,384]{1,0:T(8,128)(2,1)}, u32[]{:S(2)}, u32[]{:S(2)}) collective-permute-start(bf16[2048,384]{1,0:T(8,128)(2,1)} %bitcast.27), channel_id=1, source_target_pairs={{0,512},{512,0},{1,513},{513,1},{2,514},{514,2},{3,515},{515,3},{4... | collective-permute-start | bytes 4718600 | tf_op jit(solution)/shard_map/ppermute | solution.py:174
  26.1 1.9 %collective-permute-start.3 = (bf16[384,2048]{1,0:T(8,128)(2,1)}, bf16[384,2048]{1,0:T(8,128)(2,1)}, u32[]{:S(2)}, u32[]{:S(2)}) collective-permute-start(bf16[384,2048]{1,0:T(8,128)(2,1)} %bitcast.29), channel_id=1, source_target_pairs={{0,512},{512,0},{1,513},{513,1},{2,514},{514,2},{3,515},{515,3},{4... | collective-permute-start | bytes 4718600 | tf_op jit(solution)/shard_map/ppermute | solution.py:174
  28.0 0.0 copy-done.2
  28.0 1.9 %collective-permute-start = (bf16[64,1024]{1,0:T(8,128)(2,1)S(1)}, bf16[64,1024]{1,0:T(8,128)(2,1)S(1)}, u32[]{:S(2)}, u32[]{:S(2)}) collective-permute-start(bf16[64,1024]{1,0:T(8,128)(2,1)S(1)} %copy-done.2), channel_id=1, source_target_pairs={{0,64},{64,0},{1,65},{65,1},{2,66},{66,2},{3,67},{67,3},{4,68},{68... | collective-permute-start | bytes 393224 | tf_op jit(solution)/shard_map/ppermute | solution.py:182
  30.0 5.9 %collective-permute-done = bf16[64,1024]{1,0:T(8,128)(2,1)S(1)} collective-permute-done((bf16[64,1024]{1,0:T(8,128)(2,1)S(1)}, bf16[64,1024]{1,0:T(8,128)(2,1)S(1)}, u32[]{:S(2)}, u32[]{:S(2)}) %collective-permute-start) | collective-permute-done | bytes 131104 | tf_op jit(solution)/shard_map/ppermute | solution.py:182
  35.8 11.1 %all-to-all-done = bf16[64,8,1024]{2,1,0:T(8,128)(2,1)S(1)} async-done(((bf16[64,8,1024]{2,1,0:T(8,128)(2,1)}), bf16[64,8,1024]{2,1,0:T(8,128)(2,1)S(1)}, u32[]{:S(2)}, u32[]{:S(2)}) %all-to-all-start) | async-done | bytes 1048608 | tf_op jit(solution)/shard_map/all_to_all | solution.py:178
  47.0 0.0 collective-permute-done.1.refs_3_
  47.0 0.0 collective-permute-done.2.refs_4_
  47.0 0.0 collective-permute-done.3.refs_5_
  47.0 8.1 %expert.1 = bf16[512,512]{1,0:T(8,128)(2,1)} custom-call(bf16[512,1024]{1,0:T(8,128)(2,1)S(1)} %bitcast.24, bf16[2048,384]{1,0:T(8,128)(2,1)S(1)} %bitcast.26, bf16[2048,384]{1,0:T(8,128)(2,1)} %bitcast.28, bf16[384,2048]{1,0:T(8,128)(2,1)} %bitcast.30, bf16[2048,384]{1,0:T(8,128)(2,1)} %collective-permute-done.1.refs_3_, ...), custom_call_target="tpu_custom_call" | custom-call | flops 2013265920 | bytes 9437184 | tf_op jit(solution)/shard_map/expert/pallas_call | solution.py:83
  55.1 7.2 %all-to-all-start.1 = ((bf16[64,8,512]{2,1,0:T(8,128)(2,1)}), bf16[64,8,512]{2,1,0:T(8,128)(2,1)S(1)}, u32[]{:S(2)}, u32[]{:S(2)}) async-start(bf16[64,8,512]{2,1,0:T(8,128)(2,1)} %bitcast.9), calls=%async_computation.1 | async-start | bytes 1048576 | tf_op jit(solution)/shard_map/all_to_all | solution.py:178
  62.4 4.3 %collective-permute-start.4 = (bf16[256,256]{1,0:T(8,128)(2,1)S(1)}, bf16[256,256]{1,0:T(8,128)(2,1)S(1)}, u32[]{:S(2)}, u32[]{:S(2)}) collective-permute-start(bf16[256,256]{1,0:T(8,128)(2,1)S(1)} %pad_maximum_fusion), channel_id=1, source_target_pairs={{0,16},{16,0},{32,48},{48,32},{1,17},{17,1},{33,49},{49,33},{2,18}... | collective-permute-start | bytes 393224 | tf_op jit(solution)/shard_map/ppermute | solution.py:182
  66.8 0.2 mul.86
  67.0 0.1 copy.27
  67.1 0.1 mul.82
  67.2 0.1 copy.28
  67.3 10.7 %collective-permute-done.4 = bf16[256,256]{1,0:T(8,128)(2,1)S(1)} collective-permute-done((bf16[256,256]{1,0:T(8,128)(2,1)S(1)}, bf16[256,256]{1,0:T(8,128)(2,1)S(1)}, u32[]{:S(2)}, u32[]{:S(2)}) %collective-permute-start.4) | collective-permute-done | bytes 131104 | tf_op jit(solution)/shard_map/ppermute | solution.py:182
  78.0 0.3 all-to-all-done.1
  78.3 0.2 convolution_reduce_fusion
  78.5 1.9 %collective-permute-start.5 = (f32[2,16,512]{2,1,0:T(8,128)S(1)}, f32[2,16,512]{2,1,0:T(8,128)S(1)}, u32[]{:S(2)}, u32[]{:S(2)}) collective-permute-start(f32[2,16,512]{2,1,0:T(8,128)S(1)} %get-tuple-element.36), channel_id=1, source_target_pairs={{0,512},{512,0},{1,513},{513,1},{2,514},{514,2},{3,515},{515,3},{4... | collective-permute-start | bytes 196616 | tf_op jit(solution)/shard_map/ppermute | solution.py:174
  80.5 1.2 collective-permute-done.5.came_ref
  81.7 0.9 finish.1
  82.6 12.9 %all-to-all-start.2 = ((bf16[32,16,512]{2,1,0:T(8,128)(2,1)}), bf16[32,16,512]{2,1,0:T(8,128)(2,1)S(1)}, u32[]{:S(2)}, u32[]{:S(2)}) async-start(bf16[32,16,512]{2,1,0:T(8,128)(2,1)} %get-tuple-element.33), calls=%async_computation.2 | async-start | bytes 1048576 | tf_op jit(solution)/shard_map/all_to_all | solution.py:178
  95.5 5.1 %collective-permute-start.6 = (bf16[256,256]{1,0:T(8,128)(2,1)S(1)}, bf16[256,256]{1,0:T(8,128)(2,1)S(1)}, u32[]{:S(2)}, u32[]{:S(2)}) collective-permute-start(bf16[256,256]{1,0:T(8,128)(2,1)S(1)} %pad_maximum_fusion.1), channel_id=1, source_target_pairs={{0,32},{16,48},{32,0},{48,16},{1,33},{17,49},{33,1},{49,17},{2,34}... | collective-permute-start | bytes 393224 | tf_op jit(solution)/shard_map/ppermute | solution.py:182
  100.6 0.1 pad_add_fusion.place_ref
  100.7 12.1 %collective-permute-done.6 = bf16[256,256]{1,0:T(8,128)(2,1)S(1)} collective-permute-done((bf16[256,256]{1,0:T(8,128)(2,1)S(1)}, bf16[256,256]{1,0:T(8,128)(2,1)S(1)}, u32[]{:S(2)}, u32[]{:S(2)}) %collective-permute-start.6) | collective-permute-done | bytes 131104 | tf_op jit(solution)/shard_map/ppermute | solution.py:182
  112.9 0.0 all-to-all-done.2.refs_2_
  112.9 0.9 context_product.1
  113.8 32.6 %all_to_all.20 = bf16[16,64,128]{2,1,0:T(8,128)(2,1)S(1)} all-to-all(bf16[16,64,128]{2,1,0:T(8,128)(2,1)S(1)} %context_product.1), channel_id=1, replica_groups=mesh['pool'=2,'zh'=4,'zl'=2,'yh'=4,'yl'=2,'x'=8] {'yh','zh'}, dimensions={0} | all-to-all | bytes 524288 | tf_op jit(solution)/shard_map/all_to_all | solution.py:178
  146.3 0.7 convert_reduce_fusion
  (16 shorter events, 0.2 us)
Async XLA Ops:
  0.6 2.3 %copy-start.4 = (f32[16,8]{0,1:T(8,128)S(1)}, f32[16,8]{0,1:T(8,128)}, u32[]{:S(2)}) copy-start(f32[16,8]{0,1:T(8,128)} %param.10) | copy-start | bytes 1540
  0.6 2.5 %copy-start.1 = (bf16[16,2048]{1,0:T(8,128)(2,1)S(1)}, bf16[16,2048]{1,0:T(8,128)(2,1)}, u32[]{:S(2)}) copy-start(bf16[16,2048]{1,0:T(8,128)(2,1)} %param.9) | copy-start | bytes 196612
  0.6 2.5 %copy-start.3 = (bf16[16,2048]{1,0:T(8,128)(2,1)S(1)}, bf16[16,2048]{1,0:T(8,128)(2,1)}, u32[]{:S(2)}) copy-start(bf16[16,2048]{1,0:T(8,128)(2,1)} %param.8) | copy-start | bytes 196612
  3.2 18.6 %copy-start = (bf16[1,2048,384]{2,1,0:T(8,128)(2,1)S(1)}, bf16[1,2048,384]{2,1,0:T(8,128)(2,1)}, u32[]{:S(2)}) copy-start(bf16[1,2048,384]{2,1,0:T(8,128)(2,1)} %param.12) | copy-start | bytes 4718596
  3.2 24.9 %copy-start.2 = (bf16[64,1024]{1,0:T(8,128)(2,1)S(1)}, bf16[64,1024]{1,0:T(8,128)(2,1)}, u32[]{:S(2)}) copy-start(bf16[64,1024]{1,0:T(8,128)(2,1)} %param.15) | copy-start | bytes 393220
  4.6 42.4 %all-to-all-start = ((bf16[64,8,1024]{2,1,0:T(8,128)(2,1)}), bf16[64,8,1024]{2,1,0:T(8,128)(2,1)S(1)}, u32[]{:S(2)}, u32[]{:S(2)}) async-start(bf16[64,8,1024]{2,1,0:T(8,128)(2,1)} %fusion), calls=%async_computation | async-start | bytes 2097152 | tf_op jit(solution)/shard_map/all_to_all | solution.py:178
  21.8 25.2 %collective-permute-start.1 = (bf16[2048,384]{1,0:T(8,128)(2,1)S(1)}, bf16[2048,384]{1,0:T(8,128)(2,1)}, u32[]{:S(2)}, u32[]{:S(2)}) collective-permute-start(bf16[2048,384]{1,0:T(8,128)(2,1)S(1)} %bitcast.25), channel_id=1, source_target_pairs={{0,512},{512,0},{1,513},{513,1},{2,514},{514,2},{3,515},{515,3},{4... | collective-permute-start | bytes 4718600 | tf_op jit(solution)/shard_map/ppermute | solution.py:174
  23.7 23.3 %collective-permute-start.2 = (bf16[2048,384]{1,0:T(8,128)(2,1)}, bf16[2048,384]{1,0:T(8,128)(2,1)}, u32[]{:S(2)}, u32[]{:S(2)}) collective-permute-start(bf16[2048,384]{1,0:T(8,128)(2,1)} %bitcast.27), channel_id=1, source_target_pairs={{0,512},{512,0},{1,513},{513,1},{2,514},{514,2},{3,515},{515,3},{4... | collective-permute-start | bytes 4718600 | tf_op jit(solution)/shard_map/ppermute | solution.py:174
  26.1 20.9 %collective-permute-start.3 = (bf16[384,2048]{1,0:T(8,128)(2,1)}, bf16[384,2048]{1,0:T(8,128)(2,1)}, u32[]{:S(2)}, u32[]{:S(2)}) collective-permute-start(bf16[384,2048]{1,0:T(8,128)(2,1)} %bitcast.29), channel_id=1, source_target_pairs={{0,512},{512,0},{1,513},{513,1},{2,514},{514,2},{3,515},{515,3},{4... | collective-permute-start | bytes 4718600 | tf_op jit(solution)/shard_map/ppermute | solution.py:174
  28.0 7.8 %collective-permute-start = (bf16[64,1024]{1,0:T(8,128)(2,1)S(1)}, bf16[64,1024]{1,0:T(8,128)(2,1)S(1)}, u32[]{:S(2)}, u32[]{:S(2)}) collective-permute-start(bf16[64,1024]{1,0:T(8,128)(2,1)S(1)} %copy-done.2), channel_id=1, source_target_pairs={{0,64},{64,0},{1,65},{65,1},{2,66},{66,2},{3,67},{67,3},{4,68},{68... | collective-permute-start | bytes 393224 | tf_op jit(solution)/shard_map/ppermute | solution.py:182
  55.1 23.2 %all-to-all-start.1 = ((bf16[64,8,512]{2,1,0:T(8,128)(2,1)}), bf16[64,8,512]{2,1,0:T(8,128)(2,1)S(1)}, u32[]{:S(2)}, u32[]{:S(2)}) async-start(bf16[64,8,512]{2,1,0:T(8,128)(2,1)} %bitcast.9), calls=%async_computation.1 | async-start | bytes 1048576 | tf_op jit(solution)/shard_map/all_to_all | solution.py:178
  62.4 15.5 %collective-permute-start.4 = (bf16[256,256]{1,0:T(8,128)(2,1)S(1)}, bf16[256,256]{1,0:T(8,128)(2,1)S(1)}, u32[]{:S(2)}, u32[]{:S(2)}) collective-permute-start(bf16[256,256]{1,0:T(8,128)(2,1)S(1)} %pad_maximum_fusion), channel_id=1, source_target_pairs={{0,16},{16,0},{32,48},{48,32},{1,17},{17,1},{33,49},{49,33},{2,18}... | collective-permute-start | bytes 393224 | tf_op jit(solution)/shard_map/ppermute | solution.py:182
  78.5 3.1 %collective-permute-start.5 = (f32[2,16,512]{2,1,0:T(8,128)S(1)}, f32[2,16,512]{2,1,0:T(8,128)S(1)}, u32[]{:S(2)}, u32[]{:S(2)}) collective-permute-start(f32[2,16,512]{2,1,0:T(8,128)S(1)} %get-tuple-element.36), channel_id=1, source_target_pairs={{0,512},{512,0},{1,513},{513,1},{2,514},{514,2},{3,515},{515,3},{4... | collective-permute-start | bytes 196616 | tf_op jit(solution)/shard_map/ppermute | solution.py:174
  82.6 30.3 %all-to-all-start.2 = ((bf16[32,16,512]{2,1,0:T(8,128)(2,1)}), bf16[32,16,512]{2,1,0:T(8,128)(2,1)S(1)}, u32[]{:S(2)}, u32[]{:S(2)}) async-start(bf16[32,16,512]{2,1,0:T(8,128)(2,1)} %get-tuple-element.33), calls=%async_computation.2 | async-start | bytes 1048576 | tf_op jit(solution)/shard_map/all_to_all | solution.py:178
  95.5 17.3 %collective-permute-start.6 = (bf16[256,256]{1,0:T(8,128)(2,1)S(1)}, bf16[256,256]{1,0:T(8,128)(2,1)S(1)}, u32[]{:S(2)}, u32[]{:S(2)}) collective-permute-start(bf16[256,256]{1,0:T(8,128)(2,1)S(1)} %pad_maximum_fusion.1), channel_id=1, source_target_pairs={{0,32},{16,48},{32,0},{48,16},{1,33},{17,49},{33,1},{49,17},{2,34}... | collective-permute-start | bytes 393224 | tf_op jit(solution)/shard_map/ppermute | solution.py:182

commit v10 on v9

--- a/solution.py
+++ b/solution.py
@@ -7,7 +7,7 @@
 
 ROWS = 8
 SORT = 256
-Z_BLOCKS = 4
+Z_BLOCKS = 8
 BF = jnp.bfloat16
 F32 = jnp.float32
 
@@ -158,7 +158,7 @@
         finish_kernel,
         out_shape=(
             jax.ShapeDtypeStruct((tok, width), F32),
-            jax.ShapeDtypeStruct((2 * peers, tok, width // 2), BF),
+            jax.ShapeDtypeStruct((peers, tok, width), BF),
         ),
         in_specs=[vmem] * 3,
         out_specs=(vmem,) * 2,
@@ -239,8 +239,6 @@
     send, weights, context_t = lax.optimization_barrier((send, weights, context_t))
     received = exchange(send, plane)
     other_gate, other_up, other_down = swap_pool(w_gate[0]), swap_pool(w_up[0]), swap_pool(w_down[0])
-    beside = swapped(context_t, "zl", 2, 1)
-    received, beside = lax.optimization_barrier((received, beside))
 
     back_width = model_width * own_slots // ROWS
     back_parts = model_width // back_width
@@ -249,8 +247,9 @@
         (w_gate[0], w_up[0], w_down[0], other_gate, other_up, other_down),
         back_width,
     ).reshape(experts, ROWS, back_width)
+    back, context_t = lax.optimization_barrier((back, context_t))
     returned = exchange(back, plane)
-    pieces = [context_blocks(piece, yh_index, y_blocks) for piece in (context_t, beside)]
+    pieces = [context_blocks(context_t, yh_index, y_blocks)]
     pieces = swap_places(pieces, 1)
     returned, pieces = lax.optimization_barrier((returned, pieces))
 

time: 148 us -> 146 us (0.986)
  the two profiles are of different devices: /device:TPU:16 before, /device:TPU:18 now
where the time goes in v10:
time: 146 us; the launch traced here: 145 us
  starting transfers between devices  47.4 us (32%)
  waiting for transfers between devices  40.2 us (28%)
  blocking collectives  40 us (27%)
  Pallas kernels  9.88 us (7%)
  local copies, waits for them, and re-layouts  3.21 us (2%)
  other arithmetic  1.77 us (1%)
  matrix products  1.64 us (1%)
    all_to_all x1, blocking collectives, exchange(): return lax.all_to_all(value, axes, split_axis=0, concat_axis=0, tiled=True)  40 us
    all_to_all x3, starting transfers between devices, exchange(): return lax.all_to_all(value, axes, split_axis=0, concat_axis=0, tiled=True)  29.9 us
    all_to_all x3, waiting for transfers between devices, exchange(): return lax.all_to_all(value, axes, split_axis=0, concat_axis=0, tiled=True)  21.7 us
    ppermute x2, waiting for transfers between devices, swapped(): return lax.ppermute(value, axis, tuple(((s, s ^ bit) for s in range(size))))  14.6 us
    ppermute x2, starting transfers between devices, swapped(): return lax.ppermute(value, axis, tuple(((s, s ^ bit) for s in range(size))))  9.34 us
    ppermute x4, starting transfers between devices, swap_pool(): return lax.ppermute(value, 'pool', ((0, 1), (1, 0)))  8.17 us
    pallas_call x1, Pallas kernels, expert_rows(): pl.pallas_call(expert_kernel, out_shape=jax.ShapeDtypeStruct((slots * wid...  8.1 us
    ppermute x4, waiting for transfers between devices, swap_pool(): return lax.ppermute(value, 'pool', ((0, 1), (1, 0)))  3.91 us
  transfers between devices with their start and end apart: 9, of which 8 were waited for; matrix products, arithmetic and copies ran while one was open for 0% of the time, Pallas kernels for 0%

profile of v10, /device:TPU:18, one launch (start us, length us, event | category | flops | bytes accessed | tf_op | source)
XLA Modules:
  0.0 145.1 jit_solution(4560066206898079089)
XLA Ops:
  0.6 0.0 copy-start.6
  0.6 0.0 copy-start.5
  0.6 0.0 copy-start.3
  0.7 0.8 copy.23
  1.5 0.1 eq.52
  1.6 0.1 fusion.13
  1.7 0.2 reduce_window_sum.11
  1.8 0.2 select_reduce_fusion.1
  2.0 0.1 reduce_sum.39
  2.1 0.1 fusion.12
  2.2 0.1 copy.25
  2.4 0.3 broadcast_multiply_fusion
  2.6 0.3 mul.77
  2.9 0.0 copy-done.6
  2.9 0.1 copy.26
  3.0 0.1 select_reduce_fusion
  3.1 0.0 copy-done.5
  3.1 0.0 copy-done.3
  3.2 0.0 copy-start
  3.2 1.4 fusion
  4.6 17.1 %all-to-all-start = ((bf16[64,8,1024]{2,1,0:T(8,128)(2,1)}), bf16[64,8,1024]{2,1,0:T(8,128)(2,1)S(1)}, u32[]{:S(2)}, u32[]{:S(2)}) async-start(bf16[64,8,1024]{2,1,0:T(8,128)(2,1)} %fusion), calls=%async_computation | async-start | bytes 2097152 | tf_op jit(solution)/shard_map/all_to_all | solution.py:178
  21.7 0.0 copy-done
  21.7 1.9 %collective-permute-start = (bf16[2048,384]{1,0:T(8,128)(2,1)S(1)}, bf16[2048,384]{1,0:T(8,128)(2,1)S(1)}, u32[]{:S(2)}, u32[]{:S(2)}) collective-permute-start(bf16[2048,384]{1,0:T(8,128)(2,1)S(1)} %bitcast.24), channel_id=1, source_target_pairs={{0,512},{512,0},{1,513},{513,1},{2,514},{514,2},{3,515},{515,3},{4... | collective-permute-start | bytes 4718600 | tf_op jit(solution)/shard_map/ppermute | solution.py:174
  23.7 2.4 %collective-permute-start.1 = (bf16[2048,384]{1,0:T(8,128)(2,1)}, bf16[2048,384]{1,0:T(8,128)(2,1)S(1)}, u32[]{:S(2)}, u32[]{:S(2)}) collective-permute-start(bf16[2048,384]{1,0:T(8,128)(2,1)} %bitcast.26), channel_id=1, source_target_pairs={{0,512},{512,0},{1,513},{513,1},{2,514},{514,2},{3,515},{515,3},{4... | collective-permute-start | bytes 4718600 | tf_op jit(solution)/shard_map/ppermute | solution.py:174
  26.1 1.9 %collective-permute-start.2 = (bf16[384,2048]{1,0:T(8,128)(2,1)}, bf16[384,2048]{1,0:T(8,128)(2,1)}, u32[]{:S(2)}, u32[]{:S(2)}) collective-permute-start(bf16[384,2048]{1,0:T(8,128)(2,1)} %bitcast.28), channel_id=1, source_target_pairs={{0,512},{512,0},{1,513},{513,1},{2,514},{514,2},{3,515},{515,3},{4... | collective-permute-start | bytes 4718600 | tf_op jit(solution)/shard_map/ppermute | solution.py:174
  28.0 0.0 collective-permute-done.refs_3_
  28.0 0.0 copy-start.1
  28.0 1.5 %collective-permute-done.1.refs_4_ = bf16[2048,384]{1,0:T(8,128)(2,1)S(1)} collective-permute-done((bf16[2048,384]{1,0:T(8,128)(2,1)}, bf16[2048,384]{1,0:T(8,128)(2,1)S(1)}, u32[]{:S(2)}, u32[]{:S(2)}) %collective-permute-start.1) | collective-permute-done | bytes 1572896 | tf_op jit(solution)/shard_map/ppermute | solution.py:174
  29.5 0.0 copy-done.1
  29.5 0.0 copy-start.2
  29.5 1.2 copy-done.2
  30.7 1.2 collective-permute-done.2.refs_5_
  31.9 15.0 %all-to-all-done = bf16[64,8,1024]{2,1,0:T(8,128)(2,1)S(1)} async-done(((bf16[64,8,1024]{2,1,0:T(8,128)(2,1)}), bf16[64,8,1024]{2,1,0:T(8,128)(2,1)S(1)}, u32[]{:S(2)}, u32[]{:S(2)}) %all-to-all-start) | async-done | bytes 1048608 | tf_op jit(solution)/shard_map/all_to_all | solution.py:178
  46.9 0.0 copy-start.4
  46.9 8.1 %expert.1 = bf16[512,512]{1,0:T(8,128)(2,1)} custom-call(bf16[512,1024]{1,0:T(8,128)(2,1)S(1)} %bitcast.23, bf16[2048,384]{1,0:T(8,128)(2,1)S(1)} %bitcast.25, bf16[2048,384]{1,0:T(8,128)(2,1)} %bitcast.27, bf16[384,2048]{1,0:T(8,128)(2,1)} %bitcast.29, bf16[2048,384]{1,0:T(8,128)(2,1)} %copy-done.1, bf16[2048,384]{1,0:T(8,128)(2,1)} %copy-done.2, ...), custom_call_target="tpu_custom_call" | custom-call | flops 2013265920 | bytes 9437184 | tf_op jit(solution)/shard_map/expert/pallas_call | solution.py:83
  55.0 7.2 %all-to-all-start.1 = ((bf16[64,8,512]{2,1,0:T(8,128)(2,1)}), bf16[64,8,512]{2,1,0:T(8,128)(2,1)S(1)}, u32[]{:S(2)}, u32[]{:S(2)}) async-start(bf16[64,8,512]{2,1,0:T(8,128)(2,1)} %bitcast.9), calls=%async_computation.1 | async-start | bytes 1048576 | tf_op jit(solution)/shard_map/all_to_all | solution.py:178
  62.3 0.0 copy-done.4
  62.4 4.3 %collective-permute-start.3 = (bf16[128,256]{1,0:T(8,128)(2,1)S(1)}, bf16[128,256]{1,0:T(8,128)(2,1)S(1)}, u32[]{:S(2)}, u32[]{:S(2)}) collective-permute-start(bf16[128,256]{1,0:T(8,128)(2,1)S(1)} %pad_maximum_fusion.1), channel_id=1, source_target_pairs={{0,16},{16,0},{32,48},{48,32},{1,17},{17,1},{33,49},{49,33},{2,18}... | collective-permute-start | bytes 196616 | tf_op jit(solution)/shard_map/ppermute | solution.py:182
  66.7 0.1 copy.27
  66.8 0.1 mul.78
  66.9 0.1 copy.28
  67.0 0.2 mul.82
  67.2 7.2 %collective-permute-done.3 = bf16[128,256]{1,0:T(8,128)(2,1)S(1)} collective-permute-done((bf16[128,256]{1,0:T(8,128)(2,1)S(1)}, bf16[128,256]{1,0:T(8,128)(2,1)S(1)}, u32[]{:S(2)}, u32[]{:S(2)}) %collective-permute-start.3) | collective-permute-done | bytes 65568 | tf_op jit(solution)/shard_map/ppermute | solution.py:182
  74.5 3.5 %all-to-all-done.1 = bf16[64,8,512]{2,1,0:T(8,128)(2,1)S(1)} async-done(((bf16[64,8,512]{2,1,0:T(8,128)(2,1)}), bf16[64,8,512]{2,1,0:T(8,128)(2,1)S(1)}, u32[]{:S(2)}, u32[]{:S(2)}) %all-to-all-start.1) | async-done | bytes 524320 | tf_op jit(solution)/shard_map/all_to_all | solution.py:178
  78.0 0.2 convolution_reduce_fusion
  78.3 1.9 %collective-permute-start.4 = (f32[2,16,512]{2,1,0:T(8,128)S(1)}, f32[2,16,512]{2,1,0:T(8,128)S(1)}, u32[]{:S(2)}, u32[]{:S(2)}) collective-permute-start(f32[2,16,512]{2,1,0:T(8,128)S(1)} %get-tuple-element.26), channel_id=1, source_target_pairs={{0,512},{512,0},{1,513},{513,1},{2,514},{514,2},{3,515},{515,3},{4... | collective-permute-start | bytes 196616 | tf_op jit(solution)/shard_map/ppermute | solution.py:174
  80.2 1.2 collective-permute-done.4.came_ref
  81.4 0.9 finish.1
  82.3 5.6 %all-to-all-start.2 = ((bf16[16,16,1024]{2,1,0:T(8,128)(2,1)}), bf16[16,16,1024]{2,1,0:T(8,128)(2,1)S(1)}, u32[]{:S(2)}, u32[]{:S(2)}) async-start(bf16[16,16,1024]{2,1,0:T(8,128)(2,1)} %get-tuple-element.25), calls=%async_computation.2 | async-start | bytes 1048576 | tf_op jit(solution)/shard_map/all_to_all | solution.py:178
  87.9 5.0 %collective-permute-start.5 = (bf16[128,256]{1,0:T(8,128)(2,1)S(1)}, bf16[128,256]{1,0:T(8,128)(2,1)S(1)}, u32[]{:S(2)}, u32[]{:S(2)}) collective-permute-start(bf16[128,256]{1,0:T(8,128)(2,1)S(1)} %pad_maximum_fusion.2), channel_id=1, source_target_pairs={{0,32},{16,48},{32,0},{48,16},{1,33},{17,49},{33,1},{49,17},{2,34}... | collective-permute-start | bytes 196616 | tf_op jit(solution)/shard_map/ppermute | solution.py:182
  93.0 0.1 pad_add_fusion.place_ref
  93.0 7.4 %collective-permute-done.5 = bf16[128,256]{1,0:T(8,128)(2,1)S(1)} collective-permute-done((bf16[128,256]{1,0:T(8,128)(2,1)S(1)}, bf16[128,256]{1,0:T(8,128)(2,1)S(1)}, u32[]{:S(2)}, u32[]{:S(2)}) %collective-permute-start.5) | collective-permute-done | bytes 65568 | tf_op jit(solution)/shard_map/ppermute | solution.py:182
  100.5 3.1 %all-to-all-done.2.refs_1_ = bf16[16,16,1024]{2,1,0:T(8,128)(2,1)S(1)} async-done(((bf16[16,16,1024]{2,1,0:T(8,128)(2,1)}), bf16[16,16,1024]{2,1,0:T(8,128)(2,1)S(1)}, u32[]{:S(2)}, u32[]{:S(2)}) %all-to-all-start.2) | async-done | bytes 524320 | tf_op jit(solution)/shard_map/all_to_all | solution.py:178
  103.6 0.9 context_product.1
  104.5 40.0 %all_to_all.20 = bf16[32,64,128]{2,1,0:T(8,128)(2,1)S(1)} all-to-all(bf16[32,64,128]{2,1,0:T(8,128)(2,1)S(1)} %context_product.1), channel_id=1, replica_groups=mesh['pool'=2,'zh'=8,'zl'=1,'yh'=4,'yl'=2,'x'=8] {'yh','zh'}, dimensions={0} | all-to-all | bytes 1048576 | tf_op jit(solution)/shard_map/all_to_all | solution.py:178
  144.4 0.7 convert_reduce_fusion
  (13 shorter events, 0.2 us)
Async XLA Ops:
  0.6 2.3 %copy-start.6 = (f32[16,8]{0,1:T(8,128)S(1)}, f32[16,8]{0,1:T(8,128)}, u32[]{:S(2)}) copy-start(f32[16,8]{0,1:T(8,128)} %param.10) | copy-start | bytes 1540
  0.6 2.5 %copy-start.5 = (bf16[16,2048]{1,0:T(8,128)(2,1)S(1)}, bf16[16,2048]{1,0:T(8,128)(2,1)}, u32[]{:S(2)}) copy-start(bf16[16,2048]{1,0:T(8,128)(2,1)} %param.8) | copy-start | bytes 196612
  0.6 2.5 %copy-start.3 = (bf16[16,2048]{1,0:T(8,128)(2,1)S(1)}, bf16[16,2048]{1,0:T(8,128)(2,1)}, u32[]{:S(2)}) copy-start(bf16[16,2048]{1,0:T(8,128)(2,1)} %param.9) | copy-start | bytes 196612
  3.2 18.5 %copy-start = (bf16[1,2048,384]{2,1,0:T(8,128)(2,1)S(1)}, bf16[1,2048,384]{2,1,0:T(8,128)(2,1)}, u32[]{:S(2)}) copy-start(bf16[1,2048,384]{2,1,0:T(8,128)(2,1)} %param.12) | copy-start | bytes 4718596
  4.6 42.3 %all-to-all-start = ((bf16[64,8,1024]{2,1,0:T(8,128)(2,1)}), bf16[64,8,1024]{2,1,0:T(8,128)(2,1)S(1)}, u32[]{:S(2)}, u32[]{:S(2)}) async-start(bf16[64,8,1024]{2,1,0:T(8,128)(2,1)} %fusion), calls=%async_computation | async-start | bytes 2097152 | tf_op jit(solution)/shard_map/all_to_all | solution.py:178
  21.7 6.3 %collective-permute-start = (bf16[2048,384]{1,0:T(8,128)(2,1)S(1)}, bf16[2048,384]{1,0:T(8,128)(2,1)S(1)}, u32[]{:S(2)}, u32[]{:S(2)}) collective-permute-start(bf16[2048,384]{1,0:T(8,128)(2,1)S(1)} %bitcast.24), channel_id=1, source_target_pairs={{0,512},{512,0},{1,513},{513,1},{2,514},{514,2},{3,515},{515,3},{4... | collective-permute-start | bytes 4718600 | tf_op jit(solution)/shard_map/ppermute | solution.py:174
  23.7 5.8 %collective-permute-start.1 = (bf16[2048,384]{1,0:T(8,128)(2,1)}, bf16[2048,384]{1,0:T(8,128)(2,1)S(1)}, u32[]{:S(2)}, u32[]{:S(2)}) collective-permute-start(bf16[2048,384]{1,0:T(8,128)(2,1)} %bitcast.26), channel_id=1, source_target_pairs={{0,512},{512,0},{1,513},{513,1},{2,514},{514,2},{3,515},{515,3},{4... | collective-permute-start | bytes 4718600 | tf_op jit(solution)/shard_map/ppermute | solution.py:174
  26.1 5.8 %collective-permute-start.2 = (bf16[384,2048]{1,0:T(8,128)(2,1)}, bf16[384,2048]{1,0:T(8,128)(2,1)}, u32[]{:S(2)}, u32[]{:S(2)}) collective-permute-start(bf16[384,2048]{1,0:T(8,128)(2,1)} %bitcast.28), channel_id=1, source_target_pairs={{0,512},{512,0},{1,513},{513,1},{2,514},{514,2},{3,515},{515,3},{4... | collective-permute-start | bytes 4718600 | tf_op jit(solution)/shard_map/ppermute | solution.py:174
  28.0 1.5 %copy-start.1 = (bf16[2048,384]{1,0:T(8,128)(2,1)}, bf16[2048,384]{1,0:T(8,128)(2,1)S(1)}, u32[]{:S(2)}) copy-start(bf16[2048,384]{1,0:T(8,128)(2,1)S(1)} %collective-permute-done.refs_3_) | copy-start | bytes 4718596
  29.5 1.2 copy-start.2
  46.9 15.4 %copy-start.4 = (bf16[64,1024]{1,0:T(8,128)(2,1)S(1)}, bf16[64,1024]{1,0:T(8,128)(2,1)}, u32[]{:S(2)}) copy-start(bf16[64,1024]{1,0:T(8,128)(2,1)} %param.15) | copy-start | bytes 393220
  55.0 23.0 %all-to-all-start.1 = ((bf16[64,8,512]{2,1,0:T(8,128)(2,1)}), bf16[64,8,512]{2,1,0:T(8,128)(2,1)S(1)}, u32[]{:S(2)}, u32[]{:S(2)}) async-start(bf16[64,8,512]{2,1,0:T(8,128)(2,1)} %bitcast.9), calls=%async_computation.1 | async-start | bytes 1048576 | tf_op jit(solution)/shard_map/all_to_all | solution.py:178
  62.4 12.1 %collective-permute-start.3 = (bf16[128,256]{1,0:T(8,128)(2,1)S(1)}, bf16[128,256]{1,0:T(8,128)(2,1)S(1)}, u32[]{:S(2)}, u32[]{:S(2)}) collective-permute-start(bf16[128,256]{1,0:T(8,128)(2,1)S(1)} %pad_maximum_fusion.1), channel_id=1, source_target_pairs={{0,16},{16,0},{32,48},{48,32},{1,17},{17,1},{33,49},{49,33},{2,18}... | collective-permute-start | bytes 196616 | tf_op jit(solution)/shard_map/ppermute | solution.py:182
  78.3 3.1 %collective-permute-start.4 = (f32[2,16,512]{2,1,0:T(8,128)S(1)}, f32[2,16,512]{2,1,0:T(8,128)S(1)}, u32[]{:S(2)}, u32[]{:S(2)}) collective-permute-start(f32[2,16,512]{2,1,0:T(8,128)S(1)} %get-tuple-element.26), channel_id=1, source_target_pairs={{0,512},{512,0},{1,513},{513,1},{2,514},{514,2},{3,515},{515,3},{4... | collective-permute-start | bytes 196616 | tf_op jit(solution)/shard_map/ppermute | solution.py:174
  82.3 21.3 %all-to-all-start.2 = ((bf16[16,16,1024]{2,1,0:T(8,128)(2,1)}), bf16[16,16,1024]{2,1,0:T(8,128)(2,1)S(1)}, u32[]{:S(2)}, u32[]{:S(2)}) async-start(bf16[16,16,1024]{2,1,0:T(8,128)(2,1)} %get-tuple-element.25), calls=%async_computation.2 | async-start | bytes 1048576 | tf_op jit(solution)/shard_map/all_to_all | solution.py:178
  87.9 12.5 %collective-permute-start.5 = (bf16[128,256]{1,0:T(8,128)(2,1)S(1)}, bf16[128,256]{1,0:T(8,128)(2,1)S(1)}, u32[]{:S(2)}, u32[]{:S(2)}) collective-permute-start(bf16[128,256]{1,0:T(8,128)(2,1)S(1)} %pad_maximum_fusion.2), channel_id=1, source_target_pairs={{0,32},{16,48},{32,0},{48,16},{1,33},{17,49},{33,1},{49,17},{2,34}... | collective-permute-start | bytes 196616 | tf_op jit(solution)/shard_map/ppermute | solution.py:182

commit v11 on v10

--- a/solution.py
+++ b/solution.py
@@ -111,7 +111,7 @@
     y_blocks = blocks // z_blocks
     for z in range(z_blocks):
         for apart in range(y_blocks):
-            out_ref[jnp.bitwise_xor(yh_index, apart) * z_blocks + z] = total[
+            out_ref[z * y_blocks + jnp.bitwise_xor(yh_index, apart)] = total[
                 apart * heads:(apart + 1) * heads, z * cols:(z + 1) * cols
             ].astype(BF)
 
@@ -121,7 +121,7 @@
     width = tokens_b.shape[2]
     return pl.pallas_call(
         product_kernel,
-        out_shape=jax.ShapeDtypeStruct((y_blocks * z_blocks, rows // y_blocks, width // z_blocks), BF),
+        out_shape=jax.ShapeDtypeStruct((z_blocks * y_blocks, rows // y_blocks, width // z_blocks), BF),
         in_specs=[pl.BlockSpec(memory_space=pltpu.SMEM)]
         + [pl.BlockSpec(memory_space=pltpu.VMEM)] * (len(contexts) + 1),
         out_specs=pl.BlockSpec(memory_space=pltpu.VMEM),
@@ -271,7 +271,7 @@
     contexts = [jnp.concatenate(piece, axis=0) for piece in swap_places(pieces, 2)]
     place = jnp.stack([yh_index, zl_index]).astype(jnp.int32)
     terms = exchange(
-        context_product(place, contexts, gathered_b, y_blocks, z_blocks), ("yh", "zh")
+        context_product(place, contexts, gathered_b, y_blocks, z_blocks), ("zh", "yh")
     )
     wo_grad = jnp.sum(terms.astype(F32), axis=0)
     return (hidden_grad, wo_grad)

time: 146 us -> 146 us (level)
  no operation moved by 1% of the time
where the time goes in v11:
time: 146 us
  starting transfers between devices  47.4 us (32%)
  blocking collectives  40.7 us (28%)
  waiting for transfers between devices  40.2 us (28%)
  Pallas kernels  9.88 us (7%)
  local copies, waits for them, and re-layouts  3.21 us (2%)
  other arithmetic  1.77 us (1%)
  matrix products  1.64 us (1%)
    all_to_all x1, blocking collectives, exchange(): return lax.all_to_all(value, axes, split_axis=0, concat_axis=0, tiled=True)  40.7 us
    all_to_all x3, starting transfers between devices, exchange(): return lax.all_to_all(value, axes, split_axis=0, concat_axis=0, tiled=True)  29.9 us
    all_to_all x3, waiting for transfers between devices, exchange(): return lax.all_to_all(value, axes, split_axis=0, concat_axis=0, tiled=True)  21.7 us
    ppermute x2, waiting for transfers between devices, swapped(): return lax.ppermute(value, axis, tuple(((s, s ^ bit) for s in range(size))))  14.6 us
    ppermute x2, starting transfers between devices, swapped(): return lax.ppermute(value, axis, tuple(((s, s ^ bit) for s in range(size))))  9.34 us
    ppermute x4, starting transfers between devices, swap_pool(): return lax.ppermute(value, 'pool', ((0, 1), (1, 0)))  8.17 us
    pallas_call x1, Pallas kernels, expert_rows(): pl.pallas_call(expert_kernel, out_shape=jax.ShapeDtypeStruct((slots * wid...  8.1 us
    ppermute x4, waiting for transfers between devices, swap_pool(): return lax.ppermute(value, 'pool', ((0, 1), (1, 0)))  3.91 us
  transfers between devices with their start and end apart: 9, of which 8 were waited for; matrix products, arithmetic and copies ran while one was open for 0% of the time, Pallas kernels for 0%

profile of v11, /device:TPU:18, one launch (start us, length us, event | category | flops | bytes accessed | tf_op | source)
XLA Modules:
  0.0 145.8 jit_solution(14335805515298186911)
XLA Ops:
  0.6 0.0 copy-start.6
  0.6 0.0 copy-start.5
  0.6 0.0 copy-start.3
  0.7 0.8 copy.23
  1.5 0.1 eq.52
  1.6 0.1 fusion.13
  1.7 0.2 reduce_window_sum.11
  1.8 0.2 select_reduce_fusion.1
  2.0 0.1 reduce_sum.39
  2.1 0.1 fusion.12
  2.2 0.1 copy.25
  2.4 0.3 broadcast_multiply_fusion
  2.6 0.3 mul.77
  2.9 0.0 copy-done.6
  2.9 0.1 copy.26
  3.0 0.1 select_reduce_fusion
  3.1 0.0 copy-done.5
  3.1 0.0 copy-done.3
  3.2 0.0 copy-start
  3.2 1.4 fusion
  4.6 17.1 %all-to-all-start = ((bf16[64,8,1024]{2,1,0:T(8,128)(2,1)}), bf16[64,8,1024]{2,1,0:T(8,128)(2,1)S(1)}, u32[]{:S(2)}, u32[]{:S(2)}) async-start(bf16[64,8,1024]{2,1,0:T(8,128)(2,1)} %fusion), calls=%async_computation | async-start | bytes 2097152 | tf_op jit(solution)/shard_map/all_to_all | solution.py:178
  21.7 0.0 copy-done
  21.7 1.9 %collective-permute-start = (bf16[2048,384]{1,0:T(8,128)(2,1)S(1)}, bf16[2048,384]{1,0:T(8,128)(2,1)S(1)}, u32[]{:S(2)}, u32[]{:S(2)}) collective-permute-start(bf16[2048,384]{1,0:T(8,128)(2,1)S(1)} %bitcast.24), channel_id=1, source_target_pairs={{0,512},{512,0},{1,513},{513,1},{2,514},{514,2},{3,515},{515,3},{4... | collective-permute-start | bytes 4718600 | tf_op jit(solution)/shard_map/ppermute | solution.py:174
  23.7 2.4 %collective-permute-start.1 = (bf16[2048,384]{1,0:T(8,128)(2,1)}, bf16[2048,384]{1,0:T(8,128)(2,1)S(1)}, u32[]{:S(2)}, u32[]{:S(2)}) collective-permute-start(bf16[2048,384]{1,0:T(8,128)(2,1)} %bitcast.26), channel_id=1, source_target_pairs={{0,512},{512,0},{1,513},{513,1},{2,514},{514,2},{3,515},{515,3},{4... | collective-permute-start | bytes 4718600 | tf_op jit(solution)/shard_map/ppermute | solution.py:174
  26.1 1.9 %collective-permute-start.2 = (bf16[384,2048]{1,0:T(8,128)(2,1)}, bf16[384,2048]{1,0:T(8,128)(2,1)}, u32[]{:S(2)}, u32[]{:S(2)}) collective-permute-start(bf16[384,2048]{1,0:T(8,128)(2,1)} %bitcast.28), channel_id=1, source_target_pairs={{0,512},{512,0},{1,513},{513,1},{2,514},{514,2},{3,515},{515,3},{4... | collective-permute-start | bytes 4718600 | tf_op jit(solution)/shard_map/ppermute | solution.py:174
  28.0 0.0 collective-permute-done.refs_3_
  28.0 0.0 copy-start.1
  28.0 1.5 %collective-permute-done.1.refs_4_ = bf16[2048,384]{1,0:T(8,128)(2,1)S(1)} collective-permute-done((bf16[2048,384]{1,0:T(8,128)(2,1)}, bf16[2048,384]{1,0:T(8,128)(2,1)S(1)}, u32[]{:S(2)}, u32[]{:S(2)}) %collective-permute-start.1) | collective-permute-done | bytes 1572896 | tf_op jit(solution)/shard_map/ppermute | solution.py:174
  29.5 0.0 copy-done.1
  29.5 0.0 copy-start.2
  29.5 1.2 copy-done.2
  30.7 1.2 collective-permute-done.2.refs_5_
  31.9 15.0 %all-to-all-done = bf16[64,8,1024]{2,1,0:T(8,128)(2,1)S(1)} async-done(((bf16[64,8,1024]{2,1,0:T(8,128)(2,1)}), bf16[64,8,1024]{2,1,0:T(8,128)(2,1)S(1)}, u32[]{:S(2)}, u32[]{:S(2)}) %all-to-all-start) | async-done | bytes 1048608 | tf_op jit(solution)/shard_map/all_to_all | solution.py:178
  46.9 0.0 copy-start.4
  46.9 8.1 %expert.1 = bf16[512,512]{1,0:T(8,128)(2,1)} custom-call(bf16[512,1024]{1,0:T(8,128)(2,1)S(1)} %bitcast.23, bf16[2048,384]{1,0:T(8,128)(2,1)S(1)} %bitcast.25, bf16[2048,384]{1,0:T(8,128)(2,1)} %bitcast.27, bf16[384,2048]{1,0:T(8,128)(2,1)} %bitcast.29, bf16[2048,384]{1,0:T(8,128)(2,1)} %copy-done.1, bf16[2048,384]{1,0:T(8,128)(2,1)} %copy-done.2, ...), custom_call_target="tpu_custom_call" | custom-call | flops 2013265920 | bytes 9437184 | tf_op jit(solution)/shard_map/expert/pallas_call | solution.py:83
  55.0 7.2 %all-to-all-start.1 = ((bf16[64,8,512]{2,1,0:T(8,128)(2,1)}), bf16[64,8,512]{2,1,0:T(8,128)(2,1)S(1)}, u32[]{:S(2)}, u32[]{:S(2)}) async-start(bf16[64,8,512]{2,1,0:T(8,128)(2,1)} %bitcast.9), calls=%async_computation.1 | async-start | bytes 1048576 | tf_op jit(solution)/shard_map/all_to_all | solution.py:178
  62.3 0.0 copy-done.4
  62.4 4.3 %collective-permute-start.3 = (bf16[128,256]{1,0:T(8,128)(2,1)S(1)}, bf16[128,256]{1,0:T(8,128)(2,1)S(1)}, u32[]{:S(2)}, u32[]{:S(2)}) collective-permute-start(bf16[128,256]{1,0:T(8,128)(2,1)S(1)} %pad_maximum_fusion.1), channel_id=1, source_target_pairs={{0,16},{16,0},{32,48},{48,32},{1,17},{17,1},{33,49},{49,33},{2,18}... | collective-permute-start | bytes 196616 | tf_op jit(solution)/shard_map/ppermute | solution.py:182
  66.7 0.1 copy.27
  66.8 0.1 mul.78
  66.9 0.1 copy.28
  67.0 0.2 mul.82
  67.2 7.2 %collective-permute-done.3 = bf16[128,256]{1,0:T(8,128)(2,1)S(1)} collective-permute-done((bf16[128,256]{1,0:T(8,128)(2,1)S(1)}, bf16[128,256]{1,0:T(8,128)(2,1)S(1)}, u32[]{:S(2)}, u32[]{:S(2)}) %collective-permute-start.3) | collective-permute-done | bytes 65568 | tf_op jit(solution)/shard_map/ppermute | solution.py:182
  74.5 3.5 %all-to-all-done.1 = bf16[64,8,512]{2,1,0:T(8,128)(2,1)S(1)} async-done(((bf16[64,8,512]{2,1,0:T(8,128)(2,1)}), bf16[64,8,512]{2,1,0:T(8,128)(2,1)S(1)}, u32[]{:S(2)}, u32[]{:S(2)}) %all-to-all-start.1) | async-done | bytes 524320 | tf_op jit(solution)/shard_map/all_to_all | solution.py:178
  78.0 0.2 convolution_reduce_fusion
  78.3 1.9 %collective-permute-start.4 = (f32[2,16,512]{2,1,0:T(8,128)S(1)}, f32[2,16,512]{2,1,0:T(8,128)S(1)}, u32[]{:S(2)}, u32[]{:S(2)}) collective-permute-start(f32[2,16,512]{2,1,0:T(8,128)S(1)} %get-tuple-element.26), channel_id=1, source_target_pairs={{0,512},{512,0},{1,513},{513,1},{2,514},{514,2},{3,515},{515,3},{4... | collective-permute-start | bytes 196616 | tf_op jit(solution)/shard_map/ppermute | solution.py:174
  80.2 1.2 collective-permute-done.4.came_ref
  81.4 0.9 finish.1
  82.3 5.6 %all-to-all-start.2 = ((bf16[16,16,1024]{2,1,0:T(8,128)(2,1)}), bf16[16,16,1024]{2,1,0:T(8,128)(2,1)S(1)}, u32[]{:S(2)}, u32[]{:S(2)}) async-start(bf16[16,16,1024]{2,1,0:T(8,128)(2,1)} %get-tuple-element.25), calls=%async_computation.2 | async-start | bytes 1048576 | tf_op jit(solution)/shard_map/all_to_all | solution.py:178
  87.9 5.0 %collective-permute-start.5 = (bf16[128,256]{1,0:T(8,128)(2,1)S(1)}, bf16[128,256]{1,0:T(8,128)(2,1)S(1)}, u32[]{:S(2)}, u32[]{:S(2)}) collective-permute-start(bf16[128,256]{1,0:T(8,128)(2,1)S(1)} %pad_maximum_fusion.2), channel_id=1, source_target_pairs={{0,32},{16,48},{32,0},{48,16},{1,33},{17,49},{33,1},{49,17},{2,34}... | collective-permute-start | bytes 196616 | tf_op jit(solution)/shard_map/ppermute | solution.py:182
  93.0 0.1 pad_add_fusion.place_ref
  93.0 7.4 %collective-permute-done.5 = bf16[128,256]{1,0:T(8,128)(2,1)S(1)} collective-permute-done((bf16[128,256]{1,0:T(8,128)(2,1)S(1)}, bf16[128,256]{1,0:T(8,128)(2,1)S(1)}, u32[]{:S(2)}, u32[]{:S(2)}) %collective-permute-start.5) | collective-permute-done | bytes 65568 | tf_op jit(solution)/shard_map/ppermute | solution.py:182
  100.5 3.1 %all-to-all-done.2.refs_1_ = bf16[16,16,1024]{2,1,0:T(8,128)(2,1)S(1)} async-done(((bf16[16,16,1024]{2,1,0:T(8,128)(2,1)}), bf16[16,16,1024]{2,1,0:T(8,128)(2,1)S(1)}, u32[]{:S(2)}, u32[]{:S(2)}) %all-to-all-start.2) | async-done | bytes 524320 | tf_op jit(solution)/shard_map/all_to_all | solution.py:178
  103.6 0.9 context_product.1
  104.5 40.7 %all_to_all.20 = bf16[32,64,128]{2,1,0:T(8,128)(2,1)S(1)} all-to-all(bf16[32,64,128]{2,1,0:T(8,128)(2,1)S(1)} %context_product.1), channel_id=1, replica_groups=mesh['pool'=2,'zh'=8,'zl'=1,'yh'=4,'yl'=2,'x'=8] {'zh','yh'}, dimensions={0} | all-to-all | bytes 1048576 | tf_op jit(solution)/shard_map/all_to_all | solution.py:178
  145.1 0.7 convert_reduce_fusion
  (13 shorter events, 0.2 us)
Async XLA Ops:
  0.6 2.3 %copy-start.6 = (f32[16,8]{0,1:T(8,128)S(1)}, f32[16,8]{0,1:T(8,128)}, u32[]{:S(2)}) copy-start(f32[16,8]{0,1:T(8,128)} %param.10) | copy-start | bytes 1540
  0.6 2.5 %copy-start.5 = (bf16[16,2048]{1,0:T(8,128)(2,1)S(1)}, bf16[16,2048]{1,0:T(8,128)(2,1)}, u32[]{:S(2)}) copy-start(bf16[16,2048]{1,0:T(8,128)(2,1)} %param.8) | copy-start | bytes 196612
  0.6 2.5 %copy-start.3 = (bf16[16,2048]{1,0:T(8,128)(2,1)S(1)}, bf16[16,2048]{1,0:T(8,128)(2,1)}, u32[]{:S(2)}) copy-start(bf16[16,2048]{1,0:T(8,128)(2,1)} %param.9) | copy-start | bytes 196612
  3.2 18.5 %copy-start = (bf16[1,2048,384]{2,1,0:T(8,128)(2,1)S(1)}, bf16[1,2048,384]{2,1,0:T(8,128)(2,1)}, u32[]{:S(2)}) copy-start(bf16[1,2048,384]{2,1,0:T(8,128)(2,1)} %param.12) | copy-start | bytes 4718596
  4.6 42.3 %all-to-all-start = ((bf16[64,8,1024]{2,1,0:T(8,128)(2,1)}), bf16[64,8,1024]{2,1,0:T(8,128)(2,1)S(1)}, u32[]{:S(2)}, u32[]{:S(2)}) async-start(bf16[64,8,1024]{2,1,0:T(8,128)(2,1)} %fusion), calls=%async_computation | async-start | bytes 2097152 | tf_op jit(solution)/shard_map/all_to_all | solution.py:178
  21.7 6.3 %collective-permute-start = (bf16[2048,384]{1,0:T(8,128)(2,1)S(1)}, bf16[2048,384]{1,0:T(8,128)(2,1)S(1)}, u32[]{:S(2)}, u32[]{:S(2)}) collective-permute-start(bf16[2048,384]{1,0:T(8,128)(2,1)S(1)} %bitcast.24), channel_id=1, source_target_pairs={{0,512},{512,0},{1,513},{513,1},{2,514},{514,2},{3,515},{515,3},{4... | collective-permute-start | bytes 4718600 | tf_op jit(solution)/shard_map/ppermute | solution.py:174
  23.7 5.8 %collective-permute-start.1 = (bf16[2048,384]{1,0:T(8,128)(2,1)}, bf16[2048,384]{1,0:T(8,128)(2,1)S(1)}, u32[]{:S(2)}, u32[]{:S(2)}) collective-permute-start(bf16[2048,384]{1,0:T(8,128)(2,1)} %bitcast.26), channel_id=1, source_target_pairs={{0,512},{512,0},{1,513},{513,1},{2,514},{514,2},{3,515},{515,3},{4... | collective-permute-start | bytes 4718600 | tf_op jit(solution)/shard_map/ppermute | solution.py:174
  26.1 5.8 %collective-permute-start.2 = (bf16[384,2048]{1,0:T(8,128)(2,1)}, bf16[384,2048]{1,0:T(8,128)(2,1)}, u32[]{:S(2)}, u32[]{:S(2)}) collective-permute-start(bf16[384,2048]{1,0:T(8,128)(2,1)} %bitcast.28), channel_id=1, source_target_pairs={{0,512},{512,0},{1,513},{513,1},{2,514},{514,2},{3,515},{515,3},{4... | collective-permute-start | bytes 4718600 | tf_op jit(solution)/shard_map/ppermute | solution.py:174
  28.0 1.5 %copy-start.1 = (bf16[2048,384]{1,0:T(8,128)(2,1)}, bf16[2048,384]{1,0:T(8,128)(2,1)S(1)}, u32[]{:S(2)}) copy-start(bf16[2048,384]{1,0:T(8,128)(2,1)S(1)} %collective-permute-done.refs_3_) | copy-start | bytes 4718596
  29.5 1.2 copy-start.2
  46.9 15.4 %copy-start.4 = (bf16[64,1024]{1,0:T(8,128)(2,1)S(1)}, bf16[64,1024]{1,0:T(8,128)(2,1)}, u32[]{:S(2)}) copy-start(bf16[64,1024]{1,0:T(8,128)(2,1)} %param.15) | copy-start | bytes 393220
  55.0 23.0 %all-to-all-start.1 = ((bf16[64,8,512]{2,1,0:T(8,128)(2,1)}), bf16[64,8,512]{2,1,0:T(8,128)(2,1)S(1)}, u32[]{:S(2)}, u32[]{:S(2)}) async-start(bf16[64,8,512]{2,1,0:T(8,128)(2,1)} %bitcast.9), calls=%async_computation.1 | async-start | bytes 1048576 | tf_op jit(solution)/shard_map/all_to_all | solution.py:178
  62.4 12.1 %collective-permute-start.3 = (bf16[128,256]{1,0:T(8,128)(2,1)S(1)}, bf16[128,256]{1,0:T(8,128)(2,1)S(1)}, u32[]{:S(2)}, u32[]{:S(2)}) collective-permute-start(bf16[128,256]{1,0:T(8,128)(2,1)S(1)} %pad_maximum_fusion.1), channel_id=1, source_target_pairs={{0,16},{16,0},{32,48},{48,32},{1,17},{17,1},{33,49},{49,33},{2,18}... | collective-permute-start | bytes 196616 | tf_op jit(solution)/shard_map/ppermute | solution.py:182
  78.3 3.1 %collective-permute-start.4 = (f32[2,16,512]{2,1,0:T(8,128)S(1)}, f32[2,16,512]{2,1,0:T(8,128)S(1)}, u32[]{:S(2)}, u32[]{:S(2)}) collective-permute-start(f32[2,16,512]{2,1,0:T(8,128)S(1)} %get-tuple-element.26), channel_id=1, source_target_pairs={{0,512},{512,0},{1,513},{513,1},{2,514},{514,2},{3,515},{515,3},{4... | collective-permute-start | bytes 196616 | tf_op jit(solution)/shard_map/ppermute | solution.py:174
  82.3 21.3 %all-to-all-start.2 = ((bf16[16,16,1024]{2,1,0:T(8,128)(2,1)}), bf16[16,16,1024]{2,1,0:T(8,128)(2,1)S(1)}, u32[]{:S(2)}, u32[]{:S(2)}) async-start(bf16[16,16,1024]{2,1,0:T(8,128)(2,1)} %get-tuple-element.25), calls=%async_computation.2 | async-start | bytes 1048576 | tf_op jit(solution)/shard_map/all_to_all | solution.py:178
  87.9 12.5 %collective-permute-start.5 = (bf16[128,256]{1,0:T(8,128)(2,1)S(1)}, bf16[128,256]{1,0:T(8,128)(2,1)S(1)}, u32[]{:S(2)}, u32[]{:S(2)}) collective-permute-start(bf16[128,256]{1,0:T(8,128)(2,1)S(1)} %pad_maximum_fusion.2), channel_id=1, source_target_pairs={{0,32},{16,48},{32,0},{48,16},{1,33},{17,49},{33,1},{49,17},{2,34}... | collective-permute-start | bytes 196616 | tf_op jit(solution)/shard_map/ppermute | solution.py:182
